TPU v7x, 32 devices: a whole 2x2x4 slice. The times are simulated.
32 devices in a mesh: ctx: 8 (over z, y), exp: 4 (over x, core).
Axes of the slice: x: 2, y: 2, z: 4, core: 2. Of those that a mesh axis runs over, the one named last changes fastest.
Arguments:
- activations: bfloat16 [4, 1024, 768], P('exp', 'ctx'), may hold values from -6 to 6
- gain_one: bfloat16 [768], P(('ctx', 'exp')), may hold values from 0.5 to 1.5
- query_key_value_weight: bfloat16 [768, 2304], P(('ctx', 'exp')), may hold values from -0.21875 to 0.21875
- attention_output_weight: bfloat16 [768, 768], P(('ctx', 'exp')), may hold values from -3.5 to 3.5
- pos_table: float32 [32, 12], replicated, may hold values from -3 to 3
- gain_two: bfloat16 [768], P(('ctx', 'exp')), may hold values from 0.5 to 1.5
- w_router: bfloat16 [768, 4], P(('ctx', 'exp')), may hold values from -0.15625 to 0.15625
- w_in: bfloat16 [4, 768, 3072], P('exp', 'ctx'), may hold values from -0.21875 to 0.21875
- w_out: bfloat16 [4, 3072, 768], P('exp', 'ctx'), may hold values from -0.109375 to 0.109375
- routes: int32 [4, 1024, 2], P('exp', 'ctx'), may hold values from 0 to 3, all different within a row; in each aligned block of 128 rows (0 to 127, 128 to 255, ..., all dimensions but the last counted through in order) at most 80 rows name the same one
- pair_of_device: int32 [8], replicated, may hold values from 0 to 7, each once
- cotangent: float32 [4, 1024, 768], P('exp', 'ctx'), may hold values from -6 to 6
Outputs:
- output: float32 [4, 1024, 768], P('exp', 'ctx')
- d_activations: float32 [4, 1024, 768], P('exp', 'ctx')
- d_gain_one: float32 [768], P(('ctx', 'exp'))
- d_w_qkv: float32 [768, 2304], P(('ctx', 'exp'))
- d_w_attn_out: float32 [768, 768], P(('ctx', 'exp'))
- d_pos_table: float32 [32, 12], replicated
- d_gain_two: float32 [768], P(('ctx', 'exp'))
- d_w_router: float32 [768, 4], P(('ctx', 'exp'))
- d_w_in: float32 [4, 768, 3072], P('exp', 'ctx')
- d_w_out: float32 [4, 3072, 768], P('exp', 'ctx')
Inputs may be any that keep to these rules, and one draw needn't show every extreme that they name: `routes`: A token names 2 different experts. In each aligned block of 128 stored rows of a sequence (the rows of one device) no expert is named by more than 80 rows, a bound that some block reaches. `pair_of_device`: each value appears once.
All inputs are finite; a program needn't handle non-finite values.
Results may differ from a plain program's by a relative error of at most 0.015.
Values may be sent and summed in bfloat16 or wider, within the bound.
No kernel may reach another device: no remote copies, remote signals or barrier semaphores. Data moves between devices by JAX's collectives and lax.ppermute only.
A program may use at most 192 MiB of HBM per device.

v0:
```python
import jax
import jax.numpy as jnp
from jax import lax
from jax.sharding import PartitionSpec as P

PRECISION_FULL = lax.Precision.HIGHEST
MASKED = -1e30


def rms_norm(values, gain):
    scale = lax.rsqrt(jnp.mean(values * values, axis=-1, keepdims=True) + 1e-06)
    return values * scale * gain


def stored_positions(pair_of_device, devices_ctx, own_rows):
    half_width = own_rows // 2
    row_index = lax.broadcasted_iota(jnp.int32, (devices_ctx * own_rows, devices_ctx), 0)
    column_index = lax.broadcasted_iota(jnp.int32, (devices_ctx * own_rows, devices_ctx), 1)
    first_block = jnp.sum(
        jnp.where(row_index // own_rows == column_index, pair_of_device[None, :], 0), axis=1
    )
    within = lax.broadcasted_iota(jnp.int32, (devices_ctx * own_rows,), 0) % own_rows
    block_index = jnp.where(within < half_width, first_block, 2 * devices_ctx - 1 - first_block)
    return block_index * half_width + within % half_width


def tile_onehot(query_pos, key_pos, half_width, buckets):
    query_tiles = query_pos[::half_width] // half_width
    key_tiles = key_pos[::half_width] // half_width
    bucket = jnp.clip(query_tiles[:, None] - key_tiles[None, :], 0, buckets - 1)
    levels = lax.broadcasted_iota(jnp.int32, bucket.shape + (buckets,), 2)
    return (bucket[:, :, None] == levels).astype(jnp.float32)


def biased_scores(queries, key_rows, query_pos, key_pos, bias_table, half_width):
    head_count = queries.shape[1]
    query_count = queries.shape[0]
    key_count = key_rows.shape[0]
    raw_scores = (
        jnp.einsum("qhe,khe->hqk", queries, key_rows, preferred_element_type=jnp.float32) * 0.125
    )
    onehot = tile_onehot(query_pos, key_pos, half_width, bias_table.shape[0])
    tile_bias = jnp.einsum("abn,nh->hab", onehot, bias_table, precision=PRECISION_FULL)
    shaped = raw_scores.reshape(
        head_count, query_count // half_width, half_width, key_count // half_width, half_width
    )
    shaped = (shaped + tile_bias[:, :, None, :, None]).reshape(head_count, query_count, key_count)
    visible = query_pos[:, None] >= key_pos[None, :]
    return (jnp.where(visible[None], shaped, MASKED), onehot)


def table_grad_of(grad_scores, onehot, half_width):
    head_count, query_count, key_count = grad_scores.shape
    tile_sums = (
        grad_scores.astype(jnp.float32)
        .reshape(
            head_count, query_count // half_width, half_width, key_count // half_width, half_width
        )
        .sum(axis=(2, 4))
    )
    return jnp.einsum("hab,abn->nh", tile_sums, onehot, precision=PRECISION_FULL)


def split_pairs(paired, head_count):
    model_width = paired.shape[1] // 2
    row_count = paired.shape[0]
    key_rows = paired[:, :model_width].reshape(row_count, head_count, model_width // head_count)
    value_rows = paired[:, model_width:].reshape(row_count, head_count, model_width // head_count)
    return (key_rows, value_rows)


def body(
    activations,
    gain_one,
    query_key_value_weight,
    attention_output_weight,
    pos_table,
    gain_two,
    w_router,
    w_in,
    w_out,
    routes,
    pair_of_device,
    cotangent,
):
    seq_count, own_rows, model_width = activations.shape
    half_width = own_rows // 2
    head_count = pos_table.shape[1]
    head_size = model_width // head_count
    top_count = routes.shape[2]
    experts = w_in.shape[0] * lax.axis_size("exp")
    capacity = max(2, 5 * own_rows * top_count // (4 * experts))
    devices_ctx = lax.axis_size("ctx")
    (
        full_gain_one,
        complete_query_key_value,
        complete_attention_output,
        complete_router_weight,
        full_gain_two,
    ) = (
        lax.all_gather(gain_one, ("ctx", "exp"), axis=0, tiled=True),
        lax.all_gather(query_key_value_weight, ("ctx", "exp"), axis=0, tiled=True),
        lax.all_gather(attention_output_weight, ("ctx", "exp"), axis=0, tiled=True),
        lax.all_gather(w_router, ("ctx", "exp"), axis=0, tiled=True),
        lax.all_gather(gain_two, ("ctx", "exp"), axis=0, tiled=True),
    )
    full_first, full_second = (
        lax.all_gather(w_in, "ctx", axis=1, tiled=True),
        lax.all_gather(w_out, "ctx", axis=1, tiled=True),
    )
    full_first = full_first[0]
    full_second = full_second[0]
    all_pos = stored_positions(pair_of_device, devices_ctx, own_rows)
    own_pos = lax.dynamic_slice_in_dim(all_pos, lax.axis_index("ctx") * own_rows, own_rows)
    inputs = activations.astype(jnp.float32)
    gain_first = full_gain_one.astype(jnp.float32)
    reduced_first = rms_norm(inputs, gain_first).astype(jnp.bfloat16)
    query_key_value = jnp.einsum(
        "vbk,kr->vbr", reduced_first, complete_query_key_value, preferred_element_type=jnp.float32
    ).astype(jnp.bfloat16)
    queries = query_key_value[..., :model_width].reshape(seq_count, own_rows, head_count, head_size)
    pair_own = query_key_value[..., model_width:]

    def forward_sequence(entries):
        query_seq, pair_seq = entries
        pair_all = lax.all_gather(pair_seq, "ctx", axis=0, tiled=True)
        key_rows, value_rows = split_pairs(pair_all, head_count)
        scores, onehot = biased_scores(query_seq, key_rows, own_pos, all_pos, pos_table, half_width)
        row_max = jnp.max(scores, axis=-1, keepdims=True)
        weights = jnp.exp(scores - row_max)
        row_sum = jnp.sum(weights, axis=-1, keepdims=True)
        low_weights = (weights / row_sum).astype(jnp.bfloat16)
        mixed_seq = jnp.einsum(
            "hqk,khe->qhe", low_weights, value_rows, preferred_element_type=jnp.float32
        )
        return (
            mixed_seq.reshape(own_rows, model_width).astype(jnp.bfloat16),
            (row_max + jnp.log(row_sum))[..., 0],
        )

    merged_head_output, log_totals = lax.map(forward_sequence, (queries, pair_own))
    attention_result = jnp.einsum(
        "puw,wb->pub",
        merged_head_output,
        complete_attention_output,
        preferred_element_type=jnp.float32,
    )
    resid = inputs + attention_result
    gain_second = full_gain_two.astype(jnp.float32)
    reduced_second = rms_norm(resid, gain_second).astype(jnp.bfloat16)
    router_logits = jnp.einsum(
        "puw,wb->pub", reduced_second, complete_router_weight, preferred_element_type=jnp.float32
    )
    expert_iota = lax.broadcasted_iota(jnp.int32, (1, 1, 1, experts), 3)
    chosen_mask = (routes[..., None] == expert_iota).astype(jnp.float32)
    chosen = jnp.sum(chosen_mask * router_logits[:, :, None, :], axis=-1)
    gate_weights = jax.nn.softmax(chosen, axis=-1)
    flat_ids = routes.reshape(seq_count, own_rows * top_count)
    hits = (flat_ids[..., None] == lax.broadcasted_iota(jnp.int32, (1, 1, experts), 2)).astype(
        jnp.int32
    )
    slot_rank = jnp.sum((jnp.cumsum(hits, axis=1) - hits) * hits, axis=-1)
    target = flat_ids * capacity + slot_rank
    slot_iota = lax.broadcasted_iota(jnp.int32, (1, 1, experts * capacity), 2)
    route_map = (target[..., None] == slot_iota).astype(jnp.bfloat16)
    per_token = route_map.reshape(seq_count, own_rows, top_count, experts * capacity).sum(axis=2)
    outgoing = jnp.einsum(
        "str,std->rsd", per_token, reduced_second, preferred_element_type=jnp.float32
    )
    outgoing = outgoing.astype(jnp.bfloat16).reshape(experts, capacity * seq_count, model_width)
    rows = lax.all_to_all(outgoing, "exp", split_axis=0, concat_axis=0, tiled=True)
    hidden = jnp.einsum("nid,df->nif", rows, full_first, preferred_element_type=jnp.float32)
    active = jax.nn.gelu(hidden).astype(jnp.bfloat16)
    answer = jnp.einsum(
        "nif,fd->nid", active, full_second, preferred_element_type=jnp.float32
    ).astype(jnp.bfloat16)
    returned = lax.all_to_all(answer, "exp", split_axis=0, concat_axis=0, tiled=True)
    picked = jnp.einsum(
        "sjr,rsd->sjd",
        route_map,
        returned.reshape(experts * capacity, seq_count, model_width),
        preferred_element_type=jnp.float32,
    ).reshape(seq_count, own_rows, top_count, model_width)
    expert_sum = jnp.sum(gate_weights[..., None] * picked, axis=2)
    output = resid + expert_sum
    grad_picked = (gate_weights[..., None] * cotangent[:, :, None, :]).astype(jnp.bfloat16)
    grad_picked = grad_picked.reshape(seq_count, own_rows * top_count, model_width)
    grad_gates = jnp.sum(picked * cotangent[:, :, None, :], axis=-1)
    grad_chosen = gate_weights * (
        grad_gates - jnp.sum(gate_weights * grad_gates, axis=-1, keepdims=True)
    )
    logit_gradient = jnp.sum(grad_chosen[..., None] * chosen_mask, axis=2)
    outgoing_grad = jnp.einsum(
        "sjr,sjd->rsd", route_map, grad_picked, preferred_element_type=jnp.float32
    )
    outgoing_grad = outgoing_grad.astype(jnp.bfloat16).reshape(
        experts, capacity * seq_count, model_width
    )
    grad_answers = lax.all_to_all(outgoing_grad, "exp", split_axis=0, concat_axis=0, tiled=True)
    grad_rows = grad_answers.reshape(-1, model_width)
    rows_all = rows.reshape(-1, model_width)
    hidden_all = hidden.reshape(rows_all.shape[0], -1)
    active_all = jax.nn.gelu(hidden_all).astype(jnp.bfloat16)
    grad_second = jnp.einsum("if,id->fd", active_all, grad_rows, preferred_element_type=jnp.float32)
    grad_active = jnp.einsum(
        "id,fd->if", grad_rows, full_second, preferred_element_type=jnp.float32
    )
    gelu_value, gelu_back = jax.vjp(jax.nn.gelu, hidden_all)
    grad_hidden = gelu_back(grad_active)[0].astype(jnp.bfloat16)
    grad_first = jnp.einsum("id,if->df", rows_all, grad_hidden, preferred_element_type=jnp.float32)
    grad_rows_in = jnp.einsum(
        "if,df->id", grad_hidden, full_first, preferred_element_type=jnp.float32
    ).astype(jnp.bfloat16)
    coming = lax.all_to_all(
        grad_rows_in.reshape(experts, capacity * seq_count, model_width),
        "exp",
        split_axis=0,
        concat_axis=0,
        tiled=True,
    )
    shard_first, shard_second = (
        lax.psum_scatter(
            grad_first[None].astype(jnp.bfloat16), "ctx", scatter_dimension=1, tiled=True
        ).astype(jnp.float32),
        lax.psum_scatter(
            grad_second[None].astype(jnp.bfloat16), "ctx", scatter_dimension=1, tiled=True
        ).astype(jnp.float32),
    )
    grad_copies = jnp.einsum(
        "sjr,rsd->sjd",
        route_map,
        coming.reshape(experts * capacity, seq_count, model_width),
        preferred_element_type=jnp.float32,
    ).reshape(seq_count, own_rows, top_count, model_width)
    router_weight_wide = complete_router_weight.astype(jnp.float32)
    grad_low_two = jnp.sum(grad_copies, axis=2) + jnp.einsum(
        "mby,gy->mbg", logit_gradient, router_weight_wide, precision=PRECISION_FULL
    )
    grad_router = jnp.einsum(
        "wtg,wta->ga", reduced_second.astype(jnp.float32), logit_gradient, precision=PRECISION_FULL
    )
    norm_value, norm_two_back = jax.vjp(rms_norm, resid, gain_second)
    grad_resid_norm, grad_gain_two = norm_two_back(grad_low_two)
    grad_resid = cotangent + grad_resid_norm
    attention_gradient = grad_resid.astype(jnp.bfloat16)
    grad_attn_out = jnp.einsum(
        "wtg,wta->ga", merged_head_output, attention_gradient, preferred_element_type=jnp.float32
    )
    grad_mixed = jnp.einsum(
        "mby,gy->mbg",
        attention_gradient,
        complete_attention_output,
        preferred_element_type=jnp.float32,
    ).astype(jnp.bfloat16)

    def backward_sequence(entries):
        query_seq, pair_seq, grad_seq, totals_seq = entries
        pair_all = lax.all_gather(pair_seq, "ctx", axis=0, tiled=True)
        key_rows, value_rows = split_pairs(pair_all, head_count)
        grad_heads = grad_seq.reshape(own_rows, head_count, head_size)
        scores, onehot = biased_scores(query_seq, key_rows, own_pos, all_pos, pos_table, half_width)
        weights = jnp.exp(scores - totals_seq[..., None])
        grad_weights = jnp.einsum(
            "qhe,khe->hqk", grad_heads, value_rows, preferred_element_type=jnp.float32
        )
        row_dot = jnp.sum(weights * grad_weights, axis=-1)
        grad_scores = (weights * (grad_weights - row_dot[..., None])).astype(jnp.bfloat16)
        grad_query = (
            jnp.einsum("hqk,khe->qhe", grad_scores, key_rows, preferred_element_type=jnp.float32)
            * 0.125
        )
        table_part = table_grad_of(grad_scores, onehot, half_width)
        grad_keys = (
            jnp.einsum("hqk,qhe->khe", grad_scores, query_seq, preferred_element_type=jnp.float32)
            * 0.125
        )
        grad_values = jnp.einsum(
            "hqk,qhe->khe",
            weights.astype(jnp.bfloat16),
            grad_heads,
            preferred_element_type=jnp.float32,
        )
        key_count = pair_all.shape[0]
        grad_terms = jnp.concatenate(
            [
                grad_keys.reshape(key_count, model_width),
                grad_values.reshape(key_count, model_width),
            ],
            axis=1,
        )
        grad_pair = lax.psum_scatter(
            grad_terms.astype(jnp.bfloat16), "ctx", scatter_dimension=0, tiled=True
        ).astype(jnp.float32)
        return (grad_query.reshape(own_rows, model_width), grad_pair, table_part)

    grad_query_all, grad_pair_all, table_parts = lax.map(
        backward_sequence, (queries, pair_own, grad_mixed, log_totals)
    )
    query_key_value_gradient = jnp.concatenate([grad_query_all, grad_pair_all], axis=-1).astype(
        jnp.bfloat16
    )
    query_key_value_weight_gradient = jnp.einsum(
        "ink,int->kt", reduced_first, query_key_value_gradient, preferred_element_type=jnp.float32
    )
    normalized_gradient = jnp.einsum(
        "ptg,hg->pth",
        query_key_value_gradient,
        complete_query_key_value,
        preferred_element_type=jnp.float32,
    )
    first_value, norm_one_back = jax.vjp(rms_norm, inputs, gain_first)
    grad_in_norm, grad_gain_one = norm_one_back(normalized_gradient)
    grad_inputs = grad_resid + grad_in_norm
    table_total = lax.psum(jnp.sum(table_parts, axis=0), ("ctx", "exp"))
    shard_gain_one, shard_qkv, shard_attn_out, shard_router, shard_gain_two = (
        lax.psum_scatter(grad_gain_one, ("ctx", "exp"), scatter_dimension=0, tiled=True),
        lax.psum_scatter(
            query_key_value_weight_gradient, ("ctx", "exp"), scatter_dimension=0, tiled=True
        ),
        lax.psum_scatter(grad_attn_out, ("ctx", "exp"), scatter_dimension=0, tiled=True),
        lax.psum_scatter(grad_router, ("ctx", "exp"), scatter_dimension=0, tiled=True),
        lax.psum_scatter(grad_gain_two, ("ctx", "exp"), scatter_dimension=0, tiled=True),
    )
    return (
        output,
        grad_inputs,
        shard_gain_one,
        shard_qkv,
        shard_attn_out,
        table_total,
        shard_gain_two,
        shard_router,
        shard_first,
        shard_second,
    )


def solution(mesh):
    return jax.shard_map(
        body,
        mesh=mesh,
        in_specs=(
            P("exp", "ctx", None),
            P(("ctx", "exp")),
            P(("ctx", "exp"), None),
            P(("ctx", "exp"), None),
            P(),
            P(("ctx", "exp")),
            P(("ctx", "exp"), None),
            P("exp", "ctx", None),
            P("exp", "ctx", None),
            P("exp", "ctx", None),
            P(),
            P("exp", "ctx", None),
        ),
        out_specs=(
            P("exp", "ctx", None),
            P("exp", "ctx", None),
            P(("ctx", "exp")),
            P(("ctx", "exp"), None),
            P(("ctx", "exp"), None),
            P(),
            P(("ctx", "exp")),
            P(("ctx", "exp"), None),
            P("exp", "ctx", None),
            P("exp", "ctx", None),
        ),
        check_vma=False,
    )
```

profile of v0, /device:TPU:0, one launch (start us, length us, event | category | flops | bytes accessed | tf_op | source)
XLA Modules:
  0.0 947.6 jit_solution(3835000794750805898)
XLA Ops:
  9.7 42.1 %all-reduce.6 = (bf16[768]{0:T(1024)(128)(2,1)S(1)}, bf16[768]{0:T(1024)(128)(2,1)S(1)}) all-reduce(bf16[768]{0:T(1024)(128)(2,1)S(1)} %dynamic-update-slice, bf16[768]{0:T(1024)(128)(2,1)S(1)} %dynamic-update-slice.1), channel_id=1, replica_groups=mesh['ctx'=8,'exp'=4] {'ctx','exp'}, use_global_device_ids=true, to_apply=%add | all-reduce | flops 1536 | bytes 6144
  52.9 20.9 %all-gather.8.cloned.1.call-done = bf16[768,2304]{1,0:T(8,128)(2,1)} async-done(((bf16[24,2304]{1,0:T(8,128)(2,1)}), bf16[768,2304]{1,0:T(8,128)(2,1)}) %all-gather.8.cloned.1.call-update) | async-done | bytes 3538960 | tf_op jit(solution)/shard_map/all_gather | solution.py:102
  73.8 2.8 fusion.29
  82.3 5.4 add.168
  87.7 11.6 %add.169 = f32[12,128,1024]{2,1,0:T(8,128)} reshape(f32[12,2,64,16,64]{4,3,2,1,0:T(8,128)} %add.168) | data formatting | bytes 12582912 | tf_op jit(solution)/shard_map/while/body/eval_jaxpr/add | solution.py:47
  100.9 35.9 %all-gather.16.cloned.1.call-done = bf16[1,1024,1536]{2,1,0:T(8,128)(2,1)} async-done(((bf16[1,128,1536]{2,1,0:T(8,128)(2,1)}), bf16[1,1024,1536]{2,1,0:T(8,128)(2,1)}) %all-gather.16.cloned.1.call-update) | async-done | bytes 3145744 | tf_op jit(solution)/shard_map/while/body/eval_jaxpr/all_gather | solution.py:126
  136.8 3.2 fusion.103
  143.5 4.3 fusion.104
  150.5 1.8 fusion.47
  152.4 40.1 %all-gather.10.cloned.1.call-done = bf16[768,768]{1,0:T(8,128)(2,1)} async-done(((bf16[24,768]{1,0:T(8,128)(2,1)}), bf16[768,768]{1,0:T(8,128)(2,1)}) %all-gather.10.cloned.1.call-update) | async-done | bytes 1179664 | tf_op jit(solution)/shard_map/all_gather | solution.py:103
  195.9 4.1 all-to-all-start
  202.9 41.5 %all-gather.1 = bf16[32,24,4]{1,2,0:T(4,128)(2,1)S(1)} all-gather(bf16[1,24,4]{1,2,0:T(4,128)(2,1)S(1)} %bitcast.207), channel_id=1, replica_groups=mesh['ctx'=8,'exp'=4] {'ctx','exp'}, dimensions={0}, use_global_device_ids=true | all-gather | bytes 6336 | tf_op jit(solution)/shard_map/all_gather | solution.py:104
  248.7 24.8 %all-gather.12.cloned.1.call-done = bf16[1,768,3072]{2,1,0:T(8,128)(2,1)} async-done(((bf16[1,96,3072]{2,1,0:T(8,128)(2,1)}), bf16[1,768,3072]{2,1,0:T(8,128)(2,1)}) %all-gather.12.cloned.1.call-update) | async-done | bytes 4718608 | tf_op jit(solution)/shard_map/all_gather | solution.py:108
  273.5 6.1 fusion.6
  279.6 74.0 %all-gather.14.cloned.1.call-done = bf16[1,3072,768]{2,1,0:T(8,128)(2,1)} async-done(((bf16[1,384,768]{2,1,0:T(8,128)(2,1)}), bf16[1,3072,768]{2,1,0:T(8,128)(2,1)}) %all-gather.14.cloned.1.call-update) | async-done | bytes 4718608 | tf_op jit(solution)/shard_map/all_gather | solution.py:109
  353.6 6.7 fusion.42
  360.3 4.1 all-to-all-start.1
  365.9 7.1 all-to-all-done.1
  373.0 2.4 multiply_reduce_fusion.1
  380.1 3.5 all-to-all-start.2
  385.3 6.7 all-to-all-done.2
  392.0 7.5 fusion.18
  399.6 5.6 fusion.39
  405.1 4.1 all-to-all-start.3
  410.4 2.5 reshape.880
  414.1 2.9 multiply_reduce_fusion.2
  419.4 1.8 fusion.56
  421.8 2.0 fusion.52
  425.3 4.3 multiply_reduce_fusion
  433.3 2.0 pad_maximum_fusion
  435.3 4.6 copy.82
  440.0 7.3 fusion.11
  447.4 6.5 fusion.10
  454.2 2.9 fusion.67
  457.3 3.3 fusion.46
  460.6 51.7 %reduce-scatter.17.cloned.1.call-done = bf16[128,1536]{1,0:T(8,128)(2,1)} async-done(((bf16[1024,1536]{1,0:T(8,128)(2,1)}), bf16[128,1536]{1,0:T(8,128)(2,1)}) %reduce-scatter.17.cloned.1.call-update) | async-done | bytes 393232
  512.3 1.9 copy.83
  514.2 5.1 fusion.59
  520.8 6.9 reshape.894
  527.7 5.6 reduce_sum.237
  533.6 3.5 fusion.51
  537.1 42.0 %all-reduce.5 = (f32[768]{0:T(1024)S(1)}, f32[32,12]{0,1:T(8,128)}, f32[768]{0:T(1024)S(1)}, f32[768,4]{0,1:T(4,128)S(1)}) all-reduce(f32[768]{0:T(1024)S(1)} %get-tuple-element.58, f32[32,12]{0,1:T(8,128)S(1)} %convolution_bitcast_fusion.2, f32[768]{0:T(1024)S(1)} %copy-done.24, ...), channel_id=4, replica_groups=mesh['ctx'=8,'exp'=4] {'ctx','exp'}, use_global_device_ids=true, to_apply=%region_22.23.clone | all-reduce | flops 4992 | bytes 39936
  581.9 29.8 %reduce-scatter.15.cloned.1.call-done = bf16[1,384,768]{2,1,0:T(8,128)(2,1)} async-done(((bf16[1,3072,768]{2,1,0:T(8,128)(2,1)}), bf16[1,384,768]{2,1,0:T(8,128)(2,1)}) %reduce-scatter.15.cloned.1.call-update) | async-done | bytes 589840 | tf_op jit(solution)/shard_map/reduce_scatter | solution.py:225
  611.6 2.2 convert_element_type.198
  613.8 96.7 %reduce-scatter.13.cloned.1.call-done = bf16[1,96,3072]{2,1,0:T(8,128)(2,1)} async-done(((bf16[1,768,3072]{2,1,0:T(8,128)(2,1)}), bf16[1,96,3072]{2,1,0:T(8,128)(2,1)}) %reduce-scatter.13.cloned.1.call-update) | async-done | bytes 589840 | tf_op jit(solution)/shard_map/reduce_scatter | solution.py:222
  710.5 2.2 convert_element_type.195
  712.7 102.4 %reduce-scatter.11.cloned.1.call-done = f32[24,768]{1,0:T(8,128)} async-done(((f32[768,768]{1,0:T(8,128)}), f32[24,768]{1,0:T(8,128)}) %reduce-scatter.11.cloned.1.call-update) | async-done | bytes 73744 | tf_op jit(solution)/shard_map/reduce_scatter | solution.py:320
  815.1 125.3 %reduce-scatter.9.cloned.1.call-done = f32[24,2304]{1,0:T(8,128)} async-done(((f32[768,2304]{1,0:T(8,128)}), f32[24,2304]{1,0:T(8,128)}) %reduce-scatter.9.cloned.1.call-update) | async-done | bytes 221200 | tf_op jit(solution)/shard_map/reduce_scatter | solution.py:317
  (195 shorter events, 50.5 us)
Async XLA Ops:
  7.2 74.8 %copy-start = (f32[32,12]{0,1:T(8,128)S(1)}, f32[32,12]{0,1:T(8,128)}, u32[]{:S(2)}) copy-start(f32[32,12]{0,1:T(8,128)} %param.16) | copy-start | bytes 4612
  7.2 72.1 %copy-start.31 = (s32[1,128,2]{1,2,0:T(2,128)S(1)}, s32[1,128,2]{1,2,0:T(2,128)}, u32[]{:S(2)}) copy-start(s32[1,128,2]{1,2,0:T(2,128)} %param.21) | copy-start | bytes 3076
  7.2 73.8 %copy-start.38 = (s32[8]{0:T(128)S(1)}, s32[8]{0:T(128)}, u32[]{:S(2)}) copy-start(s32[8]{0:T(128)} %param.22) | copy-start | bytes 100
  7.2 66.6 %all-gather.8.cloned.1.call-start = ((), (), s32[]{:S(2)}) async-start(), calls=%async_computation.9 | async-start | bytes 3649536 | tf_op jit(solution)/shard_map/all_gather | solution.py:102
  7.9 128.9 %all-gather.16.cloned.1.call-start = ((), (), s32[]{:S(2)}) async-start(), calls=%async_computation.17 | async-start | bytes 3538944 | tf_op jit(solution)/shard_map/while/body/eval_jaxpr/all_gather | solution.py:126
  52.8 28.1 %copy-start.35 = (f32[128]{0:T(128)}, f32[128]{0:T(128)S(1)}, u32[]{:S(2)}) copy-start(f32[128]{0:T(128)S(1)} %fusion.54) | copy-start | bytes 1540
  52.8 25.9 %copy-start.28 = (f32[128]{0:T(128)}, f32[128]{0:T(128)S(1)}, u32[]{:S(2)}) copy-start(f32[128]{0:T(128)S(1)} %fusion.96) | copy-start | bytes 1540
  77.4 115.0 %all-gather.10.cloned.1.call-start = ((), (), s32[]{:S(2)}) async-start(), calls=%async_computation.10 | async-start | bytes 1216512 | tf_op jit(solution)/shard_map/all_gather | solution.py:103
  78.1 195.3 %all-gather.12.cloned.1.call-start = ((), (), s32[]{:S(2)}) async-start(), calls=%async_computation.11 | async-start | bytes 5308416 | tf_op jit(solution)/shard_map/all_gather | solution.py:108
  78.7 274.8 %all-gather.14.cloned.1.call-start = ((), (), s32[]{:S(2)}) async-start(), calls=%async_computation.12 | async-start | bytes 5308416 | tf_op jit(solution)/shard_map/all_gather | solution.py:109
  79.4 20.4 %copy-start.13 = (s32[1,128,2]{2,1,0:T(8,128)}, s32[1,128,2]{2,1,0:T(8,128)S(1)}, u32[]{:S(2)}) copy-start(s32[1,128,2]{2,1,0:T(8,128)S(1)} %copy.67) | copy-start | bytes 3076
  79.6 20.1 %copy-start.25 = (s32[256]{0:T(256)}, s32[256]{0:T(256)S(1)}, u32[]{:S(2)}) copy-start(s32[256]{0:T(256)S(1)} %reshape.872) | copy-start | bytes 3076
  99.7 42.1 %copy-start.26 = (s32[256]{0:T(256)}, s32[256]{0:T(256)S(1)}, u32[]{:S(2)}) copy-start(s32[256]{0:T(256)S(1)} %fusion.82) | copy-start | bytes 3076
  100.9 42.5 %copy-start.10 = (bf16[1,128,768]{1,2,0:T(8,128)(2,1)}, bf16[1,128,768]{1,2,0:T(8,128)(2,1)S(1)}, u32[]{:S(2)}) copy-start(bf16[1,128,768]{1,2,0:T(8,128)(2,1)S(1)} %copy.64) | copy-start | bytes 589828
  141.8 6.0 copy-start.3
  147.8 4.5 copy-start.19
  150.5 42.0 %copy-start.4 = (bf16[1,128,768]{2,1,0:T(8,128)(2,1)S(1)}, bf16[1,128,768]{2,1,0:T(8,128)(2,1)}, u32[]{:S(2)}) copy-start(bf16[1,128,768]{2,1,0:T(8,128)(2,1)} %param.12) | copy-start | bytes 589828
  150.5 44.3 %copy-start.18 = (bf16[128,320]{0,1:T(8,128)(2,1)S(1)}, bf16[128,320]{0,1:T(8,128)(2,1)}, u32[]{:S(2)}) copy-start(bf16[128,320]{0,1:T(8,128)(2,1)} %fusion.70) | copy-start | bytes 245764
  152.3 47.7 %copy-start.14 = (bf16[12,64,128]{2,1,0:T(8,128)(2,1)}, bf16[12,64,128]{2,1,0:T(8,128)(2,1)S(1)}, u32[]{:S(2)}) copy-start(bf16[12,64,128]{2,1,0:T(8,128)(2,1)S(1)} %fusion.47) | copy-start | bytes 589828
  152.3 47.7 %copy-start.9 = (f32[1,128,768]{2,1,0:T(8,128)S(1)}, f32[1,128,768]{2,1,0:T(8,128)}, u32[]{:S(2)}) copy-start(f32[1,128,768]{2,1,0:T(8,128)} %param.23) | copy-start | bytes 1179652
  192.5 10.5 %copy-start.32 = (bf16[24,4]{0,1:T(4,128)(2,1)S(1)}, bf16[24,4]{0,1:T(4,128)(2,1)}, u32[]{:S(2)}) copy-start(bf16[24,4]{0,1:T(4,128)(2,1)} %param.18) | copy-start | bytes 580
  194.7 49.7 %copy-start.30 = (f32[128]{0:T(128)}, f32[128]{0:T(128)S(1)}, u32[]{:S(2)}) copy-start(f32[128]{0:T(128)S(1)} %fusion.97) | copy-start | bytes 1540
  195.9 77.6 %all-to-all-start = ((bf16[4,80,768]{2,1,0:T(8,128)(2,1)}), bf16[4,80,768]{2,1,0:T(8,128)(2,1)}, u32[]{:S(2)}, u32[]{:S(2)}) async-start(bf16[4,80,768]{2,1,0:T(8,128)(2,1)} %bitcast.21), calls=%async_computation | async-start | bytes 983040 | tf_op jit(solution)/shard_map/all_to_all | solution.py:171
  245.9 118.5 %copy-start.20 = (bf16[768,4]{0,1:T(4,128)(2,1)}, bf16[768,4]{0,1:T(4,128)(2,1)S(1)}, u32[]{:S(2)}) copy-start(bf16[768,4]{0,1:T(4,128)(2,1)S(1)} %reshape.901) | copy-start | bytes 18436
  360.3 12.7 %all-to-all-start.1 = ((bf16[4,80,768]{2,1,0:T(8,128)(2,1)}), bf16[4,80,768]{2,1,0:T(8,128)(2,1)}, u32[]{:S(2)}, u32[]{:S(2)}) async-start(bf16[4,80,768]{2,1,0:T(8,128)(2,1)} %fusion.42), calls=%async_computation.1 | async-start | bytes 983040 | tf_op jit(solution)/shard_map/all_to_all | solution.py:177
  365.3 7.6 copy-start.27
  377.8 21.7 %copy-start.16 = (f32[128,2]{1,0:T(8,128)}, f32[128,2]{1,0:T(8,128)S(1)}, u32[]{:S(2)}) copy-start(f32[128,2]{1,0:T(8,128)S(1)} %copy.70) | copy-start | bytes 3076
  380.1 11.9 %all-to-all-start.2 = ((bf16[4,80,768]{2,1,0:T(8,128)(2,1)}), bf16[4,80,768]{2,1,0:T(8,128)(2,1)S(1)}, u32[]{:S(2)}, u32[]{:S(2)}) async-start(bf16[4,80,768]{2,1,0:T(8,128)(2,1)} %bitcast.31), calls=%async_computation.2 | async-start | bytes 983040 | tf_op jit(solution)/shard_map/all_to_all | solution.py:199
  392.0 7.5 copy-start.17
  399.6 5.6 copy-start.39
  405.1 12.7 %all-to-all-start.3 = ((bf16[4,80,768]{2,1,0:T(8,128)(2,1)}), bf16[4,80,768]{2,1,0:T(8,128)(2,1)}, u32[]{:S(2)}, u32[]{:S(2)}) async-start(bf16[4,80,768]{2,1,0:T(8,128)(2,1)} %bitcast.205), calls=%async_computation.3 | async-start | bytes 983040 | tf_op jit(solution)/shard_map/all_to_all | solution.py:214
  409.3 15.3 %copy-start.8 = (bf16[768,768]{1,0:T(8,128)(2,1)S(1)}, bf16[768,768]{1,0:T(8,128)(2,1)}, u32[]{:S(2)}) copy-start(bf16[768,768]{1,0:T(8,128)(2,1)} %all-gather.10.cloned.1.call-done) | copy-start | bytes 3538948
  409.3 103.0 %reduce-scatter.17.cloned.1.call-start = ((), (), s32[]{:S(2)}) async-start(), calls=%async_computation.18 | async-start | bytes 3538944
  425.3 4.3 slice-start
  425.3 4.7 slice-start.1
  439.9 171.7 %reduce-scatter.15.cloned.1.call-start = ((), (), s32[]{:S(2)}) async-start(), calls=%async_computation.16 | async-start | bytes 5308416 | tf_op jit(solution)/shard_map/reduce_scatter | solution.py:225
  447.4 263.1 %reduce-scatter.13.cloned.1.call-start = ((), (), s32[]{:S(2)}) async-start(), calls=%async_computation.15 | async-start | bytes 5308416 | tf_op jit(solution)/shard_map/reduce_scatter | solution.py:222
  453.9 361.2 %reduce-scatter.11.cloned.1.call-start = ((), (), s32[]{:S(2)}) async-start(), calls=%async_computation.14 | async-start | bytes 2433024 | tf_op jit(solution)/shard_map/reduce_scatter | solution.py:320
  457.2 57.0 %copy-start.29 = (f32[128]{0:T(128)S(1)}, f32[128]{0:T(128)}, u32[]{:S(2)}) copy-start(f32[128]{0:T(128)} %copy-done.28) | copy-start | bytes 1540
  457.2 483.2 %reduce-scatter.9.cloned.1.call-start = ((), (), s32[]{:S(2)}) async-start(), calls=%async_computation.13 | async-start | bytes 7299072 | tf_op jit(solution)/shard_map/reduce_scatter | solution.py:317
  527.7 5.6 copy-start.34
  527.7 5.9 copy-start.12
  527.7 5.9 copy-start.15
  533.3 3.8 copy-start.21
  533.3 3.8 copy-start.24
  533.3 47.6 %copy-start.36 = (f32[128]{0:T(128)S(1)}, f32[128]{0:T(128)}, u32[]{:S(2)}) copy-start(f32[128]{0:T(128)} %copy-done.35) | copy-start | bytes 1540
  533.3 47.6 %copy-start.7 = (f32[1,128,768]{2,1,0:T(8,128)S(1)}, f32[1,128,768]{2,1,0:T(8,128)}, u32[]{:S(2)}) copy-start(f32[1,128,768]{2,1,0:T(8,128)} %copy-done.6) | copy-start | bytes 1179652
  533.3 407.0 %copy-start.1 = (f32[32,12]{0,1:T(8,128)S(1)}, f32[32,12]{0,1:T(8,128)}, u32[]{:S(2)}) copy-start(f32[32,12]{0,1:T(8,128)} %param.16) | copy-start | bytes 4612
  (8 other events, 12.3 us)
Sparse Core Ops, SparseCore 0:
  10.9 62.8 all-gather.7
  77.5 59.2 all-gather.15
  139.7 52.6 all-gather.9
  194.5 78.9 all-gather.11
  275.5 78.0 all-gather.13
  440.1 72.1 reduce-scatter.16
  515.9 95.6 reduce-scatter.14
  615.3 95.1 reduce-scatter.12
  716.4 98.6 reduce-scatter.10
  822.2 118.1 reduce-scatter.8
where the time goes:
time: 957 us; the launch traced here: 948 us
  waiting for transfers between devices  619 us (65%)
  blocking collectives  126 us (13%)
  matrix products  81.8 us (9%)
  local copies, waits for them, and re-layouts  57.2 us (6%)
  other arithmetic  32.3 us (3%)
  starting transfers between devices  16.7 us (2%)
  between operations  15.3 us (2%)
    reduce_scatter x1, waiting for transfers between devices, body(): lax.psum_scatter(query_key_value_weight_gradient, ('ctx', 'exp'), scatter...  125 us
    reduce_scatter x1, waiting for transfers between devices, body(): lax.psum_scatter(grad_attn_out, ('ctx', 'exp'), scatter_dimension=0, tile...  102 us
    reduce_scatter x1, waiting for transfers between devices, body(): lax.psum_scatter(grad_first[None].astype(jnp.bfloat16), 'ctx', scatter_di...  96.7 us
    unnamed x2, blocking collectives  84.1 us
    all_gather x1, waiting for transfers between devices, body(): lax.all_gather(w_out, 'ctx', axis=1, tiled=True)  74 us
    unnamed x11, waiting for transfers between devices  54.2 us
    all_gather x1, blocking collectives, body(): lax.all_gather(w_router, ('ctx', 'exp'), axis=0, tiled=True)  41.5 us
    all_gather x1, waiting for transfers between devices, body(): lax.all_gather(attention_output_weight, ('ctx', 'exp'), axis=0, tiled=True)  40.1 us
  transfers between devices with their start and end apart: 14, of which 13 were waited for; matrix products, arithmetic and copies ran while one was open for 12% of the time, Pallas kernels for 0%

commit v1 on v0

v1 whole, which is shorter than its diff:
```python
import jax
import jax.numpy as jnp
from jax import lax
from jax.sharding import Mesh, PartitionSpec as P

PRECISION_FULL = lax.Precision.HIGHEST
MASKED = -1e30
LOW = jnp.bfloat16
WIDE = jnp.float32
EPS = 1e-06


def dot(left, right, contract):
    return lax.dot_general(left, right, (contract, ((), ())), preferred_element_type=WIDE)


def shift(x, axis, d):
    n = lax.axis_size(axis)
    return lax.ppermute(x, axis, [((j + d) % n, j) for j in range(n)])


def swap(x, axes, k):
    n = 1
    for axis in axes:
        n *= lax.axis_size(axis)
    return lax.ppermute(x, axes, [(j ^ k, j) for j in range(n)])


def from_xor(blocks, me):
    step = 1
    while step < len(blocks):
        flip = (me & step) != 0
        blocks = [jnp.where(flip, blocks[j ^ step], blocks[j]) for j in range(len(blocks))]
        step *= 2
    return blocks


def from_cyclic(blocks, me):
    n, step = len(blocks), 1
    while step < n:
        move = (me & step) != 0
        blocks = [jnp.where(move, blocks[(j - step) % n], blocks[j]) for j in range(n)]
        step *= 2
    return blocks


def pick(stack, index):
    return lax.dynamic_index_in_dim(stack, index, 0, keepdims=False)


def layer_gather(block):
    yx_count = lax.axis_size("yy") * lax.axis_size("xx")
    me_yx = lax.axis_index("yy") * lax.axis_size("xx") + lax.axis_index("xx")
    blocks = [block] + [swap(block, ("yy", "xx"), k) for k in range(1, yx_count)]
    joined = jnp.stack(from_xor(blocks, me_yx))
    both = from_xor([joined, swap(joined, ("cc",), 1)], lax.axis_index("cc"))
    full = jnp.stack(both)
    cores, layers, outer, rows, width = full.shape
    return full.transpose(2, 1, 0, 3, 4).reshape(outer * layers * cores * rows, width)


def layer_reduce(part):
    outer, yx = lax.axis_size("hz"), lax.axis_size("yy") * lax.axis_size("xx")
    me_yx = lax.axis_index("yy") * lax.axis_size("xx") + lax.axis_index("xx")
    cores = lax.axis_size("cc")
    me_c = lax.axis_index("cc")
    rows = part.shape[0] // (outer * yx * cores)
    split = part.reshape(outer, yx, cores, rows, part.shape[1]).transpose(2, 1, 0, 3, 4)
    other = swap(pick(split, 1 - me_c).astype(LOW), ("cc",), 1)
    mine = pick(split, me_c).astype(WIDE) + other.astype(WIDE)
    low = mine.astype(LOW)
    total = pick(mine, me_yx)
    for k in range(1, yx):
        total = total + swap(pick(low, me_yx ^ k), ("yy", "xx"), k).astype(WIDE)
    return total


def line_gather(block):
    n = lax.axis_size("hz")
    right, left = block, block
    from_left, from_right = [None] * n, [None] * n
    for s in range(1, n):
        right = lax.ppermute(right, "hz", [(i, i + 1) for i in range(s - 1, n - 1)])
        left = lax.ppermute(left, "hz", [(i, i - 1) for i in range(1, n - s + 1)])
        from_left[s], from_right[s] = right, left
    return [block] + [from_right[d] + from_left[n - d] for d in range(1, n)]


def line_reduce(blocks):
    n = lax.axis_size("hz")
    right = left = None
    for s in range(1, n):
        send_right, send_left = blocks[n - s], blocks[s]
        if s > 1:
            send_right = (send_right.astype(WIDE) + right.astype(WIDE)).astype(LOW)
            send_left = (send_left.astype(WIDE) + left.astype(WIDE)).astype(LOW)
        right = lax.ppermute(send_right, "hz", [(i, i + 1) for i in range(s)])
        left = lax.ppermute(send_left, "hz", [(i, i - 1) for i in range(n - s, n)])
    return blocks[0].astype(WIDE) + right.astype(WIDE) + left.astype(WIDE)


def three_terms(x):
    high = lax.reduce_precision(x, 8, 7)
    rest = x - high
    middle = lax.reduce_precision(rest, 8, 7)
    return high.astype(LOW), middle.astype(LOW), (rest - middle).astype(LOW)


def body(
    activations,
    gain_one,
    query_key_value_weight,
    attention_output_weight,
    pos_table,
    gain_two,
    w_router,
    w_in,
    w_out,
    routes,
    pair_of_device,
    cotangent,
):
    Z, Y = lax.axis_size("hz"), lax.axis_size("yy")
    X, C = lax.axis_size("xx"), lax.axis_size("cc")
    E, N = X * C, Z * Y
    z, y = lax.axis_index("hz"), lax.axis_index("yy")
    me_e = lax.axis_index("xx") * C + lax.axis_index("cc")
    _, own_rows, D = activations.shape
    half = own_rows // 2
    buckets, heads = pos_table.shape
    hd = D // heads
    hg = heads // Z
    gw = hg * hd
    top = routes.shape[2]
    shard = gain_one.shape[0]
    FF = w_in.shape[2]
    capacity = max(2, 5 * own_rows * top // (4 * E))

    acts = activations[0]
    act_blocks = [acts] + [shift(acts, "hz", d) for d in range(1, Z)]
    qkv_w = query_key_value_weight.reshape(shard, 3, Z, gw).transpose(2, 0, 1, 3)
    small = jnp.concatenate([gain_one[:, None], gain_two[:, None], w_router], axis=1)
    small_width = -(-(gw + small.shape[1]) // 128) * 128 - gw
    small = jnp.pad(small, ((0, 0), (0, small_width - small.shape[1])))
    small = jnp.broadcast_to(small[None], (Z, shard, small_width))
    payload = jnp.concatenate([qkv_w[:, :, 1], qkv_w[:, :, 2], qkv_w[:, :, 0], small], axis=-1)
    pieces = [pick(payload, z)] + [
        shift(pick(payload, (z - d) % Z), "hz", d) for d in range(1, Z)
    ]
    w_all = layer_gather(jnp.stack(from_cyclic(pieces, z)))

    w_in_split = w_in[0].reshape(D // N, Z, Y, FF // N).transpose(2, 0, 1, 3)
    w_in_split = w_in_split.reshape(Y, D // N, FF // Y)
    in_rows = [pick(w_in_split, y)] + [
        swap(pick(w_in_split, y ^ k), ("yy",), k) for k in range(1, Y)
    ]
    in_rows = jnp.concatenate(from_xor(in_rows, y), axis=0)
    in_blocks = line_gather(in_rows)
    out_blocks = line_gather(w_out[0])

    def place(blocks):
        rows = blocks[0].shape[0]
        whole = jnp.zeros((Z * rows, blocks[0].shape[1]), LOW)
        for d in range(Z):
            whole = lax.dynamic_update_slice(whole, blocks[d], (((z + d) % Z) * rows, 0))
        return whole

    attn_w_pieces = [attention_output_weight] + [
        shift(attention_output_weight, "hz", d) for d in range(1, Z)
    ]
    w_attn_out = layer_gather(jnp.stack(from_cyclic(attn_w_pieces, z)))

    gain_first = w_all[:, 3 * gw].astype(WIDE)
    gain_second = w_all[:, 3 * gw + 1].astype(WIDE)
    router = w_all[:, 3 * gw + 2 : 3 * gw + 2 + E]

    def first_of(owner):
        lanes = lax.broadcasted_iota(jnp.int32, (N,), 0)
        return jnp.sum(jnp.where(lanes == owner, pair_of_device, 0))

    def tiles_of(k):
        found = []
        for d in range(Z):
            first = first_of(((z + d) % Z) * Y + (y ^ k))
            found += [first, 2 * N - 1 - first]
        return found

    key_tile_list = [t for k in range(Y) for t in tiles_of(k)]
    key_tiles = jnp.stack(key_tile_list)
    query_tiles = key_tiles[: 2 * Z]
    n_q, n_k = 2 * Z, 2 * Z * Y
    within = lax.broadcasted_iota(jnp.int32, (1, half), 1)
    query_pos = (query_tiles[:, None] * half + within).reshape(-1)
    key_pos = (key_tiles[:, None] * half + within).reshape(-1)
    bucket = jnp.clip(query_tiles[:, None] - key_tiles[None, :], 0, buckets - 1)
    levels = lax.broadcasted_iota(jnp.int32, (n_q, n_k, buckets), 2)
    bucket_hot = bucket[:, :, None] == levels
    own_table = lax.dynamic_slice(pos_table, (0, z * hg), (buckets, hg)).T
    tile_bias = jnp.sum(jnp.where(bucket_hot[None], own_table[:, None, None, :], 0.0), axis=-1)
    bias_terms = jnp.concatenate(three_terms(tile_bias), axis=-1)
    bias_rows = jnp.broadcast_to(
        bias_terms[:, :, None, :], (hg, n_q, half, 3 * n_k)
    ).reshape(hg, n_q * half, 3 * n_k)
    key_hot = (
        lax.broadcasted_iota(jnp.int32, (n_k * half, n_k), 0) // half
        == lax.broadcasted_iota(jnp.int32, (n_k * half, n_k), 1)
    ).astype(LOW)

    x_rows = jnp.concatenate(act_blocks, axis=0).astype(WIDE)
    scale_one = lax.rsqrt(jnp.mean(x_rows * x_rows, axis=-1, keepdims=True) + EPS)
    hat_one = x_rows * scale_one
    normed_one = (hat_one * gain_first).astype(LOW)
    w_kv, w_q = w_all[:, : 2 * gw], w_all[:, 2 * gw : 3 * gw]
    kv = dot(normed_one, w_kv, ((1,), (0,))).astype(LOW)
    kv_all = jnp.concatenate([kv] + [swap(kv, ("yy",), k) for k in range(1, Y)], axis=0)
    q = dot(normed_one, w_q, ((1,), (0,))).astype(LOW)

    def by_head(rows):
        return rows.reshape(rows.shape[0], hg, hd).transpose(1, 0, 2)

    q_heads = by_head(q) * jnp.asarray(hd**-0.5, LOW)
    k_heads, v_heads = by_head(kv_all[:, :gw]), by_head(kv_all[:, gw:])
    q_wide = jnp.concatenate([q_heads, bias_rows], axis=-1)
    k_hot = jnp.broadcast_to(key_hot[None], (hg,) + key_hot.shape)
    k_wide = jnp.concatenate([k_heads, k_hot, k_hot, k_hot], axis=-1)
    scores = jnp.einsum("hqe,hke->hqk", q_wide, k_wide, preferred_element_type=WIDE)
    visible = query_pos[:, None] >= key_pos[None, :]
    scores = jnp.where(visible[None], scores, MASKED)
    weights = jnp.exp(scores - jnp.max(scores, axis=-1, keepdims=True))
    probs = weights / jnp.sum(weights, axis=-1, keepdims=True)
    probs_low = probs.astype(LOW)
    mixed_heads = jnp.einsum("hqk,hke->qhe", probs_low, v_heads, preferred_element_type=WIDE)
    mixed = mixed_heads.reshape(Z, own_rows, gw).astype(LOW)
    mixed_back = [mixed[0]] + [shift(mixed[d], "hz", -d) for d in range(1, Z)]
    mixed_back = from_cyclic([mixed_back[-d % Z] for d in range(Z)], z)
    mixed_full = jnp.concatenate(mixed_back, axis=-1)

    own_x = acts.astype(WIDE)
    resid = own_x + dot(mixed_full, w_attn_out, ((1,), (0,)))
    scale_two = lax.rsqrt(jnp.mean(resid * resid, axis=-1, keepdims=True) + EPS)
    hat_two = resid * scale_two
    normed_two = (hat_two * gain_second).astype(LOW)

    relative = routes[0] ^ me_e
    flat = relative.reshape(own_rows * top)
    expert_iota = lax.broadcasted_iota(jnp.int32, (1, E), 1)
    hits = (flat[:, None] == expert_iota).astype(LOW)
    earlier = (
        lax.broadcasted_iota(jnp.int32, (own_rows * top, own_rows * top), 0)
        > lax.broadcasted_iota(jnp.int32, (own_rows * top, own_rows * top), 1)
    ).astype(LOW)
    before = dot(earlier, hits, ((1,), (0,)))
    rank = jnp.sum(before * hits.astype(WIDE), axis=-1).astype(jnp.int32)
    target = flat * capacity + rank
    slot_iota = lax.broadcasted_iota(jnp.int32, (1, E * capacity), 1)
    route_map = (target[:, None] == slot_iota).astype(LOW)
    per_token = route_map.reshape(own_rows, top, E * capacity).sum(axis=1)
    chosen_mask = (routes[0][..., None] == expert_iota[None]).astype(WIDE)

    group = ("yy", "xx", "cc")

    def exchange(slots):
        blocks = slots.reshape(E, capacity, slots.shape[1])
        got = [
            blocks[k] if j == 0 and k == 0 else swap(blocks[k], group, j * E + k)
            for j in range(Y)
            for k in range(E)
        ]
        return jnp.concatenate(got, axis=0)

    def give_back(rows):
        blocks = rows.reshape(Y, E, capacity, rows.shape[1])
        summed = []
        for k in range(E):
            total = None
            for j in range(Y):
                block = blocks[j, k]
                if j or k:
                    block = swap(block, group, j * E + k)
                block = block.astype(WIDE)
                total = block if total is None else total + block
            summed.append(total.astype(LOW))
        return jnp.concatenate(summed, axis=0)

    rows = exchange(dot(per_token, normed_two, ((0,), (0,))).astype(LOW))
    router_logits = dot(normed_two, router, ((1,), (0,)))
    chosen = jnp.sum(chosen_mask * router_logits[:, None, :], axis=-1)
    gates = jax.nn.softmax(chosen, axis=-1)
    cot = cotangent[0]
    grad_picked = (gates[..., None] * cot[:, None, :]).astype(LOW)
    grad_picked = grad_picked.reshape(own_rows * top, D)
    grad_rows = exchange(dot(route_map, grad_picked, ((0,), (0,))).astype(LOW))

    w_first, w_second = place(in_blocks), place(out_blocks)
    hidden = dot(rows, w_first, ((1,), (0,)))
    active, gelu_back = jax.vjp(jax.nn.gelu, hidden)
    active = active.astype(LOW)
    answer = dot(active, w_second, ((1,), (0,))).astype(LOW)
    grad_active = dot(grad_rows, w_second, ((1,), (1,)))
    grad_hidden = gelu_back(grad_active)[0].astype(LOW)
    grad_copy = dot(grad_hidden, w_first, ((1,), (1,))).astype(LOW)
    returned = give_back(answer)
    coming = give_back(grad_copy)

    part_ff, part_d = FF // N, D // Z
    grad_out_blocks = [
        dot(
            lax.dynamic_slice_in_dim(active, ((z + d) % Z) * part_ff, part_ff, 1),
            grad_rows,
            ((0,), (0,)),
        ).astype(LOW)
        for d in range(Z)
    ]
    rows_t = rows.T
    grad_in_blocks = [
        dot(
            lax.dynamic_slice_in_dim(rows_t, ((z + d) % Z) * part_d, part_d, 0),
            grad_hidden,
            ((1,), (0,)),
        ).astype(LOW)
        for d in range(Z)
    ]

    picked = dot(route_map, returned, ((1,), (0,))).reshape(own_rows, top, D)
    output = resid + jnp.sum(gates[..., None] * picked, axis=1)
    grad_gates = jnp.sum(picked * cot[:, None, :], axis=-1)
    grad_chosen = gates * (grad_gates - jnp.sum(gates * grad_gates, axis=-1, keepdims=True))
    logit_gradient = jnp.sum(grad_chosen[..., None] * chosen_mask, axis=1)
    grad_normed_two = dot(per_token, coming, ((1,), (0,))) + jnp.einsum(
        "te,de->td", logit_gradient, router.astype(WIDE), precision=PRECISION_FULL
    )
    grad_router = jnp.einsum(
        "td,te->de", normed_two.astype(WIDE), logit_gradient, precision=PRECISION_FULL
    )
    grad_gain_two = jnp.sum(grad_normed_two * hat_two, axis=0)
    grad_hat = grad_normed_two * gain_second
    grad_resid = cot + scale_two * (
        grad_hat - hat_two * jnp.mean(grad_hat * hat_two, axis=-1, keepdims=True)
    )
    grad_attention = grad_resid.astype(LOW)
    grad_attn_out = dot(mixed_full, grad_attention, ((0,), (0,)))
    grad_mixed = lax.dot_general(
        w_attn_out.reshape(Z, gw, D),
        grad_attention,
        (((2,), (1,)), ((), ())),
        preferred_element_type=WIDE,
    ).transpose(0, 2, 1).astype(LOW)
    grad_mixed_rows = jnp.concatenate(
        [pick(grad_mixed, z)]
        + [shift(pick(grad_mixed, (z - d) % Z), "hz", d) for d in range(1, Z)],
        axis=0,
    )

    grad_heads = by_head(grad_mixed_rows)
    row_dot = jnp.sum(
        by_head(mixed.reshape(Z * own_rows, gw)).astype(WIDE) * grad_heads.astype(WIDE),
        axis=-1,
        keepdims=True,
    )
    grad_probs = jnp.einsum("hqe,hke->hqk", grad_heads, v_heads, preferred_element_type=WIDE)
    grad_scores = (probs_low.astype(WIDE) * (grad_probs - row_dot)).astype(LOW)
    grad_q_wide = jnp.einsum(
        "hqk,hke->hqe",
        grad_scores,
        jnp.concatenate([k_heads, k_hot], axis=-1),
        preferred_element_type=WIDE,
    )
    grad_q = grad_q_wide[..., :hd] * hd**-0.5
    tile_sums = grad_q_wide[..., hd:].reshape(hg, n_q, half, n_k).sum(axis=2)
    table_part = jnp.sum(
        jnp.where(bucket_hot[None], tile_sums[..., None], 0.0), axis=(1, 2)
    )
    grad_k = jnp.einsum("hqk,hqe->khe", grad_scores, q_heads, preferred_element_type=WIDE)
    grad_v = jnp.einsum("hqk,hqe->khe", probs_low, grad_heads, preferred_element_type=WIDE)
    grad_kv = jnp.concatenate(
        [grad_k.reshape(-1, gw), grad_v.reshape(-1, gw)], axis=1
    ).reshape(Y, Z * own_rows, 2 * gw)
    grad_kv_own = grad_kv[0]
    for k in range(1, Y):
        grad_kv_own = grad_kv_own + swap(grad_kv[k].astype(LOW), ("yy",), k).astype(WIDE)
    grad_q_rows = grad_q.transpose(1, 0, 2).reshape(-1, gw)
    grad_qkv = jnp.concatenate([grad_kv_own, grad_q_rows], axis=1).astype(LOW)

    grad_normed_part = dot(grad_qkv, w_all[:, : 3 * gw], ((1,), (1,)))
    grad_gain_one = jnp.sum(grad_normed_part * hat_one, axis=0)
    grad_low = grad_normed_part.astype(LOW).reshape(Z, own_rows, D)
    grad_normed_one = grad_normed_part[:own_rows]
    for d in range(1, Z):
        grad_normed_one = grad_normed_one + shift(grad_low[d], "hz", -d).astype(WIDE)
    own_hat = hat_one[:own_rows]
    grad_hat_one = grad_normed_one * gain_first
    grad_inputs = grad_resid + scale_one[:own_rows] * (
        grad_hat_one - own_hat * jnp.mean(grad_hat_one * own_hat, axis=-1, keepdims=True)
    )

    def pad_columns(columns):
        return jnp.pad(columns, ((0, 0), (0, 128 - columns.shape[1])))

    attn_part = jnp.concatenate(
        [grad_attn_out, pad_columns(jnp.concatenate([grad_gain_two[:, None], grad_router], 1))],
        axis=1,
    )
    attn_sum = layer_reduce(attn_part)
    attn_low = attn_sum.astype(LOW)
    attn_total = pick(attn_sum, z)
    for d in range(1, Z):
        attn_total = attn_total + shift(pick(attn_low, (z - d) % Z), "hz", d).astype(WIDE)
    shard_attn_out = attn_total[:, :D]
    shard_gain_two = attn_total[:, D]
    shard_router = attn_total[:, D + 1 : D + 1 + E]

    grad_w_qkv = dot(normed_one, grad_qkv, ((0,), (0,)))
    qkv_part = jnp.concatenate([grad_w_qkv, pad_columns(grad_gain_one[:, None])], axis=1)
    qkv_sum = layer_reduce(qkv_part)
    qkv_low = qkv_sum.astype(LOW)
    qkv_blocks = [pick(qkv_sum, z)] + [
        shift(pick(qkv_low, (z - d) % Z), "hz", d).astype(WIDE) for d in range(1, Z)
    ]
    shard_gain_one = sum(block[:, 3 * gw] for block in qkv_blocks)
    by_group = jnp.stack(from_cyclic([block[:, : 3 * gw] for block in qkv_blocks], z))
    by_group = by_group.reshape(Z, shard, 3, gw)
    shard_qkv = jnp.concatenate(
        [
            by_group[:, :, part].transpose(1, 0, 2).reshape(shard, D)
            for part in (2, 0, 1)
        ],
        axis=1,
    )

    table_sum = table_part
    table_sum = table_sum + swap(table_sum, ("cc",), 1)
    yx = ("yy", "xx")
    parts = [table_sum] + [swap(table_sum, yx, k) for k in range(1, Y * X)]
    parts = from_xor(parts, y * X + lax.axis_index("xx"))
    table_sum = sum(parts[1:], parts[0])
    tables = [table_sum] + [shift(table_sum, "hz", d) for d in range(1, Z)]
    table_total = jnp.concatenate(from_cyclic(tables, z), axis=0).T

    shard_second = line_reduce(grad_out_blocks)
    first_sum = line_reduce(grad_in_blocks).reshape(Y, D // N, FF // Y)
    first_low = first_sum.astype(LOW)
    first_parts = [pick(first_sum, y)] + [
        swap(pick(first_low, y ^ k), ("yy",), k).astype(WIDE) for k in range(1, Y)
    ]
    first_parts = jnp.stack(from_xor(first_parts, y))
    shard_first = (
        first_parts.reshape(Y, D // N, Z, part_ff).transpose(1, 2, 0, 3).reshape(D // N, FF)
    )
    return (
        output[None],
        grad_inputs[None],
        shard_gain_one,
        shard_qkv,
        shard_attn_out,
        table_total,
        shard_gain_two,
        shard_router,
        shard_first[None],
        shard_second[None],
    )


def solution(mesh):
    devices_ctx, devices_exp = mesh.shape["ctx"], mesh.shape["exp"]
    outer = 4
    parts = Mesh(
        mesh.devices.reshape(outer, devices_ctx // outer, devices_exp // 2, 2),
        ("hz", "yy", "xx", "cc"),
    )
    ctx, exp = ("hz", "yy"), ("xx", "cc")
    every = ctx + exp
    tokens = P(exp, ctx, None)
    return jax.shard_map(
        body,
        mesh=parts,
        in_specs=(
            tokens,
            P(every),
            P(every, None),
            P(every, None),
            P(),
            P(every),
            P(every, None),
            tokens,
            tokens,
            tokens,
            P(),
            tokens,
        ),
        out_specs=(
            tokens,
            tokens,
            P(every),
            P(every, None),
            P(every, None),
            P(),
            P(every),
            P(every, None),
            tokens,
            tokens,
        ),
        check_vma=False,
    )
```

time: 957 us -> 446 us (0.47)
  waiting for transfers between devices: 619 us -> 108 us
  blocking collectives: 126 us -> 0 us
  starting transfers between devices: 16.7 us -> 138 us
  matrix products: 81.8 us -> 56.3 us
  local copies, waits for them, and re-layouts: 57.2 us -> 80.8 us
  other arithmetic: 32.3 us -> 47.1 us
    reduce_scatter x4 -> x0, waiting for transfers between devices: 354 us -> none  [the longest x1 125 us: body(): lax.psum_scatter(query_key_value_weight_gradient, ('ctx', 'exp'), scatter...]
    all_gather x5 -> x0, waiting for transfers between devices: 196 us -> none  [the longest x1 74 us: body(): lax.all_gather(w_out, 'ctx', axis=1, tiled=True)]
    ppermute x0 -> x103, starting transfers between devices: none -> 138 us  [the longest x52 50.2 us: swap(): return lax.ppermute(x, axes, [(j ^ k, j) for j in range(n)])]
    ppermute x0 -> x103, waiting for transfers between devices: none -> 108 us  [the longest x52 55.1 us: swap(): return lax.ppermute(x, axes, [(j ^ k, j) for j in range(n)])]
    unnamed x2 -> x0, blocking collectives: 84.1 us -> none
    unnamed x11 -> x0, waiting for transfers between devices: 54.2 us -> none
    all_gather x1 -> x0, blocking collectives: 41.5 us -> none  [body(): lax.all_gather(w_router, ('ctx', 'exp'), axis=0, tiled=True)]
    dot_general x27 -> x33, matrix products: 81.8 us -> 56.3 us  [the longest x24 46.8 us: dot(): lax.dot_general(left, right, (contract, ((), ())), preferred_element_type...]
  transfers between devices with their start and end apart: 14 -> 103, of which waited for: 13 -> 37; matrix products, arithmetic and copies ran while one was open for 12% -> 32% of each run, Pallas kernels for 0% -> 0%
where the time goes in v1:
time: 446 us; the launch traced here: 439 us
  starting transfers between devices  138 us (31%)
  waiting for transfers between devices  108 us (24%)
  local copies, waits for them, and re-layouts  80.8 us (18%)
  matrix products  56.3 us (13%)
  other arithmetic  47.1 us (11%)
  between operations  8.05 us (2%)
    ppermute x52, waiting for transfers between devices, swap(): return lax.ppermute(x, axes, [(j ^ k, j) for j in range(n)])  55.1 us
    ppermute x52, starting transfers between devices, swap(): return lax.ppermute(x, axes, [(j ^ k, j) for j in range(n)])  50.2 us
    dot_general x24, matrix products, dot(): lax.dot_general(left, right, (contract, ((), ())), preferred_element_type...  46.8 us
    ppermute x27, starting transfers between devices, shift(): return lax.ppermute(x, axis, [((j + d) % n, j) for j in range(n)])  39.6 us
    ppermute x6, waiting for transfers between devices, line_gather(): left = lax.ppermute(left, 'hz', [(i, i - 1) for i in range(1, n - s + 1)])  32.7 us
    ppermute x6, starting transfers between devices, line_reduce(): right = lax.ppermute(send_right, 'hz', [(i, i + 1) for i in range(s)])  19.7 us
    unnamed x192, local copies, waits for them, and re-layouts  16.7 us
    ppermute x6, starting transfers between devices, line_gather(): right = lax.ppermute(right, 'hz', [(i, i + 1) for i in range(s - 1, n - 1)])  12 us
  transfers between devices with their start and end apart: 103, of which 37 were waited for; matrix products, arithmetic and copies ran while one was open for 32% of the time, Pallas kernels for 0%

profile of v1, /device:TPU:0, one launch (start us, length us, event | category | flops | bytes accessed | tf_op | source)
XLA Modules:
  0.0 438.7 jit_solution(15395160885886790015)
XLA Ops:
  0.7 4.1 collective-permute-start.15
  18.9 2.7 stack.176
  21.6 5.3 %stack.185 = s32[16]{0:T(128)S(1)} concatenate(s32[1]{0:T(128)} %bitcast.21, s32[1]{0:T(128)} %bitcast.22, s32[1]{0:T(128)} %bitcast.23, s32[1]{0:T(128)} %bitcast.24, s32[1]{0:T(128)} %bitcast.25, s32[1]{0:T(128)} %bitcast.26, s32[1]{0:T(128)} %bitcast.27, s32[1]{0:T(128)} %bitcast.28, s32[1]{0:T(128)} %bitcast.29, s32[1]{0:T(128)} %bitcast.30, s32[1]{0:T(128)} %bitcast.31, ...), dimensions={0} | concatenate | bytes 128 | tf_op jit(solution)/shard_map/stack | solution.py:189
  39.2 2.6 collective-permute-start.1
  57.4 4.5 %collective-permute-start.36 = (bf16[384,768]{1,0:T(8,128)(2,1)}, bf16[384,768]{1,0:T(8,128)(2,1)}, u32[]{:S(2)}, u32[]{:S(2)}) collective-permute-start(bf16[384,768]{1,0:T(8,128)(2,1)} %bitcast.67), channel_id=1, source_target_pairs={{0,8},{8,16},{16,24},{1,9},{9,17},{17,25},{2,10},{10,18},{18,26},{... | collective-permute-start | bytes 1769480 | tf_op jit(solution)/shard_map/ppermute | solution.py:83
  64.5 4.6 %collective-permute-done.28 = bf16[96,1536]{1,0:T(8,128)(2,1)S(1)} collective-permute-done((bf16[96,1536]{1,0:T(8,128)(2,1)S(1)}, bf16[96,1536]{1,0:T(8,128)(2,1)S(1)}, u32[]{:S(2)}, u32[]{:S(2)}) %collective-permute-start.28) | collective-permute-done | bytes 294944 | tf_op jit(solution)/shard_map/ppermute | solution.py:26
  76.1 4.9 %collective-permute-done.10 = bf16[512,384]{1,0:T(8,128)(2,1)S(1)} collective-permute-done((bf16[512,384]{1,0:T(8,128)(2,1)S(1)}, bf16[512,384]{1,0:T(8,128)(2,1)S(1)}, u32[]{:S(2)}, u32[]{:S(2)}) %collective-permute-start.10) | collective-permute-done | bytes 393248 | tf_op jit(solution)/shard_map/ppermute | solution.py:26
  82.8 2.8 fusion.152
  87.8 3.7 collective-permute-start.11
  93.1 4.6 %collective-permute-start.30 = (bf16[192,1536]{1,0:T(8,128)(2,1)S(1)}, bf16[192,1536]{1,0:T(8,128)(2,1)S(1)}, u32[]{:S(2)}, u32[]{:S(2)}) collective-permute-start(bf16[192,1536]{1,0:T(8,128)(2,1)S(1)} %copy-done.46), channel_id=1, source_target_pairs={{0,8},{8,16},{16,24},{1,9},{9,17},{17,25},{2,10},{10,18},{18,26},{... | collective-permute-start | bytes 1769480 | tf_op jit(solution)/shard_map/ppermute | solution.py:83
  101.4 8.6 %collective-permute-done.29 = bf16[192,1536]{1,0:T(8,128)(2,1)S(1)} collective-permute-done((bf16[192,1536]{1,0:T(8,128)(2,1)S(1)}, bf16[192,1536]{1,0:T(8,128)(2,1)S(1)}, u32[]{:S(2)}, u32[]{:S(2)}) %collective-permute-start.29) | collective-permute-done | bytes 589856 | tf_op jit(solution)/shard_map/ppermute | solution.py:84
  113.1 8.6 %collective-permute-done.39 = bf16[384,768]{1,0:T(8,128)(2,1)S(1)} collective-permute-done((bf16[384,768]{1,0:T(8,128)(2,1)}, bf16[384,768]{1,0:T(8,128)(2,1)S(1)}, u32[]{:S(2)}, u32[]{:S(2)}) %collective-permute-start.39) | collective-permute-done | bytes 589856 | tf_op jit(solution)/shard_map/ppermute | solution.py:84
  125.1 2.5 collective-permute-done.24
  127.6 3.6 collective-permute-done.25
  134.7 2.6 collective-permute-done.27
  142.6 9.0 %collective-permute-done.40 = bf16[384,768]{1,0:T(8,128)(2,1)S(1)} collective-permute-done((bf16[384,768]{1,0:T(8,128)(2,1)S(1)}, bf16[384,768]{1,0:T(8,128)(2,1)S(1)}, u32[]{:S(2)}, u32[]{:S(2)}) %collective-permute-start.40) | collective-permute-done | bytes 589856 | tf_op jit(solution)/shard_map/ppermute | solution.py:84
  153.9 6.6 %collective-permute-done.34 = bf16[192,1536]{1,0:T(8,128)(2,1)S(1)} collective-permute-done((bf16[192,1536]{1,0:T(8,128)(2,1)S(1)}, bf16[192,1536]{1,0:T(8,128)(2,1)S(1)}, u32[]{:S(2)}, u32[]{:S(2)}) %collective-permute-start.34) | collective-permute-done | bytes 589856 | tf_op jit(solution)/shard_map/ppermute | solution.py:84
  160.7 4.1 multiply_convert_fusion.1
  164.8 4.1 convolution_convert_fusion.5
  170.7 2.5 collective-permute-start.41
  175.0 3.1 collective-permute-start.45
  181.9 3.3 collective-permute-done.45
  187.2 3.0 multiply_reduce_fusion.1
  199.9 2.7 collective-permute-start.54
  206.2 2.5 reshape.606
  224.2 6.9 %fusion.10 = bf16[640,1536]{1,0:T(8,128)(2,1)S(1)} fusion(f32[640,1536]{1,0:T(8,128)} %get-tuple-element.218, bf16[640,768]{1,0:T(8,128)(2,1)} %constant_dynamic-update-slice_fusion.8, bf16[1536,768]{1,0:T(8,128)(2,1)} %add_dynamic-update-slice_fusion), kind=kOutput, calls=%fused_computation.14 | convolution fusion | flops 1529610240 | bytes 9240576 | tf_op jit(solution)/shard_map/dot_general | solution.py:14
  244.2 2.6 collective-permute-start.59
  250.8 3.4 collective-permute-done.59
  261.6 3.8 collective-permute-start.62
  267.2 3.3 copy.192
  270.6 2.3 fusion.32
  291.1 2.9 collective-permute-start.87
  298.0 2.5 collective-permute-start.90
  301.3 2.8 multiply_reduce_fusion
  307.0 2.3 fusion.41
  310.5 11.8 %collective-permute-done.90 = bf16[192,1536]{1,0:T(8,128)(2,1)} collective-permute-done((bf16[192,1536]{1,0:T(8,128)(2,1)S(1)}, bf16[192,1536]{1,0:T(8,128)(2,1)}, u32[]{:S(2)}, u32[]{:S(2)}) %collective-permute-start.90) | collective-permute-done | bytes 589856 | tf_op jit(solution)/shard_map/ppermute | solution.py:97
  322.3 3.3 add_convert_fusion.5
  325.7 4.1 collective-permute-start.67
  329.7 3.2 fusion.22
  338.0 2.3 collective-permute-start.79
  340.6 3.7 collective-permute-done.77
  344.4 4.0 collective-permute-done.79
  356.0 3.6 collective-permute-start.91
  374.7 4.6 %collective-permute-start.99 = (bf16[384,768]{1,0:T(8,128)(2,1)}, bf16[384,768]{1,0:T(8,128)(2,1)}, u32[]{:S(2)}, u32[]{:S(2)}) collective-permute-start(bf16[384,768]{1,0:T(8,128)(2,1)} %add_convert_fusion.1), channel_id=1, source_target_pairs={{0,8},{8,16},{16,24},{1,9},{9,17},{17,25},{2,10},{10,18},{18,26},{... | collective-permute-start | bytes 1769480 | tf_op jit(solution)/shard_map/ppermute | solution.py:97
  384.9 4.4 collective-permute-start.73
  390.6 5.8 %collective-permute-done.73 = bf16[24,704]{1,0:T(8,128)(2,1)S(1)} collective-permute-done((bf16[24,704]{1,0:T(8,128)(2,1)S(1)}, bf16[24,704]{1,0:T(8,128)(2,1)S(1)}, u32[]{:S(2)}, u32[]{:S(2)}) %collective-permute-start.73) | collective-permute-done | bytes 33824 | tf_op jit(solution)/shard_map/ppermute | solution.py:19
  396.4 4.8 %collective-permute-start.92 = (bf16[192,1536]{1,0:T(8,128)(2,1)}, bf16[192,1536]{1,0:T(8,128)(2,1)S(1)}, u32[]{:S(2)}, u32[]{:S(2)}) collective-permute-start(bf16[192,1536]{1,0:T(8,128)(2,1)} %add_convert_fusion.4), channel_id=1, source_target_pairs={{0,8},{8,16},{16,24},{1,9},{9,17},{17,25},{2,10},{10,18},{18,26},{... | collective-permute-start | bytes 1769480 | tf_op jit(solution)/shard_map/ppermute | solution.py:97
  429.0 3.1 fusion.21
  (566 shorter events, 232.7 us)
Async XLA Ops:
  0.7 41.2 %collective-permute-start.15 = (bf16[24,768]{1,0:T(8,128)(2,1)}, bf16[24,768]{1,0:T(8,128)(2,1)S(1)}, u32[]{:S(2)}, u32[]{:S(2)}) collective-permute-start(bf16[24,768]{1,0:T(8,128)(2,1)} %param.15), channel_id=1, source_target_pairs={{16,0},{24,8},{0,16},{8,24},{17,1},{25,9},{1,17},{9,25},{18,2},{26... | collective-permute-start | bytes 110600 | tf_op jit(solution)/shard_map/ppermute | solution.py:19
  4.8 38.7 %collective-permute-start.14 = (bf16[24,768]{1,0:T(8,128)(2,1)}, bf16[24,768]{1,0:T(8,128)(2,1)S(1)}, u32[]{:S(2)}, u32[]{:S(2)}) collective-permute-start(bf16[24,768]{1,0:T(8,128)(2,1)} %param.15), channel_id=1, source_target_pairs={{8,0},{16,8},{24,16},{0,24},{9,1},{17,9},{25,17},{1,25},{10,2},{18... | collective-permute-start | bytes 110600 | tf_op jit(solution)/shard_map/ppermute | solution.py:19
  8.5 28.9 %collective-permute-start.3 = (bf16[24,640]{1,0:T(8,128)(2,1)S(1)}, bf16[24,640]{1,0:T(8,128)(2,1)S(1)}, u32[]{:S(2)}, u32[]{:S(2)}) collective-permute-start(bf16[24,640]{1,0:T(8,128)(2,1)S(1)} %bitcast.419), channel_id=1, source_target_pairs={{8,0},{16,8},{24,16},{0,24},{9,1},{17,9},{25,17},{1,25},{10,2},{18... | collective-permute-start | bytes 92168 | tf_op jit(solution)/shard_map/ppermute | solution.py:19
  8.8 28.8 %collective-permute-start.4 = (bf16[24,640]{1,0:T(8,128)(2,1)S(1)}, bf16[24,640]{1,0:T(8,128)(2,1)S(1)}, u32[]{:S(2)}, u32[]{:S(2)}) collective-permute-start(bf16[24,640]{1,0:T(8,128)(2,1)S(1)} %bitcast.418), channel_id=1, source_target_pairs={{16,0},{24,8},{0,16},{8,24},{17,1},{25,9},{1,17},{9,25},{18,2},{26... | collective-permute-start | bytes 92168 | tf_op jit(solution)/shard_map/ppermute | solution.py:19
  10.7 28.5 %collective-permute-start.5 = (bf16[24,640]{1,0:T(8,128)(2,1)S(1)}, bf16[24,640]{1,0:T(8,128)(2,1)S(1)}, u32[]{:S(2)}, u32[]{:S(2)}) collective-permute-start(bf16[24,640]{1,0:T(8,128)(2,1)S(1)} %bitcast.417), channel_id=1, source_target_pairs={{24,0},{0,8},{8,16},{16,24},{25,1},{1,9},{9,17},{17,25},{26,2},{2,... | collective-permute-start | bytes 92168 | tf_op jit(solution)/shard_map/ppermute | solution.py:19
  37.5 24.6 %collective-permute-start.2 = (bf16[128,768]{1,0:T(8,128)(2,1)S(1)}, bf16[128,768]{1,0:T(8,128)(2,1)S(1)}, u32[]{:S(2)}, u32[]{:S(2)}) collective-permute-start(bf16[128,768]{1,0:T(8,128)(2,1)S(1)} %bitcast.390), channel_id=1, source_target_pairs={{24,0},{0,8},{8,16},{16,24},{25,1},{1,9},{9,17},{17,25},{26,2},{2,... | collective-permute-start | bytes 589832 | tf_op jit(solution)/shard_map/ppermute | solution.py:19
  39.2 24.5 %collective-permute-start.1 = (bf16[128,768]{1,0:T(8,128)(2,1)S(1)}, bf16[128,768]{1,0:T(8,128)(2,1)S(1)}, u32[]{:S(2)}, u32[]{:S(2)}) collective-permute-start(bf16[128,768]{1,0:T(8,128)(2,1)S(1)} %bitcast.391), channel_id=1, source_target_pairs={{16,0},{24,8},{0,16},{8,24},{17,1},{25,9},{1,17},{9,25},{18,2},{26... | collective-permute-start | bytes 589832 | tf_op jit(solution)/shard_map/ppermute | solution.py:19
  54.7 37.0 %collective-permute-start.35 = (bf16[384,768]{1,0:T(8,128)(2,1)}, bf16[384,768]{1,0:T(8,128)(2,1)}, u32[]{:S(2)}, u32[]{:S(2)}) collective-permute-start(bf16[384,768]{1,0:T(8,128)(2,1)} %bitcast.67), channel_id=1, source_target_pairs={{8,0},{16,8},{24,16},{9,1},{17,9},{25,17},{10,2},{18,10},{26,18},{... | collective-permute-start | bytes 1769480 | tf_op jit(solution)/shard_map/ppermute | solution.py:84
  57.4 35.7 %collective-permute-start.36 = (bf16[384,768]{1,0:T(8,128)(2,1)}, bf16[384,768]{1,0:T(8,128)(2,1)}, u32[]{:S(2)}, u32[]{:S(2)}) collective-permute-start(bf16[384,768]{1,0:T(8,128)(2,1)} %bitcast.67), channel_id=1, source_target_pairs={{0,8},{8,16},{16,24},{1,9},{9,17},{17,25},{2,10},{10,18},{18,26},{... | collective-permute-start | bytes 1769480 | tf_op jit(solution)/shard_map/ppermute | solution.py:83
  87.8 12.0 %collective-permute-start.11 = (bf16[128,192]{0,1:T(8,128)(2,1)S(1)}, bf16[128,192]{0,1:T(8,128)(2,1)S(1)}, u32[]{:S(2)}, u32[]{:S(2)}) collective-permute-start(bf16[128,192]{0,1:T(8,128)(2,1)S(1)} %bitcast.414), channel_id=1, source_target_pairs={{8,0},{16,8},{24,16},{0,24},{9,1},{17,9},{25,17},{1,25},{10,2},{18... | collective-permute-start | bytes 147464 | tf_op jit(solution)/shard_map/ppermute | solution.py:19
  91.7 18.3 %collective-permute-start.29 = (bf16[192,1536]{1,0:T(8,128)(2,1)S(1)}, bf16[192,1536]{1,0:T(8,128)(2,1)S(1)}, u32[]{:S(2)}, u32[]{:S(2)}) collective-permute-start(bf16[192,1536]{1,0:T(8,128)(2,1)S(1)} %copy-done.46), channel_id=1, source_target_pairs={{8,0},{16,8},{24,16},{9,1},{17,9},{25,17},{10,2},{18,10},{26,18},{... | collective-permute-start | bytes 1769480 | tf_op jit(solution)/shard_map/ppermute | solution.py:84
  93.1 18.6 %collective-permute-start.30 = (bf16[192,1536]{1,0:T(8,128)(2,1)S(1)}, bf16[192,1536]{1,0:T(8,128)(2,1)S(1)}, u32[]{:S(2)}, u32[]{:S(2)}) collective-permute-start(bf16[192,1536]{1,0:T(8,128)(2,1)S(1)} %copy-done.46), channel_id=1, source_target_pairs={{0,8},{8,16},{16,24},{1,9},{9,17},{17,25},{2,10},{10,18},{18,26},{... | collective-permute-start | bytes 1769480 | tf_op jit(solution)/shard_map/ppermute | solution.py:83
  97.7 23.9 %collective-permute-start.39 = (bf16[384,768]{1,0:T(8,128)(2,1)}, bf16[384,768]{1,0:T(8,128)(2,1)S(1)}, u32[]{:S(2)}, u32[]{:S(2)}) collective-permute-start(bf16[384,768]{1,0:T(8,128)(2,1)} %collective-permute-done.35), channel_id=1, source_target_pairs={{8,0},{16,8},{9,1},{17,9},{10,2},{18,10},{11,3},{19,11},{12,4},{20... | collective-permute-start | bytes 1769480 | tf_op jit(solution)/shard_map/ppermute | solution.py:84
  99.0 23.3 %collective-permute-start.37 = (bf16[384,768]{1,0:T(8,128)(2,1)}, bf16[384,768]{1,0:T(8,128)(2,1)S(1)}, u32[]{:S(2)}, u32[]{:S(2)}) collective-permute-start(bf16[384,768]{1,0:T(8,128)(2,1)} %collective-permute-done.36), channel_id=1, source_target_pairs={{8,16},{16,24},{9,17},{17,25},{10,18},{18,26},{11,19},{19,27},{12,... | collective-permute-start | bytes 1769480 | tf_op jit(solution)/shard_map/ppermute | solution.py:83
  100.9 23.3 %collective-permute-start.22 = (bf16[80,768]{1,0:T(8,128)(2,1)S(1)}, bf16[80,768]{1,0:T(8,128)(2,1)S(1)}, u32[]{:S(2)}, u32[]{:S(2)}) collective-permute-start(bf16[80,768]{1,0:T(8,128)(2,1)S(1)} %get-tuple-element.159), channel_id=1, source_target_pairs={{2,0},{3,1},{0,2},{1,3},{6,4},{7,5},{4,6},{5,7},{10,8},{11,9},{8,1... | collective-permute-start | bytes 368648 | tf_op jit(solution)/shard_map/ppermute | solution.py:26
  111.3 13.7 %collective-permute-start.23 = (bf16[80,768]{1,0:T(8,128)(2,1)S(1)}, bf16[80,768]{1,0:T(8,128)(2,1)S(1)}, u32[]{:S(2)}, u32[]{:S(2)}) collective-permute-start(bf16[80,768]{1,0:T(8,128)(2,1)S(1)} %get-tuple-element.158), channel_id=1, source_target_pairs={{3,0},{2,1},{1,2},{0,3},{7,4},{6,5},{5,6},{4,7},{11,8},{10,9},{9,1... | collective-permute-start | bytes 368648 | tf_op jit(solution)/shard_map/ppermute | solution.py:26
  111.8 25.6 %collective-permute-start.33 = (bf16[192,1536]{1,0:T(8,128)(2,1)S(1)}, bf16[192,1536]{1,0:T(8,128)(2,1)S(1)}, u32[]{:S(2)}, u32[]{:S(2)}) collective-permute-start(bf16[192,1536]{1,0:T(8,128)(2,1)S(1)} %collective-permute-done.29), channel_id=1, source_target_pairs={{8,0},{16,8},{9,1},{17,9},{10,2},{18,10},{11,3},{19,11},{12,4},{20... | collective-permute-start | bytes 1769480 | tf_op jit(solution)/shard_map/ppermute | solution.py:84
  121.7 17.0 %collective-permute-start.31 = (bf16[192,1536]{1,0:T(8,128)(2,1)S(1)}, bf16[192,1536]{1,0:T(8,128)(2,1)S(1)}, u32[]{:S(2)}, u32[]{:S(2)}) collective-permute-start(bf16[192,1536]{1,0:T(8,128)(2,1)S(1)} %collective-permute-done.30), channel_id=1, source_target_pairs={{8,16},{16,24},{9,17},{17,25},{10,18},{18,26},{11,19},{19,27},{12,... | collective-permute-start | bytes 1769480 | tf_op jit(solution)/shard_map/ppermute | solution.py:83
  124.3 15.3 %collective-permute-start.38 = (bf16[384,768]{1,0:T(8,128)(2,1)S(1)}, bf16[384,768]{1,0:T(8,128)(2,1)S(1)}, u32[]{:S(2)}, u32[]{:S(2)}) collective-permute-start(bf16[384,768]{1,0:T(8,128)(2,1)S(1)} %collective-permute-done.37), channel_id=1, source_target_pairs={{16,24},{17,25},{18,26},{19,27},{20,28},{21,29},{22,30},{23,31}} | collective-permute-start | bytes 1769480 | tf_op jit(solution)/shard_map/ppermute | solution.py:83
  133.4 18.1 %collective-permute-start.40 = (bf16[384,768]{1,0:T(8,128)(2,1)S(1)}, bf16[384,768]{1,0:T(8,128)(2,1)S(1)}, u32[]{:S(2)}, u32[]{:S(2)}) collective-permute-start(bf16[384,768]{1,0:T(8,128)(2,1)S(1)} %collective-permute-done.39), channel_id=1, source_target_pairs={{8,0},{9,1},{10,2},{11,3},{12,4},{13,5},{14,6},{15,7}} | collective-permute-start | bytes 1769480 | tf_op jit(solution)/shard_map/ppermute | solution.py:84
  137.3 23.2 %collective-permute-start.34 = (bf16[192,1536]{1,0:T(8,128)(2,1)S(1)}, bf16[192,1536]{1,0:T(8,128)(2,1)S(1)}, u32[]{:S(2)}, u32[]{:S(2)}) collective-permute-start(bf16[192,1536]{1,0:T(8,128)(2,1)S(1)} %collective-permute-done.33), channel_id=1, source_target_pairs={{8,0},{9,1},{10,2},{11,3},{12,4},{13,5},{14,6},{15,7}} | collective-permute-start | bytes 1769480 | tf_op jit(solution)/shard_map/ppermute | solution.py:84
  138.7 15.0 %collective-permute-start.32 = (bf16[192,1536]{1,0:T(8,128)(2,1)S(1)}, bf16[192,1536]{1,0:T(8,128)(2,1)S(1)}, u32[]{:S(2)}, u32[]{:S(2)}) collective-permute-start(bf16[192,1536]{1,0:T(8,128)(2,1)S(1)} %collective-permute-done.31), channel_id=1, source_target_pairs={{16,24},{17,25},{18,26},{19,27},{20,28},{21,29},{22,30},{23,31}} | collective-permute-start | bytes 1769480 | tf_op jit(solution)/shard_map/ppermute | solution.py:83
  199.9 22.7 %collective-permute-start.54 = (bf16[80,768]{1,0:T(8,128)(2,1)}, bf16[80,768]{1,0:T(8,128)(2,1)}, u32[]{:S(2)}, u32[]{:S(2)}) collective-permute-start(bf16[80,768]{1,0:T(8,128)(2,1)} %get-tuple-element.153), channel_id=1, source_target_pairs={{7,0},{6,1},{5,2},{4,3},{3,4},{2,5},{1,6},{0,7},{15,8},{14,9},{13,... | collective-permute-start | bytes 368648 | tf_op jit(solution)/shard_map/ppermute | solution.py:26
  202.6 14.2 %collective-permute-start.50 = (bf16[80,768]{1,0:T(8,128)(2,1)}, bf16[80,768]{1,0:T(8,128)(2,1)}, u32[]{:S(2)}, u32[]{:S(2)}) collective-permute-start(bf16[80,768]{1,0:T(8,128)(2,1)} %get-tuple-element.153), channel_id=1, source_target_pairs={{3,0},{2,1},{1,2},{0,3},{7,4},{6,5},{5,6},{4,7},{11,8},{10,9},{9,1... | collective-permute-start | bytes 368648 | tf_op jit(solution)/shard_map/ppermute | solution.py:26
  202.6 18.4 %collective-permute-start.53 = (bf16[80,768]{1,0:T(8,128)(2,1)}, bf16[80,768]{1,0:T(8,128)(2,1)}, u32[]{:S(2)}, u32[]{:S(2)}) collective-permute-start(bf16[80,768]{1,0:T(8,128)(2,1)} %get-tuple-element.154), channel_id=1, source_target_pairs={{6,0},{7,1},{4,2},{5,3},{2,4},{3,5},{0,6},{1,7},{14,8},{15,9},{12,... | collective-permute-start | bytes 368648 | tf_op jit(solution)/shard_map/ppermute | solution.py:26
  240.5 85.2 %collective-permute-start.100 = (bf16[384,768]{1,0:T(8,128)(2,1)}, bf16[384,768]{1,0:T(8,128)(2,1)}, u32[]{:S(2)}, u32[]{:S(2)}) collective-permute-start(bf16[384,768]{1,0:T(8,128)(2,1)} %convolution_convert_fusion.8), channel_id=1, source_target_pairs={{24,16},{25,17},{26,18},{27,19},{28,20},{29,21},{30,22},{31,23}} | collective-permute-start | bytes 1769480 | tf_op jit(solution)/shard_map/ppermute | solution.py:98
  285.8 15.4 %collective-permute-start.65 = (bf16[512,384]{0,1:T(8,128)(2,1)S(1)}, bf16[512,384]{0,1:T(8,128)(2,1)S(1)}, u32[]{:S(2)}, u32[]{:S(2)}) collective-permute-start(bf16[512,384]{0,1:T(8,128)(2,1)S(1)} %fusion.31), channel_id=1, source_target_pairs={{4,0},{0,4},{5,1},{1,5},{6,2},{2,6},{7,3},{3,7},{12,8},{8,12},{13,... | collective-permute-start | bytes 1179656 | tf_op jit(solution)/shard_map/ppermute | solution.py:26
  294.4 35.3 %collective-permute-start.97 = (bf16[384,768]{1,0:T(8,128)(2,1)}, bf16[384,768]{1,0:T(8,128)(2,1)}, u32[]{:S(2)}, u32[]{:S(2)}) collective-permute-start(bf16[384,768]{1,0:T(8,128)(2,1)} %convolution_convert_fusion.6), channel_id=1, source_target_pairs={{0,8},{1,9},{2,10},{3,11},{4,12},{5,13},{6,14},{7,15}} | collective-permute-start | bytes 1769480 | tf_op jit(solution)/shard_map/ppermute | solution.py:97
  296.5 14.0 %collective-permute-start.93 = (bf16[192,1536]{1,0:T(8,128)(2,1)S(1)}, bf16[192,1536]{1,0:T(8,128)(2,1)}, u32[]{:S(2)}, u32[]{:S(2)}) collective-permute-start(bf16[192,1536]{1,0:T(8,128)(2,1)S(1)} %copy-done.25), channel_id=1, source_target_pairs={{24,16},{25,17},{26,18},{27,19},{28,20},{29,21},{30,22},{31,23}} | collective-permute-start | bytes 1769480 | tf_op jit(solution)/shard_map/ppermute | solution.py:98
  298.0 24.3 %collective-permute-start.90 = (bf16[192,1536]{1,0:T(8,128)(2,1)S(1)}, bf16[192,1536]{1,0:T(8,128)(2,1)}, u32[]{:S(2)}, u32[]{:S(2)}) collective-permute-start(bf16[192,1536]{1,0:T(8,128)(2,1)S(1)} %copy-done.24), channel_id=1, source_target_pairs={{0,8},{1,9},{2,10},{3,11},{4,12},{5,13},{6,14},{7,15}} | collective-permute-start | bytes 1769480 | tf_op jit(solution)/shard_map/ppermute | solution.py:97
  301.1 34.5 %collective-permute-start.76 = (bf16[4,4,24,896]{3,2,0,1:T(8,128)(2,1)}, bf16[4,4,24,896]{3,2,0,1:T(8,128)(2,1)}, u32[]{:S(2)}, u32[]{:S(2)}) collective-permute-start(bf16[4,4,24,896]{3,2,0,1:T(8,128)(2,1)} %fusion.32), channel_id=1, source_target_pairs={{1,0},{0,1},{3,2},{2,3},{5,4},{4,5},{7,6},{6,7},{9,8},{8,9},{11,10... | collective-permute-start | bytes 2064392 | tf_op jit(solution)/shard_map/ppermute | solution.py:26
  310.5 22.4 %collective-permute-start.66 = (bf16[128,768]{1,0:T(8,128)(2,1)S(1)}, bf16[128,768]{1,0:T(8,128)(2,1)S(1)}, u32[]{:S(2)}, u32[]{:S(2)}) collective-permute-start(bf16[128,768]{1,0:T(8,128)(2,1)S(1)} %get-tuple-element.133), channel_id=1, source_target_pairs={{24,0},{0,8},{8,16},{16,24},{25,1},{1,9},{9,17},{17,25},{26,2},{2,... | collective-permute-start | bytes 589832 | tf_op jit(solution)/shard_map/ppermute | solution.py:19
  322.3 12.7 %collective-permute-start.68 = (bf16[128,768]{1,0:T(8,128)(2,1)S(1)}, bf16[128,768]{1,0:T(8,128)(2,1)S(1)}, u32[]{:S(2)}, u32[]{:S(2)}) collective-permute-start(bf16[128,768]{1,0:T(8,128)(2,1)S(1)} %get-tuple-element.134), channel_id=1, source_target_pairs={{8,0},{16,8},{24,16},{0,24},{9,1},{17,9},{25,17},{1,25},{10,2},{18... | collective-permute-start | bytes 589832 | tf_op jit(solution)/shard_map/ppermute | solution.py:19
  329.7 35.4 %collective-permute-start.69 = (bf16[4,4,24,704]{3,2,0,1:T(8,128)(2,1)}, bf16[4,4,24,704]{3,2,0,1:T(8,128)(2,1)}, u32[]{:S(2)}, u32[]{:S(2)}) collective-permute-start(bf16[4,4,24,704]{3,2,0,1:T(8,128)(2,1)} %fusion.41), channel_id=1, source_target_pairs={{1,0},{0,1},{3,2},{2,3},{5,4},{4,5},{7,6},{6,7},{9,8},{8,9},{11,10... | collective-permute-start | bytes 1622024 | tf_op jit(solution)/shard_map/ppermute | solution.py:26
  332.9 34.3 %collective-permute-start.98 = (bf16[384,768]{1,0:T(8,128)(2,1)}, bf16[384,768]{1,0:T(8,128)(2,1)}, u32[]{:S(2)}, u32[]{:S(2)}) collective-permute-start(bf16[384,768]{1,0:T(8,128)(2,1)} %get-tuple-element.141), channel_id=1, source_target_pairs={{0,8},{8,16},{1,9},{9,17},{2,10},{10,18},{3,11},{11,19},{4,12},{12... | collective-permute-start | bytes 1769480 | tf_op jit(solution)/shard_map/ppermute | solution.py:97
  354.1 16.8 %collective-permute-start.101 = (bf16[384,768]{1,0:T(8,128)(2,1)}, bf16[384,768]{1,0:T(8,128)(2,1)}, u32[]{:S(2)}, u32[]{:S(2)}) collective-permute-start(bf16[384,768]{1,0:T(8,128)(2,1)} %get-tuple-element.142), channel_id=1, source_target_pairs={{16,8},{24,16},{17,9},{25,17},{18,10},{26,18},{19,11},{27,19},{20,... | collective-permute-start | bytes 1769480 | tf_op jit(solution)/shard_map/ppermute | solution.py:98
  356.0 18.8 %collective-permute-start.91 = (bf16[192,1536]{1,0:T(8,128)(2,1)}, bf16[192,1536]{1,0:T(8,128)(2,1)}, u32[]{:S(2)}, u32[]{:S(2)}) collective-permute-start(bf16[192,1536]{1,0:T(8,128)(2,1)} %get-tuple-element.110), channel_id=1, source_target_pairs={{0,8},{8,16},{1,9},{9,17},{2,10},{10,18},{3,11},{11,19},{4,12},{12... | collective-permute-start | bytes 1769480 | tf_op jit(solution)/shard_map/ppermute | solution.py:97
  359.5 21.8 %collective-permute-start.94 = (bf16[192,1536]{1,0:T(8,128)(2,1)}, bf16[192,1536]{1,0:T(8,128)(2,1)}, u32[]{:S(2)}, u32[]{:S(2)}) collective-permute-start(bf16[192,1536]{1,0:T(8,128)(2,1)} %get-tuple-element.111), channel_id=1, source_target_pairs={{16,8},{24,16},{17,9},{25,17},{18,10},{26,18},{19,11},{27,19},{20,... | collective-permute-start | bytes 1769480 | tf_op jit(solution)/shard_map/ppermute | solution.py:98
  366.8 18.0 %collective-permute-start.70 = (bf16[4,24,704]{2,1,0:T(8,128)(2,1)S(1)}, bf16[4,24,704]{2,1,0:T(8,128)(2,1)S(1)}, u32[]{:S(2)}, u32[]{:S(2)}) collective-permute-start(bf16[4,24,704]{2,1,0:T(8,128)(2,1)S(1)} %get-tuple-element.143), channel_id=1, source_target_pairs={{2,0},{0,2},{6,4},{4,6},{3,1},{1,3},{7,5},{5,7},{10,8},{8,10},{14,... | collective-permute-start | bytes 405512 | tf_op jit(solution)/shard_map/ppermute | solution.py:26
  367.2 17.6 %collective-permute-start.72 = (bf16[4,24,704]{2,1,0:T(8,128)(2,1)S(1)}, bf16[4,24,704]{2,1,0:T(8,128)(2,1)S(1)}, u32[]{:S(2)}, u32[]{:S(2)}) collective-permute-start(bf16[4,24,704]{2,1,0:T(8,128)(2,1)S(1)} %get-tuple-element.144), channel_id=1, source_target_pairs={{6,0},{4,2},{2,4},{0,6},{7,1},{5,3},{3,5},{1,7},{14,8},{12,10},{10... | collective-permute-start | bytes 405512 | tf_op jit(solution)/shard_map/ppermute | solution.py:26
  370.8 13.9 %collective-permute-start.71 = (bf16[4,24,704]{2,1,0:T(8,128)(2,1)S(1)}, bf16[4,24,704]{2,1,0:T(8,128)(2,1)S(1)}, u32[]{:S(2)}, u32[]{:S(2)}) collective-permute-start(bf16[4,24,704]{2,1,0:T(8,128)(2,1)S(1)} %get-tuple-element.145), channel_id=1, source_target_pairs={{4,0},{6,2},{0,4},{2,6},{5,1},{7,3},{1,5},{3,7},{12,8},{14,10},{8,... | collective-permute-start | bytes 405512 | tf_op jit(solution)/shard_map/ppermute | solution.py:26
  374.7 54.3 %collective-permute-start.99 = (bf16[384,768]{1,0:T(8,128)(2,1)}, bf16[384,768]{1,0:T(8,128)(2,1)}, u32[]{:S(2)}, u32[]{:S(2)}) collective-permute-start(bf16[384,768]{1,0:T(8,128)(2,1)} %add_convert_fusion.1), channel_id=1, source_target_pairs={{0,8},{8,16},{16,24},{1,9},{9,17},{17,25},{2,10},{10,18},{18,26},{... | collective-permute-start | bytes 1769480 | tf_op jit(solution)/shard_map/ppermute | solution.py:97
  381.4 47.6 %collective-permute-start.102 = (bf16[384,768]{1,0:T(8,128)(2,1)}, bf16[384,768]{1,0:T(8,128)(2,1)}, u32[]{:S(2)}, u32[]{:S(2)}) collective-permute-start(bf16[384,768]{1,0:T(8,128)(2,1)} %add_convert_fusion), channel_id=1, source_target_pairs={{8,0},{16,8},{24,16},{9,1},{17,9},{25,17},{10,2},{18,10},{26,18},{... | collective-permute-start | bytes 1769480 | tf_op jit(solution)/shard_map/ppermute | solution.py:98
  384.9 11.6 %collective-permute-start.73 = (bf16[24,704]{1,0:T(8,128)(2,1)S(1)}, bf16[24,704]{1,0:T(8,128)(2,1)S(1)}, u32[]{:S(2)}, u32[]{:S(2)}) collective-permute-start(bf16[24,704]{1,0:T(8,128)(2,1)S(1)} %get-tuple-element.190), channel_id=1, source_target_pairs={{8,0},{16,8},{24,16},{0,24},{9,1},{17,9},{25,17},{1,25},{10,2},{18... | collective-permute-start | bytes 101384 | tf_op jit(solution)/shard_map/ppermute | solution.py:19
  389.2 12.1 %collective-permute-start.75 = (bf16[24,704]{1,0:T(8,128)(2,1)S(1)}, bf16[24,704]{1,0:T(8,128)(2,1)S(1)}, u32[]{:S(2)}, u32[]{:S(2)}) collective-permute-start(bf16[24,704]{1,0:T(8,128)(2,1)S(1)} %get-tuple-element.191), channel_id=1, source_target_pairs={{24,0},{0,8},{8,16},{16,24},{25,1},{1,9},{9,17},{17,25},{26,2},{2,... | collective-permute-start | bytes 101384 | tf_op jit(solution)/shard_map/ppermute | solution.py:19
  389.2 13.9 %collective-permute-start.74 = (bf16[24,704]{1,0:T(8,128)(2,1)S(1)}, bf16[24,704]{1,0:T(8,128)(2,1)S(1)}, u32[]{:S(2)}, u32[]{:S(2)}) collective-permute-start(bf16[24,704]{1,0:T(8,128)(2,1)S(1)} %get-tuple-element.192), channel_id=1, source_target_pairs={{16,0},{24,8},{0,16},{8,24},{17,1},{25,9},{1,17},{9,25},{18,2},{26... | collective-permute-start | bytes 101384 | tf_op jit(solution)/shard_map/ppermute | solution.py:19
  396.4 28.7 %collective-permute-start.92 = (bf16[192,1536]{1,0:T(8,128)(2,1)}, bf16[192,1536]{1,0:T(8,128)(2,1)S(1)}, u32[]{:S(2)}, u32[]{:S(2)}) collective-permute-start(bf16[192,1536]{1,0:T(8,128)(2,1)} %add_convert_fusion.4), channel_id=1, source_target_pairs={{0,8},{8,16},{16,24},{1,9},{9,17},{17,25},{2,10},{10,18},{18,26},{... | collective-permute-start | bytes 1769480 | tf_op jit(solution)/shard_map/ppermute | solution.py:97
  401.3 23.8 %collective-permute-start.95 = (bf16[192,1536]{1,0:T(8,128)(2,1)}, bf16[192,1536]{1,0:T(8,128)(2,1)}, u32[]{:S(2)}, u32[]{:S(2)}) collective-permute-start(bf16[192,1536]{1,0:T(8,128)(2,1)} %add_convert_fusion.2), channel_id=1, source_target_pairs={{8,0},{16,8},{24,16},{9,1},{17,9},{25,17},{10,2},{18,10},{26,18},{... | collective-permute-start | bytes 1769480 | tf_op jit(solution)/shard_map/ppermute | solution.py:98
  (140 other events, 1260.3 us)

commit v2 on v1

v2 whole, which is shorter than its diff:
```python
import jax
import jax.numpy as jnp
from jax import lax
from jax.experimental import pallas as pl
from jax.experimental.pallas import tpu as pltpu
from jax.sharding import Mesh, PartitionSpec as P

PRECISION_FULL = lax.Precision.HIGHEST
MASKED = -1e30
LOW = jnp.bfloat16
WIDE = jnp.float32
EPS = 1e-06
LAYER = ("yy", "xx", "cc")


def dot(left, right, contract):
    return lax.dot_general(left, right, (contract, ((), ())), preferred_element_type=WIDE)


def shift(x, axis, d):
    n = lax.axis_size(axis)
    return lax.ppermute(x, axis, [((j + d) % n, j) for j in range(n)])


def swap(x, axes, k):
    n = 1
    for axis in axes:
        n *= lax.axis_size(axis)
    return lax.ppermute(x, axes, [(j ^ k, j) for j in range(n)])


def from_xor(blocks, me):
    step = 1
    while step < len(blocks):
        flip = (me & step) != 0
        blocks = [jnp.where(flip, blocks[j ^ step], blocks[j]) for j in range(len(blocks))]
        step *= 2
    return blocks


def from_cyclic(blocks, me):
    n, step = len(blocks), 1
    while step < n:
        move = (me & step) != 0
        blocks = [jnp.where(move, blocks[(j - step) % n], blocks[j]) for j in range(n)]
        step *= 2
    return blocks


def after(x, *others):
    for other in others:
        first = lax.slice(other, (0,) * other.ndim, (1,) * other.ndim).reshape(())
        x = x + (first * 0).astype(x.dtype)
    return x


def expert_kernel(both, w_first, w_second, out, grad_first, grad_second, total, rows_t):
    step, steps = pl.program_id(0), pl.num_programs(0)
    width = w_first.shape[0]
    rows, grads = both[:, :width], both[:, width:]

    @pl.when(step == 0)
    def _():
        rows_t[...] = rows.T
        total[...] = jnp.zeros_like(total)

    hidden = dot(rows, w_first[...], ((1,), (0,)))
    square = hidden * hidden
    curve = jnp.tanh(0.7978845608028654 * (hidden + 0.044715 * square * hidden))
    active = (0.5 * hidden * (1.0 + curve)).astype(LOW)
    slope = 0.5 * (1.0 + curve) + 0.5 * hidden * (1.0 - curve * curve) * (
        0.7978845608028654 * (1.0 + 0.134145 * square)
    )
    total[:, :width] += dot(active, w_second[...], ((1,), (0,)))
    grad_second[...] = dot(active, grads, ((0,), (0,))).astype(LOW)
    grad_active = dot(grads, w_second[...], ((1,), (1,)))
    grad_hidden = (slope * grad_active).astype(LOW)
    total[:, width:] += dot(grad_hidden, w_first[...], ((1,), (1,)))
    grad_first[...] = dot(rows_t[...], grad_hidden, ((1,), (0,))).astype(LOW)

    @pl.when(step == steps - 1)
    def _():
        out[...] = total[...].astype(LOW)


def expert(both, w_first, w_second, block):
    count, width, units = both.shape[0], w_first.shape[0], w_first.shape[1]
    whole = pl.BlockSpec(memory_space=pltpu.VMEM)
    flops = 12 * count * width * units
    return pl.pallas_call(
        expert_kernel,
        grid=(units // block,),
        out_shape=(
            jax.ShapeDtypeStruct(both.shape, LOW),
            jax.ShapeDtypeStruct(w_first.shape, LOW),
            jax.ShapeDtypeStruct(w_second.shape, LOW),
        ),
        in_specs=[
            whole,
            pl.BlockSpec((width, block), lambda i: (0, i)),
            pl.BlockSpec((block, width), lambda i: (i, 0)),
        ],
        out_specs=(
            whole,
            pl.BlockSpec((width, block), lambda i: (0, i)),
            pl.BlockSpec((block, width), lambda i: (i, 0)),
        ),
        scratch_shapes=[pltpu.VMEM(both.shape, WIDE), pltpu.VMEM((width, count), LOW)],
        compiler_params=pltpu.CompilerParams(vmem_limit_bytes=56 * 1024 * 1024),
        cost_estimate=pl.CostEstimate(
            flops=flops, bytes_accessed=4 * both.size + 8 * w_first.size, transcendentals=count * units
        ),
    )(both, w_first, w_second)


def pick(stack, index):
    return lax.dynamic_index_in_dim(stack, index, 0, keepdims=False)


def layer_gather(block):
    yx_count = lax.axis_size("yy") * lax.axis_size("xx")
    me_yx = lax.axis_index("yy") * lax.axis_size("xx") + lax.axis_index("xx")
    blocks = [block] + [swap(block, ("yy", "xx"), k) for k in range(1, yx_count)]
    joined = jnp.stack(from_xor(blocks, me_yx))
    both = from_xor([joined, swap(joined, ("cc",), 1)], lax.axis_index("cc"))
    full = jnp.stack(both)
    cores, layers, outer, rows, width = full.shape
    return full.transpose(2, 1, 0, 3, 4).reshape(outer * layers * cores * rows, width)


def every_block(x, axes):
    return lax.all_to_all(x, axes, split_axis=0, concat_axis=0, tiled=True)


def low_terms(x):
    return jnp.concatenate(three_terms(x), axis=0)


def three_terms(x):
    high = lax.reduce_precision(x, 8, 7)
    rest = x - high
    middle = lax.reduce_precision(rest, 8, 7)
    return high.astype(LOW), middle.astype(LOW), (rest - middle).astype(LOW)


def body(
    activations,
    gain_one,
    query_key_value_weight,
    attention_output_weight,
    pos_table,
    gain_two,
    w_router,
    w_in,
    w_out,
    routes,
    pair_of_device,
    cotangent,
):
    Z, Y = lax.axis_size("hz"), lax.axis_size("yy")
    E, N = lax.axis_size("xx") * lax.axis_size("cc"), Z * Y
    z, y = lax.axis_index("hz"), lax.axis_index("yy")
    _, own_rows, D = activations.shape
    half = own_rows // 2
    buckets, heads = pos_table.shape
    hd = D // heads
    hg = heads // Z
    gw = hg * hd
    top = routes.shape[2]
    shard = gain_one.shape[0]
    FF = w_in.shape[2]
    capacity = max(2, 5 * own_rows * top // (4 * E))

    acts = activations[0]
    act_blocks = [acts] + [shift(acts, "hz", d) for d in range(1, Z)]
    small = jnp.concatenate([gain_one[:, None], gain_two[:, None], w_router], axis=1)
    small_width = -(-(gw + small.shape[1]) // 128) * 128 - gw
    small = jnp.pad(small, ((0, 0), (0, small_width - small.shape[1])))

    def qkv_piece(group):
        columns = [
            lax.dynamic_slice(query_key_value_weight, (0, part * D + group * gw), (shard, gw))
            for part in (1, 2, 0)
        ]
        return jnp.concatenate(columns + [small], axis=1)

    pieces = [qkv_piece(z)] + [shift(qkv_piece((z - d) % Z), "hz", d) for d in range(1, Z)]
    w_all = layer_gather(jnp.stack(from_cyclic(pieces, z)))

    w_second = lax.all_gather(w_out[0], "hz", axis=0, tiled=True)
    part_ff = FF // N

    def in_piece(part):
        columns = [
            lax.dynamic_slice(w_in[0], (0, (g * Y + part) * part_ff), (D // N, part_ff))
            for g in range(Z)
        ]
        return jnp.concatenate(columns, axis=1)

    in_rows = [in_piece(y)] + [
        swap(after(in_piece(y ^ k), *pieces[1:]), ("yy",), k) for k in range(1, Y)
    ]
    in_rows = jnp.concatenate(from_xor(in_rows, y), axis=0)
    w_first = lax.all_gather(in_rows, "hz", axis=0, tiled=True)

    own_attn_w = after(attention_output_weight, w_all)
    attn_w_pieces = [own_attn_w] + [shift(own_attn_w, "hz", d) for d in range(1, Z)]
    w_attn_out = layer_gather(jnp.stack(from_cyclic(attn_w_pieces, z)))

    gain_first = w_all[:, 3 * gw].astype(WIDE)
    gain_second = w_all[:, 3 * gw + 1].astype(WIDE)
    router = w_all[:, 3 * gw + 2 : 3 * gw + 2 + E]

    n_q, n_k = 2 * Z, 2 * Z * Y

    def tile_of(count, width, axis):
        shape = (count, 1) if axis == 0 else (1, count)
        entry = lax.broadcasted_iota(jnp.int32, shape, axis) // width
        owner = ((z + (entry // 2) % Z) % Z) * Y + (y ^ (entry // (2 * Z)))
        hot_shape = (count, N) if axis == 0 else (N, count)
        lanes = lax.broadcasted_iota(jnp.int32, hot_shape, 1 - axis)
        pairs = pair_of_device[None, :] if axis == 0 else pair_of_device[:, None]
        first = jnp.sum(jnp.where(lanes == owner, pairs, 0), axis=1 - axis, keepdims=True)
        return jnp.where(entry % 2 == 0, first, 2 * N - 1 - first)

    def position_of(count, axis):
        shape = (count, 1) if axis == 0 else (1, count)
        within = lax.broadcasted_iota(jnp.int32, shape, axis) % half
        return tile_of(count, half, axis) * half + within

    query_pos = position_of(n_q * half, 0)
    key_pos = position_of(n_k * half, 1)
    bucket = jnp.clip(tile_of(n_q, 1, 0) - tile_of(n_k, 1, 1), 0, buckets - 1)
    levels = lax.broadcasted_iota(jnp.int32, (n_q, n_k, buckets), 2)
    bucket_hot = bucket[:, :, None] == levels
    own_table = lax.dynamic_slice(pos_table, (0, z * hg), (buckets, hg)).T
    tile_bias = jnp.sum(jnp.where(bucket_hot[None], own_table[:, None, None, :], 0.0), axis=-1)
    bias_terms = jnp.concatenate(three_terms(tile_bias), axis=-1)
    bias_rows = jnp.broadcast_to(
        bias_terms[:, :, None, :], (hg, n_q, half, 3 * n_k)
    ).reshape(hg, n_q * half, 3 * n_k)
    key_hot = (
        lax.broadcasted_iota(jnp.int32, (n_k * half, n_k), 0) // half
        == lax.broadcasted_iota(jnp.int32, (n_k * half, n_k), 1)
    ).astype(LOW)

    x_rows = jnp.concatenate(act_blocks, axis=0).astype(WIDE)
    scale_one = lax.rsqrt(jnp.mean(x_rows * x_rows, axis=-1, keepdims=True) + EPS)
    hat_one = x_rows * scale_one
    normed_one = (hat_one * gain_first).astype(LOW)
    w_kv, w_q = w_all[:, : 2 * gw], w_all[:, 2 * gw : 3 * gw]
    kv = dot(normed_one, w_kv, ((1,), (0,))).astype(LOW)
    kv_all = jnp.concatenate([kv] + [swap(kv, ("yy",), k) for k in range(1, Y)], axis=0)
    q = dot(normed_one, w_q, ((1,), (0,))).astype(LOW)

    def by_head(rows):
        return rows.reshape(rows.shape[0], hg, hd).transpose(1, 0, 2)

    q_heads = by_head(q) * jnp.asarray(hd**-0.5, LOW)
    k_heads, v_heads = by_head(kv_all[:, :gw]), by_head(kv_all[:, gw:])
    q_wide = jnp.concatenate([q_heads, bias_rows], axis=-1)
    k_hot = jnp.broadcast_to(key_hot[None], (hg,) + key_hot.shape)
    k_wide = jnp.concatenate([k_heads, k_hot, k_hot, k_hot], axis=-1)
    scores = jnp.einsum("hqe,hke->hqk", q_wide, k_wide, preferred_element_type=WIDE)
    visible = query_pos >= key_pos
    scores = jnp.where(visible[None], scores, MASKED)
    weights = jnp.exp(scores - jnp.max(scores, axis=-1, keepdims=True))
    probs = weights / jnp.sum(weights, axis=-1, keepdims=True)
    probs_low = probs.astype(LOW)
    mixed_heads = jnp.einsum("hqk,hke->qhe", probs_low, v_heads, preferred_element_type=WIDE)
    mixed = mixed_heads.reshape(Z, own_rows, gw).astype(LOW)
    mixed_back = [mixed[0]] + [shift(mixed[d], "hz", -d) for d in range(1, Z)]
    mixed_back = from_cyclic([mixed_back[-d % Z] for d in range(Z)], z)
    mixed_full = jnp.concatenate(mixed_back, axis=-1)

    own_x = acts.astype(WIDE)
    resid = own_x + dot(mixed_full, w_attn_out, ((1,), (0,)))
    scale_two = lax.rsqrt(jnp.mean(resid * resid, axis=-1, keepdims=True) + EPS)
    hat_two = resid * scale_two
    normed_two = (hat_two * gain_second).astype(LOW)

    choices = [routes[0][:, t : t + 1] for t in range(top)]
    expert_iota = lax.broadcasted_iota(jnp.int32, (1, E), 1)
    chosen_masks = [(choice == expert_iota).astype(WIDE) for choice in choices]
    flat = jnp.concatenate(choices, axis=0)
    hits = (flat == expert_iota).astype(LOW)
    pairs = (own_rows * top, own_rows * top)
    earlier = lax.broadcasted_iota(jnp.int32, pairs, 0) > lax.broadcasted_iota(jnp.int32, pairs, 1)
    before = dot(earlier.astype(LOW), hits, ((1,), (0,)))
    rank = jnp.sum(before * hits.astype(WIDE), axis=-1, keepdims=True).astype(jnp.int32)
    target = flat * capacity + rank
    slots = E * capacity
    slot_iota = lax.broadcasted_iota(jnp.int32, (1, Y * slots), 1) % slots
    route_map = (target == slot_iota).astype(LOW)
    maps = [route_map[t * own_rows : (t + 1) * own_rows] for t in range(top)]
    per_token = sum(maps[1:], maps[0])

    def exchange(rows):
        blocks = rows.reshape(Y * E, capacity, rows.shape[1])
        return every_block(blocks, LAYER).reshape(rows.shape)

    rows = dot(per_token, normed_two, ((0,), (0,)))
    router_logits = dot(normed_two, router, ((1,), (0,)))
    chosen = [jnp.sum(mask * router_logits, axis=-1, keepdims=True) for mask in chosen_masks]
    highest = chosen[0]
    for value in chosen[1:]:
        highest = jnp.maximum(highest, value)
    raised = [jnp.exp(value - highest) for value in chosen]
    gates = [value / sum(raised[1:], raised[0]) for value in raised]
    cot = cotangent[0]
    grad_picked = jnp.concatenate([(gate * cot).astype(LOW) for gate in gates], axis=0)
    grad_rows = dot(route_map, grad_picked, ((0,), (0,)))
    both = exchange(jnp.concatenate([rows, grad_rows], axis=1).astype(LOW))

    block = part_ff if part_ff % 128 == 0 else FF // Y
    results, grad_first, grad_second = expert(both, w_first, w_second, block)
    back = exchange(results)
    returned, coming = back[:, :D], back[:, D:]
    first_low = lax.psum_scatter(grad_first, "hz", scatter_dimension=0, tiled=True)
    shard_second = lax.psum_scatter(grad_second, "hz", scatter_dimension=0, tiled=True)

    picked = [dot(one, returned, ((1,), (0,))) for one in maps]
    output = resid
    for gate, rows_of in zip(gates, picked):
        output = output + gate * rows_of
    grad_gates = [jnp.sum(rows_of * cot, axis=-1, keepdims=True) for rows_of in picked]
    inner = sum(gate * grad for gate, grad in zip(gates, grad_gates))
    logit_gradient = sum(
        gate * (grad - inner) * mask
        for gate, grad, mask in zip(gates, grad_gates, chosen_masks)
    )
    grad_normed_two = dot(per_token, coming, ((1,), (0,))) + jnp.einsum(
        "te,de->td", logit_gradient, router.astype(WIDE), precision=PRECISION_FULL
    )
    grad_router = jnp.einsum(
        "td,te->de", normed_two.astype(WIDE), logit_gradient, precision=PRECISION_FULL
    )
    grad_gain_two = jnp.sum(grad_normed_two * hat_two, axis=0)
    grad_hat = grad_normed_two * gain_second
    grad_resid = cot + scale_two * (
        grad_hat - hat_two * jnp.mean(grad_hat * hat_two, axis=-1, keepdims=True)
    )
    grad_attention = grad_resid.astype(LOW)
    grad_attn_out = dot(mixed_full, grad_attention, ((0,), (0,)))
    grad_mixed = lax.dot_general(
        w_attn_out.reshape(Z, gw, D),
        grad_attention,
        (((2,), (1,)), ((), ())),
        preferred_element_type=WIDE,
    ).transpose(0, 2, 1).astype(LOW)
    grad_mixed_rows = jnp.concatenate(
        [pick(grad_mixed, z)]
        + [shift(pick(grad_mixed, (z - d) % Z), "hz", d) for d in range(1, Z)],
        axis=0,
    )

    grad_heads = by_head(grad_mixed_rows)
    row_dot = jnp.sum(
        by_head(mixed.reshape(Z * own_rows, gw)).astype(WIDE) * grad_heads.astype(WIDE),
        axis=-1,
        keepdims=True,
    )
    grad_probs = jnp.einsum("hqe,hke->hqk", grad_heads, v_heads, preferred_element_type=WIDE)
    grad_scores = (probs_low.astype(WIDE) * (grad_probs - row_dot)).astype(LOW)
    grad_q_wide = jnp.einsum(
        "hqk,hke->hqe",
        grad_scores,
        jnp.concatenate([k_heads, k_hot], axis=-1),
        preferred_element_type=WIDE,
    )
    grad_q = grad_q_wide[..., :hd] * hd**-0.5
    tile_sums = grad_q_wide[..., hd:].reshape(hg, n_q, half, n_k).sum(axis=2)
    table_part = jnp.sum(
        jnp.where(bucket_hot[None], tile_sums[..., None], 0.0), axis=(1, 2)
    )
    grad_k = jnp.einsum("hqk,hqe->khe", grad_scores, q_heads, preferred_element_type=WIDE)
    grad_v = jnp.einsum("hqk,hqe->khe", probs_low, grad_heads, preferred_element_type=WIDE)
    grad_kv = jnp.concatenate(
        [grad_k.reshape(-1, gw), grad_v.reshape(-1, gw)], axis=1
    ).reshape(Y, Z * own_rows, 2 * gw)
    grad_kv_own = grad_kv[0]
    for k in range(1, Y):
        grad_kv_own = grad_kv_own + swap(grad_kv[k].astype(LOW), ("yy",), k).astype(WIDE)
    grad_q_rows = grad_q.transpose(1, 0, 2).reshape(-1, gw)
    grad_qkv = jnp.concatenate([grad_kv_own, grad_q_rows], axis=1).astype(LOW)

    grad_normed_part = dot(grad_qkv, w_all[:, : 3 * gw], ((1,), (1,)))
    grad_gain_one = jnp.sum(grad_normed_part * hat_one, axis=0)
    grad_low = grad_normed_part.astype(LOW).reshape(Z, own_rows, D)
    grad_normed_one = grad_normed_part[:own_rows]
    for d in range(1, Z):
        grad_normed_one = grad_normed_one + shift(grad_low[d], "hz", -d).astype(WIDE)
    own_hat = hat_one[:own_rows]
    grad_hat_one = grad_normed_one * gain_first
    grad_inputs = grad_resid + scale_one[:own_rows] * (
        grad_hat_one - own_hat * jnp.mean(grad_hat_one * own_hat, axis=-1, keepdims=True)
    )

    def pad_columns(columns):
        return jnp.pad(columns, ((0, 0), (0, 128 - columns.shape[1])))

    attn_part = jnp.concatenate(
        [grad_attn_out, pad_columns(jnp.concatenate([grad_gain_two[:, None], grad_router], 1))],
        axis=1,
    )
    attn_part = attn_part.astype(LOW)
    attn_width = attn_part.shape[1]
    line_rows = Z * shard
    table_size = 3 * hg * buckets

    def table_columns(table, rows):
        width = -(-table_size // rows)
        terms = jnp.pad(low_terms(table).reshape(-1), (0, rows * width - table_size))
        return terms.reshape(rows, width)

    def table_of(columns):
        terms = columns.reshape(columns.shape[0], -1)[:, :table_size]
        return terms.reshape(-1, 3, hg, buckets).sum(axis=1)

    grad_w_qkv = dot(normed_one, grad_qkv, ((0,), (0,))).astype(LOW)
    table_block = table_columns(table_part, line_rows)
    table_width = table_block.shape[1]
    extra = jnp.concatenate(
        [
            grad_gain_one[:, None].astype(LOW).reshape(Z, -1, shard, 1),
            jnp.broadcast_to(
                table_block.reshape(Z, 1, shard, table_width),
                (Z, Y * E, shard, table_width),
            ),
        ],
        axis=3,
    ).reshape(D, 1 + table_width)
    extra_width = -(-(3 * gw + 1 + table_width) // 128) * 128 - 3 * gw
    extra = jnp.pad(extra, ((0, 0), (0, extra_width - 1 - table_width)))
    outer_blocks = jnp.concatenate([grad_w_qkv, extra, attn_part], axis=1)
    full_width = outer_blocks.shape[1]
    outer_blocks = outer_blocks.reshape(Z, Y * E, shard, full_width).transpose(1, 0, 2, 3)
    got = every_block(outer_blocks.reshape(Y * E, line_rows, full_width), LAYER)
    got = got.astype(WIDE)
    layer_sum = got.sum(axis=0)
    qkv_sum, attn_sum = layer_sum[:, : 3 * gw + 1], layer_sum[:, full_width - attn_width :]
    layer_table = table_of(got[:, :, 3 * gw + 1 : 3 * gw + 1 + table_width]).sum(axis=0)
    table_block = table_columns(layer_table, shard)
    line_width = table_block.shape[1]
    line_blocks = jnp.concatenate(
        [
            attn_sum.astype(LOW).reshape(Z, shard, attn_width),
            qkv_sum.astype(LOW).reshape(Z, shard, 3 * gw + 1),
            jnp.broadcast_to(table_block[None], (Z, shard, line_width)),
        ],
        axis=2,
    )
    line_pad = -(-line_blocks.shape[2] // 128) * 128 - line_blocks.shape[2]
    line_blocks = jnp.pad(line_blocks, ((0, 0), (0, 0), (0, line_pad)))
    line = every_block(line_blocks, ("hz",)).astype(WIDE)
    attn_total, line = line[:, :, :attn_width].sum(axis=0), line[:, :, attn_width:]
    shard_attn_out = attn_total[:, :D]
    shard_gain_two = attn_total[:, D]
    shard_router = attn_total[:, D + 1 : D + 1 + E]
    shard_gain_one = line[:, :, 3 * gw].sum(axis=0)
    shard_qkv = jnp.concatenate(
        [line[g, :, part * gw : (part + 1) * gw] for part in (2, 0, 1) for g in range(Z)], axis=1
    )
    tables = table_of(line[:, :, 3 * gw + 1 : 3 * gw + 1 + line_width])
    table_total = tables.reshape(heads, buckets).T

    shard_second = shard_second.astype(WIDE)
    first_low = first_low.reshape(Y, D // N, FF // Y)
    first_parts = [pick(first_low, y)] + [
        swap(pick(first_low, y ^ k), ("yy",), k) for k in range(1, Y)
    ]
    first_parts = from_xor(first_parts, y)
    shard_first = jnp.concatenate(
        [
            first_parts[k][:, g * part_ff : (g + 1) * part_ff]
            for g in range(Z)
            for k in range(Y)
        ],
        axis=1,
    ).astype(WIDE)
    return (
        output[None],
        grad_inputs[None],
        shard_gain_one,
        shard_qkv,
        shard_attn_out,
        table_total,
        shard_gain_two,
        shard_router,
        shard_first[None],
        shard_second[None],
    )


def solution(mesh):
    devices_ctx, devices_exp = mesh.shape["ctx"], mesh.shape["exp"]
    outer = 4
    parts = Mesh(
        mesh.devices.reshape(outer, devices_ctx // outer, devices_exp // 2, 2),
        ("hz", "yy", "xx", "cc"),
    )
    ctx, exp = ("hz", "yy"), ("xx", "cc")
    every = ctx + exp
    tokens = P(exp, ctx, None)
    return jax.shard_map(
        body,
        mesh=parts,
        in_specs=(
            tokens,
            P(every),
            P(every, None),
            P(every, None),
            P(),
            P(every),
            P(every, None),
            tokens,
            tokens,
            tokens,
            P(),
            tokens,
        ),
        out_specs=(
            tokens,
            tokens,
            P(every),
            P(every, None),
            P(every, None),
            P(),
            P(every),
            P(every, None),
            tokens,
            tokens,
        ),
        check_vma=False,
    )
```

time: 446 us -> 310 us (0.70); the launches traced: 439 us -> 309 us
  starting transfers between devices: 138 us -> 63.5 us
  local copies, waits for them, and re-layouts: 80.8 us -> 24.5 us
  matrix products: 56.3 us -> 22.8 us
  blocking collectives: 0 us -> 28.8 us
  other arithmetic: 47.1 us -> 27.3 us
  Pallas kernels: 0 us -> 19 us
  between operations: 8.05 us -> 18 us
    ppermute x24 -> x0, starting transfers between devices: 48.7 us -> none  [the longest x6 19.7 us: line_reduce(): right = lax.ppermute(send_right, 'hz', [(i, i + 1) for i in range(s)])]
    ppermute x52 -> x12, waiting for transfers between devices: 55.1 us -> 9.74 us  [swap(): return lax.ppermute(x, axes, [(j ^ k, j) for j in range(n)])]
    ppermute x24 -> x0, waiting for transfers between devices: 44.5 us -> none  [the longest x6 32.7 us: line_gather(): left = lax.ppermute(left, 'hz', [(i, i - 1) for i in range(1, n - s + 1)])]
    ppermute x27 -> x18, waiting for transfers between devices: 8.34 us -> 51.6 us  [shift(): return lax.ppermute(x, axis, [((j + d) % n, j) for j in range(n)])]
    ppermute x52 -> x12, starting transfers between devices: 50.2 us -> 13.3 us  [swap(): return lax.ppermute(x, axes, [(j ^ k, j) for j in range(n)])]
    all_to_all x0 -> x3, waiting for transfers between devices: none -> 32.5 us  [every_block(): return lax.all_to_all(x, axes, split_axis=0, concat_axis=0, tiled=True)]
    dot_general x24 -> x13, matrix products: 46.8 us -> 14.9 us  [dot(): lax.dot_general(left, right, (contract, ((), ())), preferred_element_type...]
    all_to_all x0 -> x1, blocking collectives: none -> 28.8 us  [every_block(): return lax.all_to_all(x, axes, split_axis=0, concat_axis=0, tiled=True)]
  transfers between devices with their start and end apart: 103 -> 37, of which waited for: 37 -> 17; matrix products, arithmetic and copies ran while one was open for 32% -> 23% of each run, Pallas kernels for 0% -> 0%
where the time goes in v2:
time: 310 us; the launch traced here: 309 us
  waiting for transfers between devices  105 us (34%)
  starting transfers between devices  63.5 us (20%)
  blocking collectives  28.8 us (9%)
  other arithmetic  27.3 us (9%)
  local copies, waits for them, and re-layouts  24.5 us (8%)
  matrix products  22.8 us (7%)
  Pallas kernels  19 us (6%)
  between operations  18 us (6%)
    ppermute x18, waiting for transfers between devices, shift(): return lax.ppermute(x, axis, [((j + d) % n, j) for j in range(n)])  51.6 us
    all_to_all x3, waiting for transfers between devices, every_block(): return lax.all_to_all(x, axes, split_axis=0, concat_axis=0, tiled=True)  32.5 us
    ppermute x18, starting transfers between devices, shift(): return lax.ppermute(x, axis, [((j + d) % n, j) for j in range(n)])  30.9 us
    all_to_all x1, blocking collectives, every_block(): return lax.all_to_all(x, axes, split_axis=0, concat_axis=0, tiled=True)  28.8 us
    pallas_call x1, Pallas kernels, expert(): pl.pallas_call(expert_kernel, grid=(units // block,), out_shape=(jax.Shap...  19 us
    all_to_all x3, starting transfers between devices, every_block(): return lax.all_to_all(x, axes, split_axis=0, concat_axis=0, tiled=True)  19 us
    dot_general x13, matrix products, dot(): lax.dot_general(left, right, (contract, ((), ())), preferred_element_type...  14.9 us
    ppermute x12, starting transfers between devices, swap(): return lax.ppermute(x, axes, [(j ^ k, j) for j in range(n)])  13.3 us
  transfers between devices with their start and end apart: 37, of which 17 were waited for; matrix products, arithmetic and copies ran while one was open for 23% of the time, Pallas kernels for 0%

profile of v2, /device:TPU:0, one launch (start us, length us, event | category | flops | bytes accessed | tf_op | source)
XLA Modules:
  0.0 309.2 jit_solution(12534173241125997747)
XLA Ops:
  7.2 5.1 %collective-permute-start = (bf16[128,768]{1,0:T(8,128)(2,1)}, bf16[128,768]{1,0:T(8,128)(2,1)S(1)}, u32[]{:S(2)}, u32[]{:S(2)}) collective-permute-start(bf16[128,768]{1,0:T(8,128)(2,1)} %bitcast.299), channel_id=1, source_target_pairs={{8,0},{16,8},{24,16},{0,24},{9,1},{17,9},{25,17},{1,25},{10,2},{18... | collective-permute-start | bytes 589832 | tf_op jit(solution)/shard_map/ppermute | solution.py:22
  14.8 2.6 collective-permute-start.4
  17.3 1.9 collective-permute-start.5
  26.2 1.5 collective-permute-done.4
  27.9 2.5 collective-permute-start.6
  36.0 1.5 collective-permute-start.21
  37.8 10.2 %collective-permute-done.2 = bf16[128,768]{1,0:T(8,128)(2,1)S(1)} collective-permute-done((bf16[128,768]{1,0:T(8,128)(2,1)S(1)}, bf16[128,768]{1,0:T(8,128)(2,1)S(1)}, u32[]{:S(2)}, u32[]{:S(2)}) %collective-permute-start.2) | collective-permute-done | bytes 196640 | tf_op jit(solution)/shard_map/ppermute | solution.py:22
  51.2 5.9 %collective-permute-start.14 = (bf16[24,768]{1,0:T(8,128)(2,1)S(1)}, bf16[24,768]{1,0:T(8,128)(2,1)S(1)}, u32[]{:S(2)}, u32[]{:S(2)}) collective-permute-start(bf16[24,768]{1,0:T(8,128)(2,1)S(1)} %broadcast_add_fusion), channel_id=1, source_target_pairs={{8,0},{16,8},{24,16},{0,24},{9,1},{17,9},{25,17},{1,25},{10,2},{18... | collective-permute-start | bytes 110600 | tf_op jit(solution)/shard_map/ppermute | solution.py:22
  57.1 1.8 collective-permute-start.16
  59.5 1.7 collective-permute-start.10
  61.2 4.5 %collective-permute-done.15 = bf16[24,768]{1,0:T(8,128)(2,1)S(1)} collective-permute-done((bf16[24,768]{1,0:T(8,128)(2,1)S(1)}, bf16[24,768]{1,0:T(8,128)(2,1)S(1)}, u32[]{:S(2)}, u32[]{:S(2)}) %collective-permute-start.15) | collective-permute-done | bytes 36896 | tf_op jit(solution)/shard_map/ppermute | solution.py:22
  65.7 2.5 collective-permute-start.17
  69.9 2.1 collective-permute-done.17
  72.0 1.7 collective-permute-done.18
  76.8 2.8 fusion.173
  82.9 3.0 collective-permute-start.11
  88.5 2.8 collective-permute-done.12
  91.3 1.7 collective-permute-done.13
  96.7 1.3 select_reduce_fusion.8
  99.9 28.8 %all_to_all.20 = bf16[8,80,1536]{2,1,0:T(8,128)(2,1)} all-to-all(bf16[8,80,1536]{2,1,0:T(8,128)(2,1)S(1)} %pad_maximum_fusion.1), channel_id=1, replica_groups=mesh['hz'=4,'yy'=2,'xx'=2,'cc'=2] {'yy','xx','cc'}, dimensions={0} | all-to-all | bytes 3932160 | tf_op jit(solution)/shard_map/all_to_all | solution.py:132
  128.7 11.1 %all-gather.4.cloned.1.call-done.w_first = bf16[768,1536]{1,0:T(8,128)(2,1)} async-done(((bf16[192,1536]{1,0:T(8,128)(2,1)}), bf16[768,1536]{1,0:T(8,128)(2,1)}) %all-gather.4.cloned.1.call-update) | async-done | bytes 2359312 | tf_op jit(solution)/shard_map/all_gather | solution.py:204
  139.7 19.0 %shard_map.195 = (bf16[640,1536]{1,0:T(8,128)(2,1)}, bf16[768,1536]{1,0:T(8,128)(2,1)}, bf16[1536,768]{1,0:T(8,128)(2,1)}) custom-call(bf16[640,1536]{1,0:T(8,128)(2,1)} %bitcast.291, bf16[768,1536]{1,0:T(8,128)(2,1)} %all-gather.4.cloned.1.call-done.w_first, bf16[1536,768]{1,0:T(8,128)(2,1)} %bitcast.327), custom_call_target="tpu_custom_call" | custom-call | flops 9059696640 | bytes 13369344 | tf_op jit(solution)/shard_map/pallas_call | solution.py:90
  158.8 4.4 %all-to-all-start.1 = ((bf16[8,80,1536]{2,1,0:T(8,128)(2,1)}), bf16[8,80,1536]{2,1,0:T(8,128)(2,1)}, u32[]{:S(2)}, u32[]{:S(2)}) async-start(bf16[8,80,1536]{2,1,0:T(8,128)(2,1)} %bitcast.290), calls=%async_computation.1 | async-start | bytes 3932160 | tf_op jit(solution)/shard_map/all_to_all | solution.py:132
  163.7 24.7 %all-to-all-done.1 = bf16[8,80,1536]{2,1,0:T(8,128)(2,1)} async-done(((bf16[8,80,1536]{2,1,0:T(8,128)(2,1)}), bf16[8,80,1536]{2,1,0:T(8,128)(2,1)}, u32[]{:S(2)}, u32[]{:S(2)}) %all-to-all-start.1) | async-done | bytes 1966112 | tf_op jit(solution)/shard_map/all_to_all | solution.py:132
  188.4 1.8 fusion.11
  190.2 1.6 fusion.13
  191.8 2.4 fusion.48
  194.5 1.6 multiply_reduce_fusion.1
  196.3 1.5 convolution_convert_fusion
  199.7 1.9 collective-permute-start.24
  201.7 2.4 collective-permute-done.22
  204.1 4.7 %collective-permute-done.23 = bf16[128,192]{0,1:T(8,128)(2,1)S(1)} collective-permute-done((bf16[128,192]{0,1:T(8,128)(2,1)S(1)}, bf16[128,192]{0,1:T(8,128)(2,1)S(1)}, u32[]{:S(2)}, u32[]{:S(2)}) %collective-permute-start.23) | collective-permute-done | bytes 49184 | tf_op jit(solution)/shard_map/ppermute | solution.py:22
  214.0 1.5 collective-permute-start.25
  216.4 5.7 %collective-permute-done.25 = bf16[512,384]{0,1:T(8,128)(2,1)} collective-permute-done((bf16[512,384]{0,1:T(8,128)(2,1)}, bf16[512,384]{0,1:T(8,128)(2,1)}, u32[]{:S(2)}, u32[]{:S(2)}) %collective-permute-start.25) | collective-permute-done | bytes 393248 | tf_op jit(solution)/shard_map/ppermute | solution.py:29
  223.3 2.8 multiply_reduce_fusion
  227.5 2.5 copy.83
  230.0 3.3 %copy.84 = bf16[8,4,24,1536]{3,2,1,0:T(8,128)(2,1)} copy(bf16[8,4,24,1536]{3,2,0,1:T(8,128)(2,1)} %bitcast.273) | data formatting | bytes 4718592 | tf_op jit(solution)/shard_map/transpose | solution.py:437
  233.3 6.3 %all-to-all-start.2 = ((bf16[8,96,1536]{2,1,0:T(8,128)(2,1)}), bf16[8,96,1536]{2,1,0:T(8,128)(2,1)S(1)}, u32[]{:S(2)}, u32[]{:S(2)}) async-start(bf16[8,96,1536]{2,1,0:T(8,128)(2,1)} %bitcast.272), calls=%async_computation.2 | async-start | bytes 4718592 | tf_op jit(solution)/shard_map/all_to_all | solution.py:132
  240.4 1.5 collective-permute-start.27
  241.9 2.9 collective-permute-start.28
  244.8 9.6 %collective-permute-done.26 = bf16[128,768]{1,0:T(8,128)(2,1)S(1)} collective-permute-done((bf16[128,768]{1,0:T(8,128)(2,1)}, bf16[128,768]{1,0:T(8,128)(2,1)S(1)}, u32[]{:S(2)}, u32[]{:S(2)}) %collective-permute-start.26) | collective-permute-done | bytes 196640 | tf_op jit(solution)/shard_map/ppermute | solution.py:22
  254.4 13.7 %collective-permute-done.27 = bf16[128,768]{1,0:T(8,128)(2,1)S(1)} collective-permute-done((bf16[128,768]{1,0:T(8,128)(2,1)}, bf16[128,768]{1,0:T(8,128)(2,1)S(1)}, u32[]{:S(2)}, u32[]{:S(2)}) %collective-permute-start.27) | collective-permute-done | bytes 196640 | tf_op jit(solution)/shard_map/ppermute | solution.py:22
  268.6 1.4 multiply_reduce_fusion.2
  274.0 8.3 %all-to-all-start.3 = ((bf16[4,24,1536]{2,1,0:T(8,128)(2,1)}), bf16[4,24,1536]{2,1,0:T(8,128)(2,1)S(1)}, u32[]{:S(2)}, u32[]{:S(2)}) async-start(bf16[4,24,1536]{2,1,0:T(8,128)(2,1)} %pad.20), calls=%async_computation.3 | async-start | bytes 589824 | tf_op jit(solution)/shard_map/all_to_all | solution.py:132
  282.3 2.1 add_bitcast_fusion
  284.4 7.8 %all-to-all-done.3 = bf16[4,24,1536]{2,1,0:T(8,128)(2,1)S(1)} async-done(((bf16[4,24,1536]{2,1,0:T(8,128)(2,1)}), bf16[4,24,1536]{2,1,0:T(8,128)(2,1)S(1)}, u32[]{:S(2)}, u32[]{:S(2)}) %all-to-all-start.3) | async-done | bytes 294944 | tf_op jit(solution)/shard_map/all_to_all | solution.py:132
  294.1 1.4 collective-permute-start.29
  299.2 2.2 bitcast_convert_fusion
  (344 shorter events, 55.5 us)
Async XLA Ops:
  7.2 14.1 %copy-start = (f32[32,12]{0,1:T(8,128)S(1)}, f32[32,12]{0,1:T(8,128)}, u32[]{:S(2)}) copy-start(f32[32,12]{0,1:T(8,128)} %param.16) | copy-start | bytes 4612
  7.2 18.2 %copy-start.39 = (bf16[1,96,3072]{2,1,0:T(8,128)(2,1)S(1)}, bf16[1,96,3072]{2,1,0:T(8,128)(2,1)}, u32[]{:S(2)}) copy-start(bf16[1,96,3072]{2,1,0:T(8,128)(2,1)} %param.19) | copy-start | bytes 1769476
  7.2 121.5 %all-gather.6.cloned.1.call-start = ((), (), s32[]{:S(2)}) async-start(), calls=%async_computation.9 | async-start | bytes 2949120 | tf_op jit(solution)/shard_map/all_gather | solution.py:190
  7.2 30.6 %collective-permute-start = (bf16[128,768]{1,0:T(8,128)(2,1)}, bf16[128,768]{1,0:T(8,128)(2,1)S(1)}, u32[]{:S(2)}, u32[]{:S(2)}) collective-permute-start(bf16[128,768]{1,0:T(8,128)(2,1)} %bitcast.299), channel_id=1, source_target_pairs={{8,0},{16,8},{24,16},{0,24},{9,1},{17,9},{25,17},{1,25},{10,2},{18... | collective-permute-start | bytes 589832 | tf_op jit(solution)/shard_map/ppermute | solution.py:22
  12.4 25.5 %collective-permute-start.1 = (bf16[128,768]{1,0:T(8,128)(2,1)}, bf16[128,768]{1,0:T(8,128)(2,1)S(1)}, u32[]{:S(2)}, u32[]{:S(2)}) collective-permute-start(bf16[128,768]{1,0:T(8,128)(2,1)} %bitcast.300), channel_id=1, source_target_pairs={{16,0},{24,8},{0,16},{8,24},{17,1},{25,9},{1,17},{9,25},{18,2},{26... | collective-permute-start | bytes 589832 | tf_op jit(solution)/shard_map/ppermute | solution.py:22
  14.3 11.9 %collective-permute-start.3 = (bf16[24,640]{1,0:T(8,128)(2,1)S(1)}, bf16[24,640]{1,0:T(8,128)(2,1)S(1)}, u32[]{:S(2)}, u32[]{:S(2)}) collective-permute-start(bf16[24,640]{1,0:T(8,128)(2,1)S(1)} %get-tuple-element.153), channel_id=1, source_target_pairs={{8,0},{16,8},{24,16},{0,24},{9,1},{17,9},{25,17},{1,25},{10,2},{18... | collective-permute-start | bytes 92168 | tf_op jit(solution)/shard_map/ppermute | solution.py:22
  14.8 12.9 %collective-permute-start.4 = (bf16[24,640]{1,0:T(8,128)(2,1)S(1)}, bf16[24,640]{1,0:T(8,128)(2,1)S(1)}, u32[]{:S(2)}, u32[]{:S(2)}) collective-permute-start(bf16[24,640]{1,0:T(8,128)(2,1)S(1)} %get-tuple-element.154), channel_id=1, source_target_pairs={{16,0},{24,8},{0,16},{8,24},{17,1},{25,9},{1,17},{9,25},{18,2},{26... | collective-permute-start | bytes 92168 | tf_op jit(solution)/shard_map/ppermute | solution.py:22
  17.3 10.3 %collective-permute-start.5 = (bf16[24,640]{1,0:T(8,128)(2,1)S(1)}, bf16[24,640]{1,0:T(8,128)(2,1)S(1)}, u32[]{:S(2)}, u32[]{:S(2)}) collective-permute-start(bf16[24,640]{1,0:T(8,128)(2,1)S(1)} %get-tuple-element.155), channel_id=1, source_target_pairs={{24,0},{0,8},{8,16},{16,24},{25,1},{1,9},{9,17},{17,25},{26,2},{2,... | collective-permute-start | bytes 92168 | tf_op jit(solution)/shard_map/ppermute | solution.py:22
  19.3 120.4 %all-gather.4.cloned.1.call-start = ((), (), s32[]{:S(2)}) async-start(), calls=%async_computation.6 | async-start | bytes 2949120 | tf_op jit(solution)/shard_map/all_gather | solution.py:204
  27.9 7.2 %collective-permute-start.6 = (bf16[4,24,640]{2,1,0:T(8,128)(2,1)S(1)}, bf16[4,24,640]{2,1,0:T(8,128)(2,1)S(1)}, u32[]{:S(2)}, u32[]{:S(2)}) collective-permute-start(bf16[4,24,640]{2,1,0:T(8,128)(2,1)S(1)} %pad_maximum_fusion.15), channel_id=1, source_target_pairs={{6,0},{4,2},{2,4},{0,6},{7,1},{5,3},{3,5},{1,7},{14,8},{12,10},{10... | collective-permute-start | bytes 368648 | tf_op jit(solution)/shard_map/ppermute | solution.py:29
  30.4 5.6 %collective-permute-start.7 = (bf16[4,24,640]{2,1,0:T(8,128)(2,1)S(1)}, bf16[4,24,640]{2,1,0:T(8,128)(2,1)S(1)}, u32[]{:S(2)}, u32[]{:S(2)}) collective-permute-start(bf16[4,24,640]{2,1,0:T(8,128)(2,1)S(1)} %pad_maximum_fusion.15), channel_id=1, source_target_pairs={{4,0},{6,2},{0,4},{2,6},{5,1},{7,3},{1,5},{3,7},{12,8},{14,10},{8,... | collective-permute-start | bytes 368648 | tf_op jit(solution)/shard_map/ppermute | solution.py:29
  30.9 6.6 %collective-permute-start.8 = (bf16[4,24,640]{2,1,0:T(8,128)(2,1)S(1)}, bf16[4,24,640]{2,1,0:T(8,128)(2,1)S(1)}, u32[]{:S(2)}, u32[]{:S(2)}) collective-permute-start(bf16[4,24,640]{2,1,0:T(8,128)(2,1)S(1)} %pad_maximum_fusion.15), channel_id=1, source_target_pairs={{2,0},{0,2},{6,4},{4,6},{3,1},{1,3},{7,5},{5,7},{10,8},{8,10},{14,... | collective-permute-start | bytes 368648 | tf_op jit(solution)/shard_map/ppermute | solution.py:29
  35.1 13.0 %collective-permute-start.2 = (bf16[128,768]{1,0:T(8,128)(2,1)S(1)}, bf16[128,768]{1,0:T(8,128)(2,1)S(1)}, u32[]{:S(2)}, u32[]{:S(2)}) collective-permute-start(bf16[128,768]{1,0:T(8,128)(2,1)S(1)} %bitcast.301), channel_id=1, source_target_pairs={{24,0},{0,8},{8,16},{16,24},{25,1},{1,9},{9,17},{17,25},{26,2},{2,... | collective-permute-start | bytes 589832 | tf_op jit(solution)/shard_map/ppermute | solution.py:22
  36.0 12.3 %collective-permute-start.21 = (bf16[96,1536]{1,0:T(8,128)(2,1)S(1)}, bf16[96,1536]{1,0:T(8,128)(2,1)S(1)}, u32[]{:S(2)}, u32[]{:S(2)}) collective-permute-start(bf16[96,1536]{1,0:T(8,128)(2,1)S(1)} %fusion.59), channel_id=1, source_target_pairs={{4,0},{0,4},{5,1},{1,5},{6,2},{2,6},{7,3},{3,7},{12,8},{8,12},{13,... | collective-permute-start | bytes 884744 | tf_op jit(solution)/shard_map/ppermute | solution.py:29
  37.7 11.6 %collective-permute-start.9 = (bf16[4,4,24,640]{3,2,1,0:T(8,128)(2,1)S(1)}, bf16[4,4,24,640]{3,2,1,0:T(8,128)(2,1)S(1)}, u32[]{:S(2)}, u32[]{:S(2)}) collective-permute-start(bf16[4,4,24,640]{3,2,1,0:T(8,128)(2,1)S(1)} %pad_maximum_fusion.9), channel_id=1, source_target_pairs={{1,0},{0,1},{3,2},{2,3},{5,4},{4,5},{7,6},{6,7},{9,8},{8,9},{11,10... | collective-permute-start | bytes 1474568 | tf_op jit(solution)/shard_map/ppermute | solution.py:29
  37.8 31.5 %copy-start.51 = (bf16[128,768]{1,0:T(8,128)(2,1)}, bf16[128,768]{1,0:T(8,128)(2,1)S(1)}, u32[]{:S(2)}) copy-start(bf16[128,768]{1,0:T(8,128)(2,1)S(1)} %collective-permute-done) | copy-start | bytes 589828
  37.8 31.5 %copy-start.53 = (bf16[128,768]{1,0:T(8,128)(2,1)}, bf16[128,768]{1,0:T(8,128)(2,1)S(1)}, u32[]{:S(2)}) copy-start(bf16[128,768]{1,0:T(8,128)(2,1)S(1)} %collective-permute-done.1) | copy-start | bytes 589828
  48.1 21.2 %copy-start.55 = (bf16[128,768]{1,0:T(8,128)(2,1)}, bf16[128,768]{1,0:T(8,128)(2,1)S(1)}, u32[]{:S(2)}) copy-start(bf16[128,768]{1,0:T(8,128)(2,1)S(1)} %collective-permute-done.2) | copy-start | bytes 589828
  48.3 21.0 %copy-start.71 = (f32[512]{0:T(512)}, f32[512]{0:T(512)S(1)}, u32[]{:S(2)}) copy-start(f32[512]{0:T(512)S(1)} %add_rsqrt_fusion) | copy-start | bytes 6148
  49.6 19.7 %copy-start.15 = (bf16[4,4,2,24,640]{4,3,2,1,0:T(8,128)(2,1)}, bf16[4,4,2,24,640]{4,3,2,1,0:T(8,128)(2,1)S(1)}, u32[]{:S(2)}) copy-start(bf16[4,4,2,24,640]{4,3,2,1,0:T(8,128)(2,1)S(1)} %copy.73) | copy-start | bytes 2949124
  51.2 10.0 %collective-permute-start.14 = (bf16[24,768]{1,0:T(8,128)(2,1)S(1)}, bf16[24,768]{1,0:T(8,128)(2,1)S(1)}, u32[]{:S(2)}, u32[]{:S(2)}) collective-permute-start(bf16[24,768]{1,0:T(8,128)(2,1)S(1)} %broadcast_add_fusion), channel_id=1, source_target_pairs={{8,0},{16,8},{24,16},{0,24},{9,1},{17,9},{25,17},{1,25},{10,2},{18... | collective-permute-start | bytes 110600 | tf_op jit(solution)/shard_map/ppermute | solution.py:22
  57.1 8.6 %collective-permute-start.15 = (bf16[24,768]{1,0:T(8,128)(2,1)S(1)}, bf16[24,768]{1,0:T(8,128)(2,1)S(1)}, u32[]{:S(2)}, u32[]{:S(2)}) collective-permute-start(bf16[24,768]{1,0:T(8,128)(2,1)S(1)} %broadcast_add_fusion), channel_id=1, source_target_pairs={{16,0},{24,8},{0,16},{8,24},{17,1},{25,9},{1,17},{9,25},{18,2},{26... | collective-permute-start | bytes 110600 | tf_op jit(solution)/shard_map/ppermute | solution.py:22
  57.1 8.6 %collective-permute-start.16 = (bf16[24,768]{1,0:T(8,128)(2,1)S(1)}, bf16[24,768]{1,0:T(8,128)(2,1)S(1)}, u32[]{:S(2)}, u32[]{:S(2)}) collective-permute-start(bf16[24,768]{1,0:T(8,128)(2,1)S(1)} %broadcast_add_fusion), channel_id=1, source_target_pairs={{24,0},{0,8},{8,16},{16,24},{25,1},{1,9},{9,17},{17,25},{26,2},{2,... | collective-permute-start | bytes 110600 | tf_op jit(solution)/shard_map/ppermute | solution.py:22
  59.5 15.5 %collective-permute-start.10 = (bf16[512,384]{1,0:T(8,128)(2,1)S(1)}, bf16[512,384]{1,0:T(8,128)(2,1)S(1)}, u32[]{:S(2)}, u32[]{:S(2)}) collective-permute-start(bf16[512,384]{1,0:T(8,128)(2,1)S(1)} %convolution_convert_fusion.4), channel_id=1, source_target_pairs={{4,0},{0,4},{5,1},{1,5},{6,2},{2,6},{7,3},{3,7},{12,8},{8,12},{13,... | collective-permute-start | bytes 1179656 | tf_op jit(solution)/shard_map/ppermute | solution.py:29
  65.7 6.2 %collective-permute-start.17 = (bf16[4,24,768]{2,1,0:T(8,128)(2,1)S(1)}, bf16[4,24,768]{2,1,0:T(8,128)(2,1)S(1)}, u32[]{:S(2)}, u32[]{:S(2)}) collective-permute-start(bf16[4,24,768]{2,1,0:T(8,128)(2,1)S(1)} %pad_maximum_fusion.14), channel_id=1, source_target_pairs={{6,0},{4,2},{2,4},{0,6},{7,1},{5,3},{3,5},{1,7},{14,8},{12,10},{10... | collective-permute-start | bytes 442376 | tf_op jit(solution)/shard_map/ppermute | solution.py:29
  68.2 5.5 %collective-permute-start.18 = (bf16[4,24,768]{2,1,0:T(8,128)(2,1)S(1)}, bf16[4,24,768]{2,1,0:T(8,128)(2,1)S(1)}, u32[]{:S(2)}, u32[]{:S(2)}) collective-permute-start(bf16[4,24,768]{2,1,0:T(8,128)(2,1)S(1)} %pad_maximum_fusion.14), channel_id=1, source_target_pairs={{4,0},{6,2},{0,4},{2,6},{5,1},{7,3},{1,5},{3,7},{12,8},{14,10},{8,... | collective-permute-start | bytes 442376 | tf_op jit(solution)/shard_map/ppermute | solution.py:29
  68.8 5.1 %collective-permute-start.19 = (bf16[4,24,768]{2,1,0:T(8,128)(2,1)S(1)}, bf16[4,24,768]{2,1,0:T(8,128)(2,1)S(1)}, u32[]{:S(2)}, u32[]{:S(2)}) collective-permute-start(bf16[4,24,768]{2,1,0:T(8,128)(2,1)S(1)} %pad_maximum_fusion.14), channel_id=1, source_target_pairs={{2,0},{0,2},{6,4},{4,6},{3,1},{1,3},{7,5},{5,7},{10,8},{8,10},{14,... | collective-permute-start | bytes 442376 | tf_op jit(solution)/shard_map/ppermute | solution.py:29
  75.0 18.9 %collective-permute-start.20 = (bf16[4,4,24,768]{3,2,0,1:T(8,128)(2,1)}, bf16[4,4,24,768]{3,2,0,1:T(8,128)(2,1)}, u32[]{:S(2)}, u32[]{:S(2)}) collective-permute-start(bf16[4,4,24,768]{3,2,0,1:T(8,128)(2,1)} %pad_maximum_fusion.5), channel_id=1, source_target_pairs={{1,0},{0,1},{3,2},{2,3},{5,4},{4,5},{7,6},{6,7},{9,8},{8,9},{11,10... | collective-permute-start | bytes 1769480 | tf_op jit(solution)/shard_map/ppermute | solution.py:29
  81.6 12.3 %copy-start.22 = (bf16[1,4,24,768]{3,2,0,1:T(8,128)(2,1)S(1)}, bf16[1,4,24,768]{3,2,0,1:T(8,128)(2,1)}, u32[]{:S(2)}) copy-start(bf16[1,4,24,768]{3,2,0,1:T(8,128)(2,1)} %copy-done.21) | copy-start | bytes 442372
  81.6 12.3 %copy-start.24 = (bf16[1,4,24,768]{3,2,0,1:T(8,128)(2,1)S(1)}, bf16[1,4,24,768]{3,2,0,1:T(8,128)(2,1)}, u32[]{:S(2)}) copy-start(bf16[1,4,24,768]{3,2,0,1:T(8,128)(2,1)} %copy-done.23) | copy-start | bytes 442372
  82.9 5.5 %collective-permute-start.11 = (bf16[128,192]{0,1:T(8,128)(2,1)}, bf16[128,192]{0,1:T(8,128)(2,1)S(1)}, u32[]{:S(2)}, u32[]{:S(2)}) collective-permute-start(bf16[128,192]{0,1:T(8,128)(2,1)} %bitcast.23), channel_id=1, source_target_pairs={{8,0},{16,8},{24,16},{0,24},{9,1},{17,9},{25,17},{1,25},{10,2},{18... | collective-permute-start | bytes 147464 | tf_op jit(solution)/shard_map/ppermute | solution.py:22
  85.9 5.4 %collective-permute-start.12 = (bf16[128,192]{0,1:T(8,128)(2,1)}, bf16[128,192]{0,1:T(8,128)(2,1)}, u32[]{:S(2)}, u32[]{:S(2)}) collective-permute-start(bf16[128,192]{0,1:T(8,128)(2,1)} %bitcast.24), channel_id=1, source_target_pairs={{16,0},{24,8},{0,16},{8,24},{17,1},{25,9},{1,17},{9,25},{18,2},{26... | collective-permute-start | bytes 147464 | tf_op jit(solution)/shard_map/ppermute | solution.py:22
  86.8 6.2 %collective-permute-start.13 = (bf16[128,192]{0,1:T(8,128)(2,1)}, bf16[128,192]{0,1:T(8,128)(2,1)}, u32[]{:S(2)}, u32[]{:S(2)}) collective-permute-start(bf16[128,192]{0,1:T(8,128)(2,1)} %bitcast.25), channel_id=1, source_target_pairs={{24,0},{0,8},{8,16},{16,24},{25,1},{1,9},{9,17},{17,25},{26,2},{2,... | collective-permute-start | bytes 147464 | tf_op jit(solution)/shard_map/ppermute | solution.py:22
  88.2 204.8 %reduce-scatter.3.cloned.1.call-start = ((), (), s32[]{:S(2)}) async-start(), calls=%async_computation.7 | async-start | bytes 2949120 | tf_op jit(solution)/shard_map/reduce_scatter | solution.py:319
  158.8 29.6 %all-to-all-start.1 = ((bf16[8,80,1536]{2,1,0:T(8,128)(2,1)}), bf16[8,80,1536]{2,1,0:T(8,128)(2,1)}, u32[]{:S(2)}, u32[]{:S(2)}) async-start(bf16[8,80,1536]{2,1,0:T(8,128)(2,1)} %bitcast.290), calls=%async_computation.1 | async-start | bytes 3932160 | tf_op jit(solution)/shard_map/all_to_all | solution.py:132
  163.1 136.0 %reduce-scatter.5.cloned.1.call-start = ((), (), s32[]{:S(2)}) async-start(), calls=%async_computation.8 | async-start | bytes 2949120 | tf_op jit(solution)/shard_map/reduce_scatter | solution.py:320
  198.3 5.8 %collective-permute-start.22 = (bf16[128,192]{0,1:T(8,128)(2,1)S(1)}, bf16[128,192]{0,1:T(8,128)(2,1)S(1)}, u32[]{:S(2)}, u32[]{:S(2)}) collective-permute-start(bf16[128,192]{0,1:T(8,128)(2,1)S(1)} %get-tuple-element.122), channel_id=1, source_target_pairs={{8,0},{16,8},{24,16},{0,24},{9,1},{17,9},{25,17},{1,25},{10,2},{18... | collective-permute-start | bytes 147464 | tf_op jit(solution)/shard_map/ppermute | solution.py:22
  199.3 9.5 %collective-permute-start.23 = (bf16[128,192]{0,1:T(8,128)(2,1)S(1)}, bf16[128,192]{0,1:T(8,128)(2,1)S(1)}, u32[]{:S(2)}, u32[]{:S(2)}) collective-permute-start(bf16[128,192]{0,1:T(8,128)(2,1)S(1)} %get-tuple-element.121), channel_id=1, source_target_pairs={{16,0},{24,8},{0,16},{8,24},{17,1},{25,9},{1,17},{9,25},{18,2},{26... | collective-permute-start | bytes 147464 | tf_op jit(solution)/shard_map/ppermute | solution.py:22
  199.7 9.0 %collective-permute-start.24 = (bf16[128,192]{0,1:T(8,128)(2,1)S(1)}, bf16[128,192]{0,1:T(8,128)(2,1)S(1)}, u32[]{:S(2)}, u32[]{:S(2)}) collective-permute-start(bf16[128,192]{0,1:T(8,128)(2,1)S(1)} %get-tuple-element.120), channel_id=1, source_target_pairs={{24,0},{0,8},{8,16},{16,24},{25,1},{1,9},{9,17},{17,25},{26,2},{2,... | collective-permute-start | bytes 147464 | tf_op jit(solution)/shard_map/ppermute | solution.py:22
  214.0 8.1 %collective-permute-start.25 = (bf16[512,384]{0,1:T(8,128)(2,1)}, bf16[512,384]{0,1:T(8,128)(2,1)}, u32[]{:S(2)}, u32[]{:S(2)}) collective-permute-start(bf16[512,384]{0,1:T(8,128)(2,1)} %fusion.20), channel_id=1, source_target_pairs={{4,0},{0,4},{5,1},{1,5},{6,2},{2,6},{7,3},{3,7},{12,8},{8,12},{13,... | collective-permute-start | bytes 1179656 | tf_op jit(solution)/shard_map/ppermute | solution.py:29
  233.3 36.7 %all-to-all-start.2 = ((bf16[8,96,1536]{2,1,0:T(8,128)(2,1)}), bf16[8,96,1536]{2,1,0:T(8,128)(2,1)S(1)}, u32[]{:S(2)}, u32[]{:S(2)}) async-start(bf16[8,96,1536]{2,1,0:T(8,128)(2,1)} %bitcast.272), calls=%async_computation.2 | async-start | bytes 4718592 | tf_op jit(solution)/shard_map/all_to_all | solution.py:132
  240.4 14.0 %collective-permute-start.26 = (bf16[128,768]{1,0:T(8,128)(2,1)}, bf16[128,768]{1,0:T(8,128)(2,1)S(1)}, u32[]{:S(2)}, u32[]{:S(2)}) collective-permute-start(bf16[128,768]{1,0:T(8,128)(2,1)} %get-tuple-element.83), channel_id=1, source_target_pairs={{24,0},{0,8},{8,16},{16,24},{25,1},{1,9},{9,17},{17,25},{26,2},{2,... | collective-permute-start | bytes 589832 | tf_op jit(solution)/shard_map/ppermute | solution.py:22
  240.4 27.7 %collective-permute-start.27 = (bf16[128,768]{1,0:T(8,128)(2,1)}, bf16[128,768]{1,0:T(8,128)(2,1)S(1)}, u32[]{:S(2)}, u32[]{:S(2)}) collective-permute-start(bf16[128,768]{1,0:T(8,128)(2,1)} %get-tuple-element.85), channel_id=1, source_target_pairs={{16,0},{24,8},{0,16},{8,24},{17,1},{25,9},{1,17},{9,25},{18,2},{26... | collective-permute-start | bytes 589832 | tf_op jit(solution)/shard_map/ppermute | solution.py:22
  241.9 26.7 %collective-permute-start.28 = (bf16[128,768]{1,0:T(8,128)(2,1)}, bf16[128,768]{1,0:T(8,128)(2,1)S(1)}, u32[]{:S(2)}, u32[]{:S(2)}) collective-permute-start(bf16[128,768]{1,0:T(8,128)(2,1)} %get-tuple-element.84), channel_id=1, source_target_pairs={{8,0},{16,8},{24,16},{0,24},{9,1},{17,9},{25,17},{1,25},{10,2},{18... | collective-permute-start | bytes 589832 | tf_op jit(solution)/shard_map/ppermute | solution.py:22
  270.4 11.9 %copy-start.7 = (f32[128,768]{1,0:T(8,128)S(1)}, f32[128,768]{1,0:T(8,128)}, u32[]{:S(2)}) copy-start(f32[128,768]{1,0:T(8,128)} %copy-done.6) | copy-start | bytes 1179652
  270.4 11.9 %slice-start = ((f32[512]{0:T(512)}), f32[128]{0:T(128)S(1)}, s32[]{:S(2)}) async-start(f32[512]{0:T(512)} %copy-done.71), calls=%async_computation.10 | async-start | bytes 1024 | tf_op jit(solution)/shard_map/slice | solution.py:395
  274.0 18.2 %all-to-all-start.3 = ((bf16[4,24,1536]{2,1,0:T(8,128)(2,1)}), bf16[4,24,1536]{2,1,0:T(8,128)(2,1)S(1)}, u32[]{:S(2)}, u32[]{:S(2)}) async-start(bf16[4,24,1536]{2,1,0:T(8,128)(2,1)} %pad.20), calls=%async_computation.3 | async-start | bytes 589824 | tf_op jit(solution)/shard_map/all_to_all | solution.py:132
  294.1 7.2 %collective-permute-start.29 = (bf16[96,1536]{1,0:T(8,128)(2,1)S(1)}, bf16[96,1536]{1,0:T(8,128)(2,1)S(1)}, u32[]{:S(2)}, u32[]{:S(2)}) collective-permute-start(bf16[96,1536]{1,0:T(8,128)(2,1)S(1)} %dynamic-slice_bitcast_fusion), channel_id=1, source_target_pairs={{4,0},{0,4},{5,1},{1,5},{6,2},{2,6},{7,3},{3,7},{12,8},{8,12},{13,... | collective-permute-start | bytes 884744 | tf_op jit(solution)/shard_map/ppermute | solution.py:29
  (63 other events, 197.8 us)
Sparse Core Ops, SparseCore 0:
  19.4 57.1 all-gather.5
  88.4 51.3 all-gather.3
  158.9 49.9 reduce-scatter.2
  211.0 59.1 reduce-scatter.4

commit v3 on v2

--- a/solution.py
+++ b/solution.py
@@ -385,67 +385,71 @@
     grad_qkv = jnp.concatenate([grad_kv_own, grad_q_rows], axis=1).astype(LOW)
 
     grad_normed_part = dot(grad_qkv, w_all[:, : 3 * gw], ((1,), (1,)))
-    grad_gain_one = jnp.sum(grad_normed_part * hat_one, axis=0)
     grad_low = grad_normed_part.astype(LOW).reshape(Z, own_rows, D)
     grad_normed_one = grad_normed_part[:own_rows]
     for d in range(1, Z):
         grad_normed_one = grad_normed_one + shift(grad_low[d], "hz", -d).astype(WIDE)
+    def pad_columns(columns):
+        return jnp.pad(columns, ((0, 0), (0, 128 - columns.shape[1])))
+
+    attn_part = jnp.concatenate(
+        [grad_attn_out, pad_columns(jnp.concatenate([grad_gain_two[:, None], grad_router], 1))],
+        axis=1,
+    )
+    me_c = lax.axis_index("cc")
+    cores = lax.axis_size("cc")
+    yx = Y * E // cores
+
+    def to_chip(part):
+        split = part.astype(LOW).reshape(Z, yx, cores, shard, part.shape[1])
+        split = split.transpose(2, 1, 0, 3, 4).reshape(cores, yx, Z * shard, part.shape[1])
+        other = swap(pick(split, 1 - me_c), ("cc",), 1)
+        return (pick(split, me_c).astype(WIDE) + other.astype(WIDE)).astype(LOW)
+
+    attn_chip = to_chip(attn_part)
+
+    line_rows = Z * shard
+    table_size = 3 * hg * buckets
+
+    def table_columns(table, rows):
+        width = -(-table_size // rows)
+        terms = jnp.pad(low_terms(table).reshape(-1), (0, rows * width - table_size))
+        return terms.reshape(rows, width)
+
+    def table_of(columns):
+        terms = columns.reshape(columns.shape[0], -1)[:, :table_size]
+        return terms.reshape(-1, 3, hg, buckets).sum(axis=1)
+
+    grad_w_qkv = dot(normed_one, grad_qkv, ((0,), (0,))).astype(LOW)
+    table_chip = table_part + swap(table_part, ("cc",), 1)
+    table_block = table_columns(table_chip, line_rows)
+    table_width = table_block.shape[1]
+    extra_width = -(-(3 * gw + table_width) // 128) * 128 - 3 * gw
+    table_block = jnp.pad(table_block, ((0, 0), (0, extra_width - table_width)))
+    extra = jnp.broadcast_to(table_block[None], (yx, line_rows, extra_width))
+    attn_width = attn_part.shape[1]
+    chip_blocks = jnp.concatenate([attn_chip, to_chip(grad_w_qkv), extra], axis=2)
+    got = every_block(chip_blocks, ("yy", "xx")).astype(WIDE)
+    layer_sum = got[:, :, : attn_width + 3 * gw].sum(axis=0)
+    attn_sum, qkv_sum = layer_sum[:, :attn_width], layer_sum[:, attn_width:]
+    table_at = attn_width + 3 * gw
+    layer_table = table_of(got[:, :, table_at : table_at + table_width]).sum(axis=0)
+    first_low = first_low.reshape(Y, D // N, FF // Y)
+    first_sent = [pick(first_low, y ^ k) for k in range(1, Y)]
+    first_got = [swap(sent, ("yy",), k) for k, sent in enumerate(first_sent, 1)]
+    first_parts = from_xor([pick(first_low, y)] + first_got, y)
+    table_block = after(table_columns(layer_table, shard), grad_low, *first_sent)
+    line_width = table_block.shape[1]
+    grad_normed_one = after(grad_normed_one, *first_got)
     own_hat = hat_one[:own_rows]
     grad_hat_one = grad_normed_one * gain_first
     grad_inputs = grad_resid + scale_one[:own_rows] * (
         grad_hat_one - own_hat * jnp.mean(grad_hat_one * own_hat, axis=-1, keepdims=True)
     )
-
-    def pad_columns(columns):
-        return jnp.pad(columns, ((0, 0), (0, 128 - columns.shape[1])))
-
-    attn_part = jnp.concatenate(
-        [grad_attn_out, pad_columns(jnp.concatenate([grad_gain_two[:, None], grad_router], 1))],
-        axis=1,
-    )
-    attn_part = attn_part.astype(LOW)
-    attn_width = attn_part.shape[1]
-    line_rows = Z * shard
-    table_size = 3 * hg * buckets
-
-    def table_columns(table, rows):
-        width = -(-table_size // rows)
-        terms = jnp.pad(low_terms(table).reshape(-1), (0, rows * width - table_size))
-        return terms.reshape(rows, width)
-
-    def table_of(columns):
-        terms = columns.reshape(columns.shape[0], -1)[:, :table_size]
-        return terms.reshape(-1, 3, hg, buckets).sum(axis=1)
-
-    grad_w_qkv = dot(normed_one, grad_qkv, ((0,), (0,))).astype(LOW)
-    table_block = table_columns(table_part, line_rows)
-    table_width = table_block.shape[1]
-    extra = jnp.concatenate(
-        [
-            grad_gain_one[:, None].astype(LOW).reshape(Z, -1, shard, 1),
-            jnp.broadcast_to(
-                table_block.reshape(Z, 1, shard, table_width),
-                (Z, Y * E, shard, table_width),
-            ),
-        ],
-        axis=3,
-    ).reshape(D, 1 + table_width)
-    extra_width = -(-(3 * gw + 1 + table_width) // 128) * 128 - 3 * gw
-    extra = jnp.pad(extra, ((0, 0), (0, extra_width - 1 - table_width)))
-    outer_blocks = jnp.concatenate([grad_w_qkv, extra, attn_part], axis=1)
-    full_width = outer_blocks.shape[1]
-    outer_blocks = outer_blocks.reshape(Z, Y * E, shard, full_width).transpose(1, 0, 2, 3)
-    got = every_block(outer_blocks.reshape(Y * E, line_rows, full_width), LAYER)
-    got = got.astype(WIDE)
-    layer_sum = got.sum(axis=0)
-    qkv_sum, attn_sum = layer_sum[:, : 3 * gw + 1], layer_sum[:, full_width - attn_width :]
-    layer_table = table_of(got[:, :, 3 * gw + 1 : 3 * gw + 1 + table_width]).sum(axis=0)
-    table_block = table_columns(layer_table, shard)
-    line_width = table_block.shape[1]
     line_blocks = jnp.concatenate(
         [
             attn_sum.astype(LOW).reshape(Z, shard, attn_width),
-            qkv_sum.astype(LOW).reshape(Z, shard, 3 * gw + 1),
+            qkv_sum.astype(LOW).reshape(Z, shard, 3 * gw),
             jnp.broadcast_to(table_block[None], (Z, shard, line_width)),
         ],
         axis=2,
@@ -453,23 +457,21 @@
     line_pad = -(-line_blocks.shape[2] // 128) * 128 - line_blocks.shape[2]
     line_blocks = jnp.pad(line_blocks, ((0, 0), (0, 0), (0, line_pad)))
     line = every_block(line_blocks, ("hz",)).astype(WIDE)
-    attn_total, line = line[:, :, :attn_width].sum(axis=0), line[:, :, attn_width:]
+    attn_total = line[:, :, :attn_width].sum(axis=0)
     shard_attn_out = attn_total[:, :D]
     shard_gain_two = attn_total[:, D]
     shard_router = attn_total[:, D + 1 : D + 1 + E]
-    shard_gain_one = line[:, :, 3 * gw].sum(axis=0)
+    line = line[:, :, attn_width:]
     shard_qkv = jnp.concatenate(
         [line[g, :, part * gw : (part + 1) * gw] for part in (2, 0, 1) for g in range(Z)], axis=1
     )
-    tables = table_of(line[:, :, 3 * gw + 1 : 3 * gw + 1 + line_width])
+    shard_gain_one = jnp.sum(
+        shard_qkv * query_key_value_weight.astype(WIDE), axis=1
+    ) / gain_one.astype(WIDE)
+    tables = table_of(line[:, :, 3 * gw : 3 * gw + line_width])
     table_total = tables.reshape(heads, buckets).T
 
-    shard_second = shard_second.astype(WIDE)
-    first_low = first_low.reshape(Y, D // N, FF // Y)
-    first_parts = [pick(first_low, y)] + [
-        swap(pick(first_low, y ^ k), ("yy",), k) for k in range(1, Y)
-    ]
-    first_parts = from_xor(first_parts, y)
+    shard_second = after(shard_second, table_block).astype(WIDE)
     shard_first = jnp.concatenate(
         [
             first_parts[k][:, g * part_ff : (g + 1) * part_ff]

time: 310 us -> 296 us (0.955)
  waiting for transfers between devices: 105 us -> 84.8 us
  other arithmetic: 27.3 us -> 33.5 us
  starting transfers between devices: 63.5 us -> 58.3 us
    ppermute x18, waiting for transfers between devices: 51.6 us -> 23.3 us  [shift(): return lax.ppermute(x, axis, [((j + d) % n, j) for j in range(n)])]
    reduce_scatter x1, waiting for transfers between devices: 0.01 us -> 9.11 us  [body(): lax.psum_scatter(grad_second, 'hz', scatter_dimension=0, tiled=True)]
    all_to_all x3, starting transfers between devices: 19 us -> 14.2 us  [every_block(): return lax.all_to_all(x, axes, split_axis=0, concat_axis=0, tiled=True)]
    transpose x1, local copies, waits for them, and re-layouts: 3.28 us -> 0.09 us  [to_chip(): split.transpose(2, 1, 0, 3, 4).reshape(cores, yx, Z * shard, part.shape[1])]
    ppermute x12 -> x15, waiting for transfers between devices: 9.74 us -> 10.2 us  [swap(): return lax.ppermute(x, axes, [(j ^ k, j) for j in range(n)])]
    ppermute x12 -> x15, starting transfers between devices: 13.3 us -> 13.4 us  [swap(): return lax.ppermute(x, axes, [(j ^ k, j) for j in range(n)])]
  transfers between devices with their start and end apart: 37 -> 40, of which waited for: 17 -> 16; matrix products, arithmetic and copies ran while one was open for 23% -> 25% of each run, Pallas kernels for 0% -> 0%
where the time goes in v3:
time: 296 us; the launch traced here: 293 us
  waiting for transfers between devices  84.8 us (29%)
  starting transfers between devices  58.3 us (20%)
  other arithmetic  33.5 us (11%)
  blocking collectives  28.8 us (10%)
  local copies, waits for them, and re-layouts  25.3 us (9%)
  matrix products  22 us (7%)
  between operations  20.9 us (7%)
  Pallas kernels  19 us (6%)
    all_to_all x3, waiting for transfers between devices, every_block(): return lax.all_to_all(x, axes, split_axis=0, concat_axis=0, tiled=True)  30.6 us
    ppermute x18, starting transfers between devices, shift(): return lax.ppermute(x, axis, [((j + d) % n, j) for j in range(n)])  30.4 us
    all_to_all x1, blocking collectives, every_block(): return lax.all_to_all(x, axes, split_axis=0, concat_axis=0, tiled=True)  28.8 us
    ppermute x18, waiting for transfers between devices, shift(): return lax.ppermute(x, axis, [((j + d) % n, j) for j in range(n)])  23.3 us
    pallas_call x1, Pallas kernels, expert(): pl.pallas_call(expert_kernel, grid=(units // block,), out_shape=(jax.Shap...  19 us
    all_to_all x3, starting transfers between devices, every_block(): return lax.all_to_all(x, axes, split_axis=0, concat_axis=0, tiled=True)  14.2 us
    dot_general x13, matrix products, dot(): lax.dot_general(left, right, (contract, ((), ())), preferred_element_type...  14.1 us
    ppermute x15, starting transfers between devices, swap(): return lax.ppermute(x, axes, [(j ^ k, j) for j in range(n)])  13.4 us
  transfers between devices with their start and end apart: 40, of which 16 were waited for; matrix products, arithmetic and copies ran while one was open for 25% of the time, Pallas kernels for 0%

profile of v3, /device:TPU:0, one launch (start us, length us, event | category | flops | bytes accessed | tf_op | source)
XLA Modules:
  0.0 292.7 jit_solution(10548580819007036365)
XLA Ops:
  7.2 5.1 %collective-permute-start = (bf16[128,768]{1,0:T(8,128)(2,1)}, bf16[128,768]{1,0:T(8,128)(2,1)S(1)}, u32[]{:S(2)}, u32[]{:S(2)}) collective-permute-start(bf16[128,768]{1,0:T(8,128)(2,1)} %bitcast.315), channel_id=1, source_target_pairs={{8,0},{16,8},{24,16},{0,24},{9,1},{17,9},{25,17},{1,25},{10,2},{18... | collective-permute-start | bytes 589832 | tf_op jit(solution)/shard_map/ppermute | solution.py:22
  14.8 2.6 collective-permute-start.4
  17.3 1.9 collective-permute-start.5
  26.2 1.5 collective-permute-done.4
  27.9 2.5 collective-permute-start.6
  36.0 1.5 collective-permute-start.21
  37.8 10.2 %collective-permute-done.2 = bf16[128,768]{1,0:T(8,128)(2,1)S(1)} collective-permute-done((bf16[128,768]{1,0:T(8,128)(2,1)S(1)}, bf16[128,768]{1,0:T(8,128)(2,1)S(1)}, u32[]{:S(2)}, u32[]{:S(2)}) %collective-permute-start.2) | collective-permute-done | bytes 196640 | tf_op jit(solution)/shard_map/ppermute | solution.py:22
  51.2 5.9 %collective-permute-start.14 = (bf16[24,768]{1,0:T(8,128)(2,1)S(1)}, bf16[24,768]{1,0:T(8,128)(2,1)S(1)}, u32[]{:S(2)}, u32[]{:S(2)}) collective-permute-start(bf16[24,768]{1,0:T(8,128)(2,1)S(1)} %broadcast_add_fusion), channel_id=1, source_target_pairs={{8,0},{16,8},{24,16},{0,24},{9,1},{17,9},{25,17},{1,25},{10,2},{18... | collective-permute-start | bytes 110600 | tf_op jit(solution)/shard_map/ppermute | solution.py:22
  57.1 1.8 collective-permute-start.16
  59.5 1.7 collective-permute-start.10
  61.2 4.5 %collective-permute-done.15 = bf16[24,768]{1,0:T(8,128)(2,1)S(1)} collective-permute-done((bf16[24,768]{1,0:T(8,128)(2,1)S(1)}, bf16[24,768]{1,0:T(8,128)(2,1)S(1)}, u32[]{:S(2)}, u32[]{:S(2)}) %collective-permute-start.15) | collective-permute-done | bytes 36896 | tf_op jit(solution)/shard_map/ppermute | solution.py:22
  65.7 2.5 collective-permute-start.17
  69.9 2.1 collective-permute-done.17
  72.0 1.7 collective-permute-done.18
  76.8 2.8 fusion.171
  82.9 3.0 %collective-permute-start.11 = (bf16[128,192]{0,1:T(8,128)(2,1)}, bf16[128,192]{0,1:T(8,128)(2,1)S(1)}, u32[]{:S(2)}, u32[]{:S(2)}) collective-permute-start(bf16[128,192]{0,1:T(8,128)(2,1)} %bitcast.23), channel_id=1, source_target_pairs={{8,0},{16,8},{24,16},{0,24},{9,1},{17,9},{25,17},{1,25},{10,2},{18... | collective-permute-start | bytes 147464 | tf_op jit(solution)/shard_map/ppermute | solution.py:22
  88.5 2.8 collective-permute-done.12
  91.3 1.7 collective-permute-done.13
  96.7 1.3 select_reduce_fusion.8
  99.9 28.8 %all_to_all.20 = bf16[8,80,1536]{2,1,0:T(8,128)(2,1)} all-to-all(bf16[8,80,1536]{2,1,0:T(8,128)(2,1)S(1)} %pad_maximum_fusion), channel_id=1, replica_groups=mesh['hz'=4,'yy'=2,'xx'=2,'cc'=2] {'yy','xx','cc'}, dimensions={0} | all-to-all | bytes 3932160 | tf_op jit(solution)/shard_map/all_to_all | solution.py:132
  128.7 11.1 %all-gather.4.cloned.1.call-done.w_first = bf16[768,1536]{1,0:T(8,128)(2,1)} async-done(((bf16[192,1536]{1,0:T(8,128)(2,1)}), bf16[768,1536]{1,0:T(8,128)(2,1)}) %all-gather.4.cloned.1.call-update) | async-done | bytes 2359312 | tf_op jit(solution)/shard_map/all_gather | solution.py:204
  139.7 19.0 %shard_map.195 = (bf16[640,1536]{1,0:T(8,128)(2,1)}, bf16[768,1536]{1,0:T(8,128)(2,1)}, bf16[1536,768]{1,0:T(8,128)(2,1)}) custom-call(bf16[640,1536]{1,0:T(8,128)(2,1)} %bitcast.313, bf16[768,1536]{1,0:T(8,128)(2,1)} %all-gather.4.cloned.1.call-done.w_first, bf16[1536,768]{1,0:T(8,128)(2,1)} %bitcast.350), custom_call_target="tpu_custom_call" | custom-call | flops 9059696640 | bytes 13369344 | tf_op jit(solution)/shard_map/pallas_call | solution.py:90
  158.7 4.4 %all-to-all-start.1 = ((bf16[8,80,1536]{2,1,0:T(8,128)(2,1)}), bf16[8,80,1536]{2,1,0:T(8,128)(2,1)}, u32[]{:S(2)}, u32[]{:S(2)}) async-start(bf16[8,80,1536]{2,1,0:T(8,128)(2,1)} %bitcast.312), calls=%async_computation.1 | async-start | bytes 3932160 | tf_op jit(solution)/shard_map/all_to_all | solution.py:132
  163.7 24.7 %all-to-all-done.1 = bf16[8,80,1536]{2,1,0:T(8,128)(2,1)} async-done(((bf16[8,80,1536]{2,1,0:T(8,128)(2,1)}), bf16[8,80,1536]{2,1,0:T(8,128)(2,1)}, u32[]{:S(2)}, u32[]{:S(2)}) %all-to-all-start.1) | async-done | bytes 1966112 | tf_op jit(solution)/shard_map/all_to_all | solution.py:132
  188.3 1.8 fusion.12
  190.1 1.6 fusion.15
  191.7 2.4 fusion.49
  194.4 1.6 multiply_reduce_fusion
  196.2 1.5 convolution_convert_fusion
  200.2 2.0 collective-permute-start.24
  203.8 1.4 pad_maximum_fusion.1
  206.2 2.5 collective-permute-done.23
  212.7 1.5 collective-permute-start.25
  215.9 6.1 %collective-permute-done.25 = bf16[512,384]{0,1:T(8,128)(2,1)S(1)} collective-permute-done((bf16[512,384]{0,1:T(8,128)(2,1)}, bf16[512,384]{0,1:T(8,128)(2,1)S(1)}, u32[]{:S(2)}, u32[]{:S(2)}) %collective-permute-start.25) | collective-permute-done | bytes 393248 | tf_op jit(solution)/shard_map/ppermute | solution.py:29
  225.3 1.3 fusion.7
  227.9 1.8 concatenate.173
  229.7 5.7 %all-to-all-start.2 = ((bf16[4,96,1536]{2,1,0:T(8,128)(2,1)}), bf16[4,96,1536]{2,1,0:T(8,128)(2,1)S(1)}, u32[]{:S(2)}, u32[]{:S(2)}) async-start(bf16[4,96,1536]{2,1,0:T(8,128)(2,1)} %concatenate.173), calls=%async_computation.3 | async-start | bytes 2359296 | tf_op jit(solution)/shard_map/all_to_all | solution.py:132
  235.5 1.4 convert_multiply_fusion
  237.3 2.1 fusion.172
  241.3 3.2 %collective-permute-start.28 = (bf16[128,768]{1,0:T(8,128)(2,1)}, bf16[128,768]{1,0:T(8,128)(2,1)}, u32[]{:S(2)}, u32[]{:S(2)}) collective-permute-start(bf16[128,768]{1,0:T(8,128)(2,1)} %get-tuple-element.81), channel_id=1, source_target_pairs={{8,0},{16,8},{24,16},{0,24},{9,1},{17,9},{25,17},{1,25},{10,2},{18... | collective-permute-start | bytes 589832 | tf_op jit(solution)/shard_map/ppermute | solution.py:22
  245.2 5.9 %all-to-all-done.2 = bf16[4,96,1536]{2,1,0:T(8,128)(2,1)S(1)} async-done(((bf16[4,96,1536]{2,1,0:T(8,128)(2,1)}), bf16[4,96,1536]{2,1,0:T(8,128)(2,1)S(1)}, u32[]{:S(2)}, u32[]{:S(2)}) %all-to-all-start.2) | async-done | bytes 1179680 | tf_op jit(solution)/shard_map/all_to_all | solution.py:132
  253.3 1.5 collective-permute-start.29
  257.6 4.1 %all-to-all-start.3 = ((bf16[4,24,1536]{2,1,0:T(8,128)(2,1)}), bf16[4,24,1536]{2,1,0:T(8,128)(2,1)}, u32[]{:S(2)}, u32[]{:S(2)}) async-start(bf16[4,24,1536]{2,1,0:T(8,128)(2,1)} %pad.20), calls=%async_computation.4 | async-start | bytes 589824 | tf_op jit(solution)/shard_map/all_to_all | solution.py:132
  261.7 9.1 %reduce-scatter.5.cloned.1.call-done = bf16[384,768]{1,0:T(8,128)(2,1)} async-done(((bf16[1536,768]{1,0:T(8,128)(2,1)}), bf16[384,768]{1,0:T(8,128)(2,1)}) %reduce-scatter.5.cloned.1.call-update) | async-done | bytes 589840 | tf_op jit(solution)/shard_map/reduce_scatter | solution.py:320
  270.8 2.2 bitcast_convert_fusion
  275.1 1.3 slice.322
  277.1 1.3 multiply_reduce_fusion.1
  278.5 2.1 add_bitcast_fusion
  (388 shorter events, 61.6 us)
Async XLA Ops:
  7.2 14.1 %copy-start = (f32[32,12]{0,1:T(8,128)S(1)}, f32[32,12]{0,1:T(8,128)}, u32[]{:S(2)}) copy-start(f32[32,12]{0,1:T(8,128)} %param.16) | copy-start | bytes 4612
  7.2 18.2 %copy-start.55 = (bf16[1,96,3072]{2,1,0:T(8,128)(2,1)S(1)}, bf16[1,96,3072]{2,1,0:T(8,128)(2,1)}, u32[]{:S(2)}) copy-start(bf16[1,96,3072]{2,1,0:T(8,128)(2,1)} %param.19) | copy-start | bytes 1769476
  7.2 121.5 %all-gather.6.cloned.1.call-start = ((), (), s32[]{:S(2)}) async-start(), calls=%async_computation.9 | async-start | bytes 2949120 | tf_op jit(solution)/shard_map/all_gather | solution.py:190
  7.2 30.6 %collective-permute-start = (bf16[128,768]{1,0:T(8,128)(2,1)}, bf16[128,768]{1,0:T(8,128)(2,1)S(1)}, u32[]{:S(2)}, u32[]{:S(2)}) collective-permute-start(bf16[128,768]{1,0:T(8,128)(2,1)} %bitcast.315), channel_id=1, source_target_pairs={{8,0},{16,8},{24,16},{0,24},{9,1},{17,9},{25,17},{1,25},{10,2},{18... | collective-permute-start | bytes 589832 | tf_op jit(solution)/shard_map/ppermute | solution.py:22
  12.4 25.5 %collective-permute-start.1 = (bf16[128,768]{1,0:T(8,128)(2,1)}, bf16[128,768]{1,0:T(8,128)(2,1)S(1)}, u32[]{:S(2)}, u32[]{:S(2)}) collective-permute-start(bf16[128,768]{1,0:T(8,128)(2,1)} %bitcast.316), channel_id=1, source_target_pairs={{16,0},{24,8},{0,16},{8,24},{17,1},{25,9},{1,17},{9,25},{18,2},{26... | collective-permute-start | bytes 589832 | tf_op jit(solution)/shard_map/ppermute | solution.py:22
  14.3 11.9 %collective-permute-start.3 = (bf16[24,640]{1,0:T(8,128)(2,1)S(1)}, bf16[24,640]{1,0:T(8,128)(2,1)S(1)}, u32[]{:S(2)}, u32[]{:S(2)}) collective-permute-start(bf16[24,640]{1,0:T(8,128)(2,1)S(1)} %get-tuple-element.150), channel_id=1, source_target_pairs={{8,0},{16,8},{24,16},{0,24},{9,1},{17,9},{25,17},{1,25},{10,2},{18... | collective-permute-start | bytes 92168 | tf_op jit(solution)/shard_map/ppermute | solution.py:22
  14.8 12.9 %collective-permute-start.4 = (bf16[24,640]{1,0:T(8,128)(2,1)S(1)}, bf16[24,640]{1,0:T(8,128)(2,1)S(1)}, u32[]{:S(2)}, u32[]{:S(2)}) collective-permute-start(bf16[24,640]{1,0:T(8,128)(2,1)S(1)} %get-tuple-element.151), channel_id=1, source_target_pairs={{16,0},{24,8},{0,16},{8,24},{17,1},{25,9},{1,17},{9,25},{18,2},{26... | collective-permute-start | bytes 92168 | tf_op jit(solution)/shard_map/ppermute | solution.py:22
  17.3 10.3 %collective-permute-start.5 = (bf16[24,640]{1,0:T(8,128)(2,1)S(1)}, bf16[24,640]{1,0:T(8,128)(2,1)S(1)}, u32[]{:S(2)}, u32[]{:S(2)}) collective-permute-start(bf16[24,640]{1,0:T(8,128)(2,1)S(1)} %get-tuple-element.152), channel_id=1, source_target_pairs={{24,0},{0,8},{8,16},{16,24},{25,1},{1,9},{9,17},{17,25},{26,2},{2,... | collective-permute-start | bytes 92168 | tf_op jit(solution)/shard_map/ppermute | solution.py:22
  19.3 120.4 %all-gather.4.cloned.1.call-start = ((), (), s32[]{:S(2)}) async-start(), calls=%async_computation.6 | async-start | bytes 2949120 | tf_op jit(solution)/shard_map/all_gather | solution.py:204
  27.9 7.2 %collective-permute-start.6 = (bf16[4,24,640]{2,1,0:T(8,128)(2,1)S(1)}, bf16[4,24,640]{2,1,0:T(8,128)(2,1)S(1)}, u32[]{:S(2)}, u32[]{:S(2)}) collective-permute-start(bf16[4,24,640]{2,1,0:T(8,128)(2,1)S(1)} %pad_maximum_fusion.15), channel_id=1, source_target_pairs={{6,0},{4,2},{2,4},{0,6},{7,1},{5,3},{3,5},{1,7},{14,8},{12,10},{10... | collective-permute-start | bytes 368648 | tf_op jit(solution)/shard_map/ppermute | solution.py:29
  30.4 5.6 %collective-permute-start.7 = (bf16[4,24,640]{2,1,0:T(8,128)(2,1)S(1)}, bf16[4,24,640]{2,1,0:T(8,128)(2,1)S(1)}, u32[]{:S(2)}, u32[]{:S(2)}) collective-permute-start(bf16[4,24,640]{2,1,0:T(8,128)(2,1)S(1)} %pad_maximum_fusion.15), channel_id=1, source_target_pairs={{4,0},{6,2},{0,4},{2,6},{5,1},{7,3},{1,5},{3,7},{12,8},{14,10},{8,... | collective-permute-start | bytes 368648 | tf_op jit(solution)/shard_map/ppermute | solution.py:29
  30.9 6.6 %collective-permute-start.8 = (bf16[4,24,640]{2,1,0:T(8,128)(2,1)S(1)}, bf16[4,24,640]{2,1,0:T(8,128)(2,1)S(1)}, u32[]{:S(2)}, u32[]{:S(2)}) collective-permute-start(bf16[4,24,640]{2,1,0:T(8,128)(2,1)S(1)} %pad_maximum_fusion.15), channel_id=1, source_target_pairs={{2,0},{0,2},{6,4},{4,6},{3,1},{1,3},{7,5},{5,7},{10,8},{8,10},{14,... | collective-permute-start | bytes 368648 | tf_op jit(solution)/shard_map/ppermute | solution.py:29
  35.1 13.0 %collective-permute-start.2 = (bf16[128,768]{1,0:T(8,128)(2,1)S(1)}, bf16[128,768]{1,0:T(8,128)(2,1)S(1)}, u32[]{:S(2)}, u32[]{:S(2)}) collective-permute-start(bf16[128,768]{1,0:T(8,128)(2,1)S(1)} %bitcast.317), channel_id=1, source_target_pairs={{24,0},{0,8},{8,16},{16,24},{25,1},{1,9},{9,17},{17,25},{26,2},{2,... | collective-permute-start | bytes 589832 | tf_op jit(solution)/shard_map/ppermute | solution.py:22
  36.0 12.3 %collective-permute-start.21 = (bf16[96,1536]{1,0:T(8,128)(2,1)S(1)}, bf16[96,1536]{1,0:T(8,128)(2,1)S(1)}, u32[]{:S(2)}, u32[]{:S(2)}) collective-permute-start(bf16[96,1536]{1,0:T(8,128)(2,1)S(1)} %fusion.60), channel_id=1, source_target_pairs={{4,0},{0,4},{5,1},{1,5},{6,2},{2,6},{7,3},{3,7},{12,8},{8,12},{13,... | collective-permute-start | bytes 884744 | tf_op jit(solution)/shard_map/ppermute | solution.py:29
  37.7 11.6 %collective-permute-start.9 = (bf16[4,4,24,640]{3,2,1,0:T(8,128)(2,1)S(1)}, bf16[4,4,24,640]{3,2,1,0:T(8,128)(2,1)S(1)}, u32[]{:S(2)}, u32[]{:S(2)}) collective-permute-start(bf16[4,4,24,640]{3,2,1,0:T(8,128)(2,1)S(1)} %pad_maximum_fusion.9), channel_id=1, source_target_pairs={{1,0},{0,1},{3,2},{2,3},{5,4},{4,5},{7,6},{6,7},{9,8},{8,9},{11,10... | collective-permute-start | bytes 1474568 | tf_op jit(solution)/shard_map/ppermute | solution.py:29
  37.8 31.5 %copy-start.42 = (bf16[128,768]{1,0:T(8,128)(2,1)}, bf16[128,768]{1,0:T(8,128)(2,1)S(1)}, u32[]{:S(2)}) copy-start(bf16[128,768]{1,0:T(8,128)(2,1)S(1)} %collective-permute-done) | copy-start | bytes 589828
  37.8 31.5 %copy-start.45 = (bf16[128,768]{1,0:T(8,128)(2,1)}, bf16[128,768]{1,0:T(8,128)(2,1)S(1)}, u32[]{:S(2)}) copy-start(bf16[128,768]{1,0:T(8,128)(2,1)S(1)} %collective-permute-done.1) | copy-start | bytes 589828
  48.1 21.2 %copy-start.48 = (bf16[128,768]{1,0:T(8,128)(2,1)}, bf16[128,768]{1,0:T(8,128)(2,1)S(1)}, u32[]{:S(2)}) copy-start(bf16[128,768]{1,0:T(8,128)(2,1)S(1)} %collective-permute-done.2) | copy-start | bytes 589828
  48.3 21.0 %copy-start.79 = (f32[512]{0:T(512)}, f32[512]{0:T(512)S(1)}, u32[]{:S(2)}) copy-start(f32[512]{0:T(512)S(1)} %add_rsqrt_fusion) | copy-start | bytes 6148
  49.6 19.7 %copy-start.6 = (bf16[4,4,2,24,640]{4,3,2,1,0:T(8,128)(2,1)}, bf16[4,4,2,24,640]{4,3,2,1,0:T(8,128)(2,1)S(1)}, u32[]{:S(2)}) copy-start(bf16[4,4,2,24,640]{4,3,2,1,0:T(8,128)(2,1)S(1)} %copy.79) | copy-start | bytes 2949124
  51.2 10.0 %collective-permute-start.14 = (bf16[24,768]{1,0:T(8,128)(2,1)S(1)}, bf16[24,768]{1,0:T(8,128)(2,1)S(1)}, u32[]{:S(2)}, u32[]{:S(2)}) collective-permute-start(bf16[24,768]{1,0:T(8,128)(2,1)S(1)} %broadcast_add_fusion), channel_id=1, source_target_pairs={{8,0},{16,8},{24,16},{0,24},{9,1},{17,9},{25,17},{1,25},{10,2},{18... | collective-permute-start | bytes 110600 | tf_op jit(solution)/shard_map/ppermute | solution.py:22
  57.1 8.6 %collective-permute-start.15 = (bf16[24,768]{1,0:T(8,128)(2,1)S(1)}, bf16[24,768]{1,0:T(8,128)(2,1)S(1)}, u32[]{:S(2)}, u32[]{:S(2)}) collective-permute-start(bf16[24,768]{1,0:T(8,128)(2,1)S(1)} %broadcast_add_fusion), channel_id=1, source_target_pairs={{16,0},{24,8},{0,16},{8,24},{17,1},{25,9},{1,17},{9,25},{18,2},{26... | collective-permute-start | bytes 110600 | tf_op jit(solution)/shard_map/ppermute | solution.py:22
  57.1 8.6 %collective-permute-start.16 = (bf16[24,768]{1,0:T(8,128)(2,1)S(1)}, bf16[24,768]{1,0:T(8,128)(2,1)S(1)}, u32[]{:S(2)}, u32[]{:S(2)}) collective-permute-start(bf16[24,768]{1,0:T(8,128)(2,1)S(1)} %broadcast_add_fusion), channel_id=1, source_target_pairs={{24,0},{0,8},{8,16},{16,24},{25,1},{1,9},{9,17},{17,25},{26,2},{2,... | collective-permute-start | bytes 110600 | tf_op jit(solution)/shard_map/ppermute | solution.py:22
  59.5 15.5 %collective-permute-start.10 = (bf16[512,384]{1,0:T(8,128)(2,1)S(1)}, bf16[512,384]{1,0:T(8,128)(2,1)S(1)}, u32[]{:S(2)}, u32[]{:S(2)}) collective-permute-start(bf16[512,384]{1,0:T(8,128)(2,1)S(1)} %convolution_convert_fusion.4), channel_id=1, source_target_pairs={{4,0},{0,4},{5,1},{1,5},{6,2},{2,6},{7,3},{3,7},{12,8},{8,12},{13,... | collective-permute-start | bytes 1179656 | tf_op jit(solution)/shard_map/ppermute | solution.py:29
  65.7 6.2 %collective-permute-start.17 = (bf16[4,24,768]{2,1,0:T(8,128)(2,1)S(1)}, bf16[4,24,768]{2,1,0:T(8,128)(2,1)S(1)}, u32[]{:S(2)}, u32[]{:S(2)}) collective-permute-start(bf16[4,24,768]{2,1,0:T(8,128)(2,1)S(1)} %pad_maximum_fusion.14), channel_id=1, source_target_pairs={{6,0},{4,2},{2,4},{0,6},{7,1},{5,3},{3,5},{1,7},{14,8},{12,10},{10... | collective-permute-start | bytes 442376 | tf_op jit(solution)/shard_map/ppermute | solution.py:29
  68.2 5.5 %collective-permute-start.18 = (bf16[4,24,768]{2,1,0:T(8,128)(2,1)S(1)}, bf16[4,24,768]{2,1,0:T(8,128)(2,1)S(1)}, u32[]{:S(2)}, u32[]{:S(2)}) collective-permute-start(bf16[4,24,768]{2,1,0:T(8,128)(2,1)S(1)} %pad_maximum_fusion.14), channel_id=1, source_target_pairs={{4,0},{6,2},{0,4},{2,6},{5,1},{7,3},{1,5},{3,7},{12,8},{14,10},{8,... | collective-permute-start | bytes 442376 | tf_op jit(solution)/shard_map/ppermute | solution.py:29
  68.8 5.1 %collective-permute-start.19 = (bf16[4,24,768]{2,1,0:T(8,128)(2,1)S(1)}, bf16[4,24,768]{2,1,0:T(8,128)(2,1)S(1)}, u32[]{:S(2)}, u32[]{:S(2)}) collective-permute-start(bf16[4,24,768]{2,1,0:T(8,128)(2,1)S(1)} %pad_maximum_fusion.14), channel_id=1, source_target_pairs={{2,0},{0,2},{6,4},{4,6},{3,1},{1,3},{7,5},{5,7},{10,8},{8,10},{14,... | collective-permute-start | bytes 442376 | tf_op jit(solution)/shard_map/ppermute | solution.py:29
  75.0 18.9 %collective-permute-start.20 = (bf16[4,4,24,768]{3,2,0,1:T(8,128)(2,1)}, bf16[4,4,24,768]{3,2,0,1:T(8,128)(2,1)}, u32[]{:S(2)}, u32[]{:S(2)}) collective-permute-start(bf16[4,4,24,768]{3,2,0,1:T(8,128)(2,1)} %pad_maximum_fusion.5), channel_id=1, source_target_pairs={{1,0},{0,1},{3,2},{2,3},{5,4},{4,5},{7,6},{6,7},{9,8},{8,9},{11,10... | collective-permute-start | bytes 1769480 | tf_op jit(solution)/shard_map/ppermute | solution.py:29
  82.9 5.6 %collective-permute-start.11 = (bf16[128,192]{0,1:T(8,128)(2,1)}, bf16[128,192]{0,1:T(8,128)(2,1)S(1)}, u32[]{:S(2)}, u32[]{:S(2)}) collective-permute-start(bf16[128,192]{0,1:T(8,128)(2,1)} %bitcast.23), channel_id=1, source_target_pairs={{8,0},{16,8},{24,16},{0,24},{9,1},{17,9},{25,17},{1,25},{10,2},{18... | collective-permute-start | bytes 147464 | tf_op jit(solution)/shard_map/ppermute | solution.py:22
  85.9 5.4 %collective-permute-start.12 = (bf16[128,192]{0,1:T(8,128)(2,1)}, bf16[128,192]{0,1:T(8,128)(2,1)}, u32[]{:S(2)}, u32[]{:S(2)}) collective-permute-start(bf16[128,192]{0,1:T(8,128)(2,1)} %bitcast.24), channel_id=1, source_target_pairs={{16,0},{24,8},{0,16},{8,24},{17,1},{25,9},{1,17},{9,25},{18,2},{26... | collective-permute-start | bytes 147464 | tf_op jit(solution)/shard_map/ppermute | solution.py:22
  86.8 6.2 %collective-permute-start.13 = (bf16[128,192]{0,1:T(8,128)(2,1)}, bf16[128,192]{0,1:T(8,128)(2,1)}, u32[]{:S(2)}, u32[]{:S(2)}) collective-permute-start(bf16[128,192]{0,1:T(8,128)(2,1)} %bitcast.25), channel_id=1, source_target_pairs={{24,0},{0,8},{8,16},{16,24},{25,1},{1,9},{9,17},{17,25},{26,2},{2,... | collective-permute-start | bytes 147464 | tf_op jit(solution)/shard_map/ppermute | solution.py:22
  88.2 163.6 %reduce-scatter.3.cloned.1.call-start = ((), (), s32[]{:S(2)}) async-start(), calls=%async_computation.7 | async-start | bytes 2949120 | tf_op jit(solution)/shard_map/reduce_scatter | solution.py:319
  158.7 29.6 %all-to-all-start.1 = ((bf16[8,80,1536]{2,1,0:T(8,128)(2,1)}), bf16[8,80,1536]{2,1,0:T(8,128)(2,1)}, u32[]{:S(2)}, u32[]{:S(2)}) async-start(bf16[8,80,1536]{2,1,0:T(8,128)(2,1)} %bitcast.312), calls=%async_computation.1 | async-start | bytes 3932160 | tf_op jit(solution)/shard_map/all_to_all | solution.py:132
  163.1 107.7 %reduce-scatter.5.cloned.1.call-start = ((), (), s32[]{:S(2)}) async-start(), calls=%async_computation.8 | async-start | bytes 2949120 | tf_op jit(solution)/shard_map/reduce_scatter | solution.py:320
  198.8 7.4 %collective-permute-start.22 = (bf16[128,192]{0,1:T(8,128)(2,1)}, bf16[128,192]{0,1:T(8,128)(2,1)S(1)}, u32[]{:S(2)}, u32[]{:S(2)}) collective-permute-start(bf16[128,192]{0,1:T(8,128)(2,1)} %get-tuple-element.119), channel_id=1, source_target_pairs={{8,0},{16,8},{24,16},{0,24},{9,1},{17,9},{25,17},{1,25},{10,2},{18... | collective-permute-start | bytes 147464 | tf_op jit(solution)/shard_map/ppermute | solution.py:22
  199.7 9.0 %collective-permute-start.23 = (bf16[128,192]{0,1:T(8,128)(2,1)}, bf16[128,192]{0,1:T(8,128)(2,1)S(1)}, u32[]{:S(2)}, u32[]{:S(2)}) collective-permute-start(bf16[128,192]{0,1:T(8,128)(2,1)} %get-tuple-element.118), channel_id=1, source_target_pairs={{16,0},{24,8},{0,16},{8,24},{17,1},{25,9},{1,17},{9,25},{18,2},{26... | collective-permute-start | bytes 147464 | tf_op jit(solution)/shard_map/ppermute | solution.py:22
  200.2 8.5 %collective-permute-start.24 = (bf16[128,192]{0,1:T(8,128)(2,1)}, bf16[128,192]{0,1:T(8,128)(2,1)S(1)}, u32[]{:S(2)}, u32[]{:S(2)}) collective-permute-start(bf16[128,192]{0,1:T(8,128)(2,1)} %get-tuple-element.117), channel_id=1, source_target_pairs={{24,0},{0,8},{8,16},{16,24},{25,1},{1,9},{9,17},{17,25},{26,2},{2,... | collective-permute-start | bytes 147464 | tf_op jit(solution)/shard_map/ppermute | solution.py:22
  206.2 19.1 %collective-permute-start.30 = (bf16[4,96,896]{2,1,0:T(8,128)(2,1)}, bf16[4,96,896]{2,1,0:T(8,128)(2,1)}, u32[]{:S(2)}, u32[]{:S(2)}) collective-permute-start(bf16[4,96,896]{2,1,0:T(8,128)(2,1)} %dynamic-slice_bitcast_fusion), channel_id=1, source_target_pairs={{1,0},{0,1},{3,2},{2,3},{5,4},{4,5},{7,6},{6,7},{9,8},{8,9},{11,10... | collective-permute-start | bytes 2064392 | tf_op jit(solution)/shard_map/ppermute | solution.py:29
  212.7 9.3 %collective-permute-start.25 = (bf16[512,384]{0,1:T(8,128)(2,1)}, bf16[512,384]{0,1:T(8,128)(2,1)S(1)}, u32[]{:S(2)}, u32[]{:S(2)}) collective-permute-start(bf16[512,384]{0,1:T(8,128)(2,1)} %fusion.22), channel_id=1, source_target_pairs={{4,0},{0,4},{5,1},{1,5},{6,2},{2,6},{7,3},{3,7},{12,8},{8,12},{13,... | collective-permute-start | bytes 1179656 | tf_op jit(solution)/shard_map/ppermute | solution.py:29
  215.8 8.8 %collective-permute-start.32 = (f32[3,32]{1,0:T(4,128)S(1)}, f32[3,32]{1,0:T(4,128)}, u32[]{:S(2)}, u32[]{:S(2)}) collective-permute-start(f32[3,32]{1,0:T(4,128)S(1)} %select_reduce_fusion.1), channel_id=1, source_target_pairs={{1,0},{0,1},{3,2},{2,3},{5,4},{4,5},{7,6},{6,7},{9,8},{8,9},{11,10... | collective-permute-start | bytes 1160 | tf_op jit(solution)/shard_map/ppermute | solution.py:29
  224.5 2.2 collective-permute-start.31
  229.7 21.4 %all-to-all-start.2 = ((bf16[4,96,1536]{2,1,0:T(8,128)(2,1)}), bf16[4,96,1536]{2,1,0:T(8,128)(2,1)S(1)}, u32[]{:S(2)}, u32[]{:S(2)}) async-start(bf16[4,96,1536]{2,1,0:T(8,128)(2,1)} %concatenate.173), calls=%async_computation.3 | async-start | bytes 2359296 | tf_op jit(solution)/shard_map/all_to_all | solution.py:132
  240.7 36.4 %collective-permute-start.26 = (bf16[128,768]{1,0:T(8,128)(2,1)}, bf16[128,768]{1,0:T(8,128)(2,1)}, u32[]{:S(2)}, u32[]{:S(2)}) collective-permute-start(bf16[128,768]{1,0:T(8,128)(2,1)} %get-tuple-element.80), channel_id=1, source_target_pairs={{24,0},{0,8},{8,16},{16,24},{25,1},{1,9},{9,17},{17,25},{26,2},{2,... | collective-permute-start | bytes 589832 | tf_op jit(solution)/shard_map/ppermute | solution.py:22
  240.7 36.4 %collective-permute-start.27 = (bf16[128,768]{1,0:T(8,128)(2,1)}, bf16[128,768]{1,0:T(8,128)(2,1)}, u32[]{:S(2)}, u32[]{:S(2)}) collective-permute-start(bf16[128,768]{1,0:T(8,128)(2,1)} %get-tuple-element.82), channel_id=1, source_target_pairs={{16,0},{24,8},{0,16},{8,24},{17,1},{25,9},{1,17},{9,25},{18,2},{26... | collective-permute-start | bytes 589832 | tf_op jit(solution)/shard_map/ppermute | solution.py:22
  241.3 35.8 %collective-permute-start.28 = (bf16[128,768]{1,0:T(8,128)(2,1)}, bf16[128,768]{1,0:T(8,128)(2,1)}, u32[]{:S(2)}, u32[]{:S(2)}) collective-permute-start(bf16[128,768]{1,0:T(8,128)(2,1)} %get-tuple-element.81), channel_id=1, source_target_pairs={{8,0},{16,8},{24,16},{0,24},{9,1},{17,9},{25,17},{1,25},{10,2},{18... | collective-permute-start | bytes 589832 | tf_op jit(solution)/shard_map/ppermute | solution.py:22
  253.3 19.6 %collective-permute-start.29 = (bf16[96,1536]{1,0:T(8,128)(2,1)S(1)}, bf16[96,1536]{1,0:T(8,128)(2,1)S(1)}, u32[]{:S(2)}, u32[]{:S(2)}) collective-permute-start(bf16[96,1536]{1,0:T(8,128)(2,1)S(1)} %dynamic-slice_bitcast_fusion.2), channel_id=1, source_target_pairs={{4,0},{0,4},{5,1},{1,5},{6,2},{2,6},{7,3},{3,7},{12,8},{8,12},{13,... | collective-permute-start | bytes 884744 | tf_op jit(solution)/shard_map/ppermute | solution.py:29
  256.9 16.8 %copy-start.56 = (bf16[192,1536]{1,0:T(8,128)(2,1)S(1)}, bf16[192,1536]{1,0:T(8,128)(2,1)}, u32[]{:S(2)}) copy-start(bf16[192,1536]{1,0:T(8,128)(2,1)} %reduce-scatter.3.cloned.1.call-done) | copy-start | bytes 1769476
  257.6 23.0 %all-to-all-start.3 = ((bf16[4,24,1536]{2,1,0:T(8,128)(2,1)}), bf16[4,24,1536]{2,1,0:T(8,128)(2,1)}, u32[]{:S(2)}, u32[]{:S(2)}) async-start(bf16[4,24,1536]{2,1,0:T(8,128)(2,1)} %pad.20), calls=%async_computation.4 | async-start | bytes 589824 | tf_op jit(solution)/shard_map/all_to_all | solution.py:132
  (79 other events, 257.6 us)
Sparse Core Ops, SparseCore 0:
  19.4 57.1 all-gather.5
  88.3 51.3 all-gather.3
  158.8 49.5 reduce-scatter.2
  210.6 60.2 reduce-scatter.4

commit v4 on v3

--- a/solution.py
+++ b/solution.py
@@ -182,10 +182,11 @@
             lax.dynamic_slice(query_key_value_weight, (0, part * D + group * gw), (shard, gw))
             for part in (1, 2, 0)
         ]
-        return jnp.concatenate(columns + [small], axis=1)
+        return jnp.concatenate(columns + [small, attention_output_weight], axis=1)
 
     pieces = [qkv_piece(z)] + [shift(qkv_piece((z - d) % Z), "hz", d) for d in range(1, Z)]
-    w_all = layer_gather(jnp.stack(from_cyclic(pieces, z)))
+    pieces_in_line = jnp.stack(from_cyclic(pieces, z))
+    w_all = layer_gather(pieces_in_line[:, :, : gw * 3 + small_width])
 
     w_second = lax.all_gather(w_out[0], "hz", axis=0, tiled=True)
     part_ff = FF // N
@@ -198,14 +199,10 @@
         return jnp.concatenate(columns, axis=1)
 
     in_rows = [in_piece(y)] + [
-        swap(after(in_piece(y ^ k), *pieces[1:]), ("yy",), k) for k in range(1, Y)
+        swap(after(in_piece(y ^ k), pieces[1]), ("yy",), k) for k in range(1, Y)
     ]
-    in_rows = jnp.concatenate(from_xor(in_rows, y), axis=0)
+    in_rows = lax.optimization_barrier(jnp.concatenate(from_xor(in_rows, y), axis=0))
     w_first = lax.all_gather(in_rows, "hz", axis=0, tiled=True)
-
-    own_attn_w = after(attention_output_weight, w_all)
-    attn_w_pieces = [own_attn_w] + [shift(own_attn_w, "hz", d) for d in range(1, Z)]
-    w_attn_out = layer_gather(jnp.stack(from_cyclic(attn_w_pieces, z)))
 
     gain_first = w_all[:, 3 * gw].astype(WIDE)
     gain_second = w_all[:, 3 * gw + 1].astype(WIDE)
@@ -250,12 +247,15 @@
     normed_one = (hat_one * gain_first).astype(LOW)
     w_kv, w_q = w_all[:, : 2 * gw], w_all[:, 2 * gw : 3 * gw]
     kv = dot(normed_one, w_kv, ((1,), (0,))).astype(LOW)
+    attn_pieces = after(pieces_in_line[:, :, 3 * gw + small_width :], kv)
+    w_attn_out = layer_gather(attn_pieces)
     kv_all = jnp.concatenate([kv] + [swap(kv, ("yy",), k) for k in range(1, Y)], axis=0)
     q = dot(normed_one, w_q, ((1,), (0,))).astype(LOW)
 
     def by_head(rows):
         return rows.reshape(rows.shape[0], hg, hd).transpose(1, 0, 2)
 
+    bias_rows = after(bias_rows, in_rows)
     q_heads = by_head(q) * jnp.asarray(hd**-0.5, LOW)
     k_heads, v_heads = by_head(kv_all[:, :gw]), by_head(kv_all[:, gw:])
     q_wide = jnp.concatenate([q_heads, bias_rows], axis=-1)
@@ -312,7 +312,7 @@
     grad_rows = dot(route_map, grad_picked, ((0,), (0,)))
     both = exchange(jnp.concatenate([rows, grad_rows], axis=1).astype(LOW))
 
-    block = part_ff if part_ff % 128 == 0 else FF // Y
+    block = 512 if (FF // Y) % 512 == 0 else FF // Y
     results, grad_first, grad_second = expert(both, w_first, w_second, block)
     back = exchange(results)
     returned, coming = back[:, :D], back[:, D:]

time: 296 us -> 292 us (0.986)
  Pallas kernels: 19 us -> 16 us
    ppermute x15, waiting for transfers between devices: 10.2 us -> 13.5 us  [swap(): return lax.ppermute(x, axes, [(j ^ k, j) for j in range(n)])]
    pallas_call x1, Pallas kernels: 19 us -> 16 us  [expert(): pl.pallas_call(expert_kernel, grid=(units // block,), out_shape=(jax.Shap...]
    ppermute x18 -> x15, starting transfers between devices: 30.4 us -> 29.4 us  [shift(): return lax.ppermute(x, axis, [((j + d) % n, j) for j in range(n)])]
    ppermute x18 -> x15, waiting for transfers between devices: 23.3 us -> 22.4 us  [shift(): return lax.ppermute(x, axis, [((j + d) % n, j) for j in range(n)])]
  transfers between devices with their start and end apart: 40 -> 37, of which waited for: 16 -> 16; matrix products, arithmetic and copies ran while one was open for 25% -> 25% of each run, Pallas kernels for 0% -> 0%
where the time goes in v4:
time: 292 us; the launch traced here: 289 us
  waiting for transfers between devices  87.1 us (30%)
  starting transfers between devices  56.2 us (19%)
  other arithmetic  31.4 us (11%)
  blocking collectives  28.8 us (10%)
  local copies, waits for them, and re-layouts  26.9 us (9%)
  matrix products  22 us (8%)
  between operations  20.3 us (7%)
  Pallas kernels  16 us (5%)
    all_to_all x3, waiting for transfers between devices, every_block(): return lax.all_to_all(x, axes, split_axis=0, concat_axis=0, tiled=True)  30.7 us
    ppermute x15, starting transfers between devices, shift(): return lax.ppermute(x, axis, [((j + d) % n, j) for j in range(n)])  29.4 us
    all_to_all x1, blocking collectives, every_block(): return lax.all_to_all(x, axes, split_axis=0, concat_axis=0, tiled=True)  28.8 us
    ppermute x15, waiting for transfers between devices, shift(): return lax.ppermute(x, axis, [((j + d) % n, j) for j in range(n)])  22.4 us
    pallas_call x1, Pallas kernels, expert(): pl.pallas_call(expert_kernel, grid=(units // block,), out_shape=(jax.Shap...  16 us
    all_to_all x3, starting transfers between devices, every_block(): return lax.all_to_all(x, axes, split_axis=0, concat_axis=0, tiled=True)  14.2 us
    dot_general x13, matrix products, dot(): lax.dot_general(left, right, (contract, ((), ())), preferred_element_type...  14.1 us
    ppermute x15, waiting for transfers between devices, swap(): return lax.ppermute(x, axes, [(j ^ k, j) for j in range(n)])  13.5 us
  transfers between devices with their start and end apart: 37, of which 16 were waited for; matrix products, arithmetic and copies ran while one was open for 25% of the time, Pallas kernels for 0%

profile of v4, /device:TPU:0, one launch (start us, length us, event | category | flops | bytes accessed | tf_op | source)
XLA Modules:
  0.0 288.8 jit_solution(1500085663791521576)
XLA Ops:
  7.3 5.1 %collective-permute-start = (bf16[128,768]{1,0:T(8,128)(2,1)}, bf16[128,768]{1,0:T(8,128)(2,1)S(1)}, u32[]{:S(2)}, u32[]{:S(2)}) collective-permute-start(bf16[128,768]{1,0:T(8,128)(2,1)} %bitcast.296), channel_id=1, source_target_pairs={{8,0},{16,8},{24,16},{0,24},{9,1},{17,9},{25,17},{1,25},{10,2},{18... | collective-permute-start | bytes 589832 | tf_op jit(solution)/shard_map/ppermute | solution.py:22
  16.5 1.6 collective-permute-start.5
  19.0 3.0 %collective-permute-start.4 = (bf16[24,1408]{1,0:T(8,128)(2,1)S(1)}, bf16[24,1408]{1,0:T(8,128)(2,1)S(1)}, u32[]{:S(2)}, u32[]{:S(2)}) collective-permute-start(bf16[24,1408]{1,0:T(8,128)(2,1)S(1)} %concatenate.143), channel_id=1, source_target_pairs={{16,0},{24,8},{0,16},{8,24},{17,1},{25,9},{1,17},{9,25},{18,2},{26... | collective-permute-start | bytes 202760 | tf_op jit(solution)/shard_map/ppermute | solution.py:22
  25.5 5.3 %collective-permute-done.4 = bf16[24,1408]{1,0:T(8,128)(2,1)S(1)} collective-permute-done((bf16[24,1408]{1,0:T(8,128)(2,1)S(1)}, bf16[24,1408]{1,0:T(8,128)(2,1)S(1)}, u32[]{:S(2)}, u32[]{:S(2)}) %collective-permute-start.4) | collective-permute-done | bytes 67616 | tf_op jit(solution)/shard_map/ppermute | solution.py:22
  30.9 2.5 collective-permute-start.6
  35.7 2.1 collective-permute-done.6
  37.8 5.0 %collective-permute-start.2 = (bf16[128,768]{1,0:T(8,128)(2,1)S(1)}, bf16[128,768]{1,0:T(8,128)(2,1)S(1)}, u32[]{:S(2)}, u32[]{:S(2)}) collective-permute-start(bf16[128,768]{1,0:T(8,128)(2,1)S(1)} %bitcast.298), channel_id=1, source_target_pairs={{24,0},{0,8},{8,16},{16,24},{25,1},{1,9},{9,17},{17,25},{26,2},{2,... | collective-permute-start | bytes 589832 | tf_op jit(solution)/shard_map/ppermute | solution.py:22
  44.8 8.9 %collective-permute-done.2 = bf16[128,768]{1,0:T(8,128)(2,1)S(1)} collective-permute-done((bf16[128,768]{1,0:T(8,128)(2,1)S(1)}, bf16[128,768]{1,0:T(8,128)(2,1)S(1)}, u32[]{:S(2)}, u32[]{:S(2)}) %collective-permute-start.2) | collective-permute-done | bytes 196640 | tf_op jit(solution)/shard_map/ppermute | solution.py:22
  56.1 1.2 select_bitcast_fusion.3
  58.4 1.3 collective-permute-start.10
  60.9 1.5 collective-permute-start.15
  62.4 1.6 collective-permute-start.16
  65.0 2.1 collective-permute-done.15
  67.1 3.2 %collective-permute-done.16 = bf16[4,24,768]{2,1,0:T(8,128)(2,1)S(1)} collective-permute-done((bf16[4,24,768]{2,1,0:T(8,128)(2,1)S(1)}, bf16[4,24,768]{2,1,0:T(8,128)(2,1)S(1)}, u32[]{:S(2)}, u32[]{:S(2)}) %collective-permute-start.16) | collective-permute-done | bytes 147488 | tf_op jit(solution)/shard_map/ppermute | solution.py:29
  73.2 2.8 fusion.165
  79.4 6.5 %collective-permute-start.12 = (bf16[128,192]{0,1:T(8,128)(2,1)}, bf16[128,192]{0,1:T(8,128)(2,1)S(1)}, u32[]{:S(2)}, u32[]{:S(2)}) collective-permute-start(bf16[128,192]{0,1:T(8,128)(2,1)} %bitcast.33), channel_id=1, source_target_pairs={{8,0},{16,8},{24,16},{0,24},{9,1},{17,9},{25,17},{1,25},{10,2},{18... | collective-permute-start | bytes 147464 | tf_op jit(solution)/shard_map/ppermute | solution.py:22
  88.3 3.9 %collective-permute-done.13 = bf16[128,192]{0,1:T(8,128)(2,1)} collective-permute-done((bf16[128,192]{0,1:T(8,128)(2,1)}, bf16[128,192]{0,1:T(8,128)(2,1)}, u32[]{:S(2)}, u32[]{:S(2)}) %collective-permute-start.13) | collective-permute-done | bytes 49184 | tf_op jit(solution)/shard_map/ppermute | solution.py:22
  93.1 1.3 select_bitcast_fusion.1
  96.1 1.3 select_reduce_fusion.8
  99.3 28.8 %all_to_all.20 = bf16[8,80,1536]{2,1,0:T(8,128)(2,1)} all-to-all(bf16[8,80,1536]{2,1,0:T(8,128)(2,1)S(1)} %pad_maximum_fusion), channel_id=1, replica_groups=mesh['hz'=4,'yy'=2,'xx'=2,'cc'=2] {'yy','xx','cc'}, dimensions={0} | all-to-all | bytes 3932160 | tf_op jit(solution)/shard_map/all_to_all | solution.py:132
  128.1 10.8 %all-gather.4.cloned.1.call-done.w_first = bf16[768,1536]{1,0:T(8,128)(2,1)} async-done(((bf16[192,1536]{1,0:T(8,128)(2,1)}), bf16[768,1536]{1,0:T(8,128)(2,1)}) %all-gather.4.cloned.1.call-update) | async-done | bytes 2359312 | tf_op jit(solution)/shard_map/all_gather | solution.py:205
  138.9 16.0 %shard_map.195 = (bf16[640,1536]{1,0:T(8,128)(2,1)}, bf16[768,1536]{1,0:T(8,128)(2,1)}, bf16[1536,768]{1,0:T(8,128)(2,1)}) custom-call(bf16[640,1536]{1,0:T(8,128)(2,1)} %bitcast.294, bf16[768,1536]{1,0:T(8,128)(2,1)} %all-gather.4.cloned.1.call-done.w_first, bf16[1536,768]{1,0:T(8,128)(2,1)} %bitcast.331), custom_call_target="tpu_custom_call" | custom-call | flops 9059696640 | bytes 13369344 | tf_op jit(solution)/shard_map/pallas_call | solution.py:90
  154.9 4.4 %all-to-all-start.1 = ((bf16[8,80,1536]{2,1,0:T(8,128)(2,1)}), bf16[8,80,1536]{2,1,0:T(8,128)(2,1)}, u32[]{:S(2)}, u32[]{:S(2)}) async-start(bf16[8,80,1536]{2,1,0:T(8,128)(2,1)} %bitcast.293), calls=%async_computation.1 | async-start | bytes 3932160 | tf_op jit(solution)/shard_map/all_to_all | solution.py:132
  159.9 24.7 %all-to-all-done.1 = bf16[8,80,1536]{2,1,0:T(8,128)(2,1)} async-done(((bf16[8,80,1536]{2,1,0:T(8,128)(2,1)}), bf16[8,80,1536]{2,1,0:T(8,128)(2,1)}, u32[]{:S(2)}, u32[]{:S(2)}) %all-to-all-start.1) | async-done | bytes 1966112 | tf_op jit(solution)/shard_map/all_to_all | solution.py:132
  184.5 1.8 fusion.12
  186.3 1.6 fusion.15
  187.9 2.4 fusion.49
  190.6 1.6 multiply_reduce_fusion
  192.4 1.5 convolution_convert_fusion
  196.4 1.9 collective-permute-start.21
  199.9 1.4 pad_maximum_fusion.1
  202.4 2.5 collective-permute-done.20
  208.8 1.5 collective-permute-start.22
  212.0 6.0 %collective-permute-done.22 = bf16[512,384]{0,1:T(8,128)(2,1)S(1)} collective-permute-done((bf16[512,384]{0,1:T(8,128)(2,1)}, bf16[512,384]{0,1:T(8,128)(2,1)S(1)}, u32[]{:S(2)}, u32[]{:S(2)}) %collective-permute-start.22) | collective-permute-done | bytes 393248 | tf_op jit(solution)/shard_map/ppermute | solution.py:29
  221.5 1.3 fusion.7
  224.0 1.8 concatenate.173
  225.8 5.8 %all-to-all-start.2 = ((bf16[4,96,1536]{2,1,0:T(8,128)(2,1)}), bf16[4,96,1536]{2,1,0:T(8,128)(2,1)S(1)}, u32[]{:S(2)}, u32[]{:S(2)}) async-start(bf16[4,96,1536]{2,1,0:T(8,128)(2,1)} %concatenate.173), calls=%async_computation.3 | async-start | bytes 2359296 | tf_op jit(solution)/shard_map/all_to_all | solution.py:132
  231.6 1.4 convert_multiply_fusion
  233.4 2.1 fusion.166
  237.5 3.1 %collective-permute-start.25 = (bf16[128,768]{1,0:T(8,128)(2,1)}, bf16[128,768]{1,0:T(8,128)(2,1)}, u32[]{:S(2)}, u32[]{:S(2)}) collective-permute-start(bf16[128,768]{1,0:T(8,128)(2,1)} %get-tuple-element.81), channel_id=1, source_target_pairs={{8,0},{16,8},{24,16},{0,24},{9,1},{17,9},{25,17},{1,25},{10,2},{18... | collective-permute-start | bytes 589832 | tf_op jit(solution)/shard_map/ppermute | solution.py:22
  241.3 5.9 %all-to-all-done.2 = bf16[4,96,1536]{2,1,0:T(8,128)(2,1)S(1)} async-done(((bf16[4,96,1536]{2,1,0:T(8,128)(2,1)}), bf16[4,96,1536]{2,1,0:T(8,128)(2,1)S(1)}, u32[]{:S(2)}, u32[]{:S(2)}) %all-to-all-start.2) | async-done | bytes 1179680 | tf_op jit(solution)/shard_map/all_to_all | solution.py:132
  249.5 1.4 collective-permute-start.26
  253.8 4.1 %all-to-all-start.3 = ((bf16[4,24,1536]{2,1,0:T(8,128)(2,1)}), bf16[4,24,1536]{2,1,0:T(8,128)(2,1)}, u32[]{:S(2)}, u32[]{:S(2)}) async-start(bf16[4,24,1536]{2,1,0:T(8,128)(2,1)} %pad.20), calls=%async_computation.4 | async-start | bytes 589824 | tf_op jit(solution)/shard_map/all_to_all | solution.py:132
  257.9 9.1 %reduce-scatter.5.cloned.1.call-done = bf16[384,768]{1,0:T(8,128)(2,1)} async-done(((bf16[1536,768]{1,0:T(8,128)(2,1)}), bf16[384,768]{1,0:T(8,128)(2,1)}) %reduce-scatter.5.cloned.1.call-update) | async-done | bytes 589840 | tf_op jit(solution)/shard_map/reduce_scatter | solution.py:320
  267.0 2.2 bitcast_convert_fusion
  271.2 1.3 slice.325
  273.2 1.3 multiply_reduce_fusion.1
  274.6 2.1 add_bitcast_fusion
  (383 shorter events, 58.8 us)
Async XLA Ops:
  7.2 15.5 %copy-start = (f32[32,12]{0,1:T(8,128)S(1)}, f32[32,12]{0,1:T(8,128)}, u32[]{:S(2)}) copy-start(f32[32,12]{0,1:T(8,128)} %param.16) | copy-start | bytes 4612
  7.2 16.5 %copy-start.56 = (bf16[24,768]{1,0:T(8,128)(2,1)S(1)}, bf16[24,768]{1,0:T(8,128)(2,1)}, u32[]{:S(2)}) copy-start(bf16[24,768]{1,0:T(8,128)(2,1)} %param.15) | copy-start | bytes 110596
  7.2 15.0 %copy-start.84 = (s32[8]{0:T(128)S(1)}, s32[8]{0:T(128)}, u32[]{:S(2)}) copy-start(s32[8]{0:T(128)} %param.22) | copy-start | bytes 100
  7.2 15.8 %copy-start.85 = (s32[1,128,2]{1,2,0:T(2,128)S(1)}, s32[1,128,2]{1,2,0:T(2,128)}, u32[]{:S(2)}) copy-start(s32[1,128,2]{1,2,0:T(2,128)} %param.21) | copy-start | bytes 3076
  7.2 17.2 %copy-start.54 = (bf16[1,96,3072]{2,1,0:T(8,128)(2,1)S(1)}, bf16[1,96,3072]{2,1,0:T(8,128)(2,1)}, u32[]{:S(2)}) copy-start(bf16[1,96,3072]{2,1,0:T(8,128)(2,1)} %param.19) | copy-start | bytes 1769476
  7.2 120.8 %all-gather.6.cloned.1.call-start = ((), (), s32[]{:S(2)}) async-start(), calls=%async_computation.9 | async-start | bytes 2949120 | tf_op jit(solution)/shard_map/all_gather | solution.py:191
  7.3 37.5 %collective-permute-start = (bf16[128,768]{1,0:T(8,128)(2,1)}, bf16[128,768]{1,0:T(8,128)(2,1)S(1)}, u32[]{:S(2)}, u32[]{:S(2)}) collective-permute-start(bf16[128,768]{1,0:T(8,128)(2,1)} %bitcast.296), channel_id=1, source_target_pairs={{8,0},{16,8},{24,16},{0,24},{9,1},{17,9},{25,17},{1,25},{10,2},{18... | collective-permute-start | bytes 589832 | tf_op jit(solution)/shard_map/ppermute | solution.py:22
  12.4 32.4 %collective-permute-start.1 = (bf16[128,768]{1,0:T(8,128)(2,1)}, bf16[128,768]{1,0:T(8,128)(2,1)S(1)}, u32[]{:S(2)}, u32[]{:S(2)}) collective-permute-start(bf16[128,768]{1,0:T(8,128)(2,1)} %bitcast.297), channel_id=1, source_target_pairs={{16,0},{24,8},{0,16},{8,24},{17,1},{25,9},{1,17},{9,25},{18,2},{26... | collective-permute-start | bytes 589832 | tf_op jit(solution)/shard_map/ppermute | solution.py:22
  15.1 9.4 %collective-permute-start.3 = (bf16[24,1408]{1,0:T(8,128)(2,1)S(1)}, bf16[24,1408]{1,0:T(8,128)(2,1)S(1)}, u32[]{:S(2)}, u32[]{:S(2)}) collective-permute-start(bf16[24,1408]{1,0:T(8,128)(2,1)S(1)} %concatenate.142), channel_id=1, source_target_pairs={{8,0},{16,8},{24,16},{0,24},{9,1},{17,9},{25,17},{1,25},{10,2},{18... | collective-permute-start | bytes 202760 | tf_op jit(solution)/shard_map/ppermute | solution.py:22
  16.5 9.1 %collective-permute-start.5 = (bf16[24,1408]{1,0:T(8,128)(2,1)S(1)}, bf16[24,1408]{1,0:T(8,128)(2,1)S(1)}, u32[]{:S(2)}, u32[]{:S(2)}) collective-permute-start(bf16[24,1408]{1,0:T(8,128)(2,1)S(1)} %concatenate.144), channel_id=1, source_target_pairs={{24,0},{0,8},{8,16},{16,24},{25,1},{1,9},{9,17},{17,25},{26,2},{2,... | collective-permute-start | bytes 202760 | tf_op jit(solution)/shard_map/ppermute | solution.py:22
  19.0 11.9 %collective-permute-start.4 = (bf16[24,1408]{1,0:T(8,128)(2,1)S(1)}, bf16[24,1408]{1,0:T(8,128)(2,1)S(1)}, u32[]{:S(2)}, u32[]{:S(2)}) collective-permute-start(bf16[24,1408]{1,0:T(8,128)(2,1)S(1)} %concatenate.143), channel_id=1, source_target_pairs={{16,0},{24,8},{0,16},{8,24},{17,1},{25,9},{1,17},{9,25},{18,2},{26... | collective-permute-start | bytes 202760 | tf_op jit(solution)/shard_map/ppermute | solution.py:22
  22.0 116.9 %all-gather.4.cloned.1.call-start = ((), (), s32[]{:S(2)}) async-start(), calls=%async_computation.6 | async-start | bytes 2949120 | tf_op jit(solution)/shard_map/all_gather | solution.py:205
  23.7 14.2 %copy-start.25 = (bf16[1,128,768]{2,1,0:T(8,128)(2,1)S(1)}, bf16[1,128,768]{2,1,0:T(8,128)(2,1)}, u32[]{:S(2)}) copy-start(bf16[1,128,768]{2,1,0:T(8,128)(2,1)} %param.12) | copy-start | bytes 589828
  30.9 6.9 %collective-permute-start.6 = (bf16[4,24,640]{2,1,0:T(8,128)(2,1)S(1)}, bf16[4,24,640]{2,1,0:T(8,128)(2,1)S(1)}, u32[]{:S(2)}, u32[]{:S(2)}) collective-permute-start(bf16[4,24,640]{2,1,0:T(8,128)(2,1)S(1)} %pad_maximum_fusion.16), channel_id=1, source_target_pairs={{6,0},{4,2},{2,4},{0,6},{7,1},{5,3},{3,5},{1,7},{14,8},{12,10},{10... | collective-permute-start | bytes 368648 | tf_op jit(solution)/shard_map/ppermute | solution.py:29
  33.5 9.4 %collective-permute-start.7 = (bf16[4,24,640]{2,1,0:T(8,128)(2,1)S(1)}, bf16[4,24,640]{2,1,0:T(8,128)(2,1)S(1)}, u32[]{:S(2)}, u32[]{:S(2)}) collective-permute-start(bf16[4,24,640]{2,1,0:T(8,128)(2,1)S(1)} %pad_maximum_fusion.16), channel_id=1, source_target_pairs={{4,0},{6,2},{0,4},{2,6},{5,1},{7,3},{1,5},{3,7},{12,8},{14,10},{8,... | collective-permute-start | bytes 368648 | tf_op jit(solution)/shard_map/ppermute | solution.py:29
  34.0 9.9 %collective-permute-start.8 = (bf16[4,24,640]{2,1,0:T(8,128)(2,1)S(1)}, bf16[4,24,640]{2,1,0:T(8,128)(2,1)S(1)}, u32[]{:S(2)}, u32[]{:S(2)}) collective-permute-start(bf16[4,24,640]{2,1,0:T(8,128)(2,1)S(1)} %pad_maximum_fusion.16), channel_id=1, source_target_pairs={{2,0},{0,2},{6,4},{4,6},{3,1},{1,3},{7,5},{5,7},{10,8},{8,10},{14,... | collective-permute-start | bytes 368648 | tf_op jit(solution)/shard_map/ppermute | solution.py:29
  37.8 15.9 %collective-permute-start.2 = (bf16[128,768]{1,0:T(8,128)(2,1)S(1)}, bf16[128,768]{1,0:T(8,128)(2,1)S(1)}, u32[]{:S(2)}, u32[]{:S(2)}) collective-permute-start(bf16[128,768]{1,0:T(8,128)(2,1)S(1)} %bitcast.298), channel_id=1, source_target_pairs={{24,0},{0,8},{8,16},{16,24},{25,1},{1,9},{9,17},{17,25},{26,2},{2,... | collective-permute-start | bytes 589832 | tf_op jit(solution)/shard_map/ppermute | solution.py:22
  42.9 11.2 %collective-permute-start.11 = (bf16[96,1536]{1,0:T(8,128)(2,1)S(1)}, bf16[96,1536]{1,0:T(8,128)(2,1)S(1)}, u32[]{:S(2)}, u32[]{:S(2)}) collective-permute-start(bf16[96,1536]{1,0:T(8,128)(2,1)S(1)} %maximum_add_fusion), channel_id=1, source_target_pairs={{4,0},{0,4},{5,1},{1,5},{6,2},{2,6},{7,3},{3,7},{12,8},{8,12},{13,... | collective-permute-start | bytes 884744 | tf_op jit(solution)/shard_map/ppermute | solution.py:29
  44.8 11.3 %collective-permute-start.9 = (bf16[4,4,24,640]{3,2,1,0:T(8,128)(2,1)}, bf16[4,4,24,640]{3,2,1,0:T(8,128)(2,1)}, u32[]{:S(2)}, u32[]{:S(2)}) collective-permute-start(bf16[4,4,24,640]{3,2,1,0:T(8,128)(2,1)} %pad_maximum_fusion.8), channel_id=1, source_target_pairs={{1,0},{0,1},{3,2},{2,3},{5,4},{4,5},{7,6},{6,7},{9,8},{8,9},{11,10... | collective-permute-start | bytes 1474568 | tf_op jit(solution)/shard_map/ppermute | solution.py:29
  44.8 19.6 %copy-start.41 = (bf16[128,768]{1,0:T(8,128)(2,1)}, bf16[128,768]{1,0:T(8,128)(2,1)S(1)}, u32[]{:S(2)}) copy-start(bf16[128,768]{1,0:T(8,128)(2,1)S(1)} %collective-permute-done) | copy-start | bytes 589828
  44.8 19.6 %copy-start.44 = (bf16[128,768]{1,0:T(8,128)(2,1)}, bf16[128,768]{1,0:T(8,128)(2,1)S(1)}, u32[]{:S(2)}) copy-start(bf16[128,768]{1,0:T(8,128)(2,1)S(1)} %collective-permute-done.1) | copy-start | bytes 589828
  58.4 13.1 %collective-permute-start.10 = (bf16[512,384]{1,0:T(8,128)(2,1)S(1)}, bf16[512,384]{1,0:T(8,128)(2,1)S(1)}, u32[]{:S(2)}, u32[]{:S(2)}) collective-permute-start(bf16[512,384]{1,0:T(8,128)(2,1)S(1)} %convolution_convert_fusion.4), channel_id=1, source_target_pairs={{4,0},{0,4},{5,1},{1,5},{6,2},{2,6},{7,3},{3,7},{12,8},{8,12},{13,... | collective-permute-start | bytes 1179656 | tf_op jit(solution)/shard_map/ppermute | solution.py:29
  60.9 6.2 %collective-permute-start.15 = (bf16[4,24,768]{2,1,0:T(8,128)(2,1)S(1)}, bf16[4,24,768]{2,1,0:T(8,128)(2,1)S(1)}, u32[]{:S(2)}, u32[]{:S(2)}) collective-permute-start(bf16[4,24,768]{2,1,0:T(8,128)(2,1)S(1)} %fusion.63), channel_id=1, source_target_pairs={{6,0},{4,2},{2,4},{0,6},{7,1},{5,3},{3,5},{1,7},{14,8},{12,10},{10... | collective-permute-start | bytes 442376 | tf_op jit(solution)/shard_map/ppermute | solution.py:29
  62.4 7.9 %collective-permute-start.16 = (bf16[4,24,768]{2,1,0:T(8,128)(2,1)S(1)}, bf16[4,24,768]{2,1,0:T(8,128)(2,1)S(1)}, u32[]{:S(2)}, u32[]{:S(2)}) collective-permute-start(bf16[4,24,768]{2,1,0:T(8,128)(2,1)S(1)} %fusion.63), channel_id=1, source_target_pairs={{4,0},{6,2},{0,4},{2,6},{5,1},{7,3},{1,5},{3,7},{12,8},{14,10},{8,... | collective-permute-start | bytes 442376 | tf_op jit(solution)/shard_map/ppermute | solution.py:29
  63.9 6.4 %collective-permute-start.17 = (bf16[4,24,768]{2,1,0:T(8,128)(2,1)S(1)}, bf16[4,24,768]{2,1,0:T(8,128)(2,1)S(1)}, u32[]{:S(2)}, u32[]{:S(2)}) collective-permute-start(bf16[4,24,768]{2,1,0:T(8,128)(2,1)S(1)} %fusion.63), channel_id=1, source_target_pairs={{2,0},{0,2},{6,4},{4,6},{3,1},{1,3},{7,5},{5,7},{10,8},{8,10},{14,... | collective-permute-start | bytes 442376 | tf_op jit(solution)/shard_map/ppermute | solution.py:29
  71.4 21.7 %collective-permute-start.18 = (bf16[4,4,24,768]{3,2,1,0:T(8,128)(2,1)}, bf16[4,4,24,768]{3,2,1,0:T(8,128)(2,1)}, u32[]{:S(2)}, u32[]{:S(2)}) collective-permute-start(bf16[4,4,24,768]{3,2,1,0:T(8,128)(2,1)} %pad_maximum_fusion.5), channel_id=1, source_target_pairs={{1,0},{0,1},{3,2},{2,3},{5,4},{4,5},{7,6},{6,7},{9,8},{8,9},{11,10... | collective-permute-start | bytes 1769480 | tf_op jit(solution)/shard_map/ppermute | solution.py:29
  78.0 15.1 %copy-start.31 = (bf16[1,4,24,768]{3,2,1,0:T(8,128)(2,1)S(1)}, bf16[1,4,24,768]{3,2,1,0:T(8,128)(2,1)}, u32[]{:S(2)}) copy-start(bf16[1,4,24,768]{3,2,1,0:T(8,128)(2,1)} %copy-done.30) | copy-start | bytes 442372
  78.0 15.1 %copy-start.33 = (bf16[1,4,24,768]{3,2,1,0:T(8,128)(2,1)S(1)}, bf16[1,4,24,768]{3,2,1,0:T(8,128)(2,1)}, u32[]{:S(2)}) copy-start(bf16[1,4,24,768]{3,2,1,0:T(8,128)(2,1)} %copy-done.32) | copy-start | bytes 442372
  79.4 8.9 %collective-permute-start.12 = (bf16[128,192]{0,1:T(8,128)(2,1)}, bf16[128,192]{0,1:T(8,128)(2,1)S(1)}, u32[]{:S(2)}, u32[]{:S(2)}) collective-permute-start(bf16[128,192]{0,1:T(8,128)(2,1)} %bitcast.33), channel_id=1, source_target_pairs={{8,0},{16,8},{24,16},{0,24},{9,1},{17,9},{25,17},{1,25},{10,2},{18... | collective-permute-start | bytes 147464 | tf_op jit(solution)/shard_map/ppermute | solution.py:22
  85.8 6.4 %collective-permute-start.13 = (bf16[128,192]{0,1:T(8,128)(2,1)}, bf16[128,192]{0,1:T(8,128)(2,1)}, u32[]{:S(2)}, u32[]{:S(2)}) collective-permute-start(bf16[128,192]{0,1:T(8,128)(2,1)} %bitcast.34), channel_id=1, source_target_pairs={{16,0},{24,8},{0,16},{8,24},{17,1},{25,9},{1,17},{9,25},{18,2},{26... | collective-permute-start | bytes 147464 | tf_op jit(solution)/shard_map/ppermute | solution.py:22
  85.8 6.4 %collective-permute-start.14 = (bf16[128,192]{0,1:T(8,128)(2,1)}, bf16[128,192]{0,1:T(8,128)(2,1)}, u32[]{:S(2)}, u32[]{:S(2)}) collective-permute-start(bf16[128,192]{0,1:T(8,128)(2,1)} %bitcast.35), channel_id=1, source_target_pairs={{24,0},{0,8},{8,16},{16,24},{25,1},{1,9},{9,17},{17,25},{26,2},{2,... | collective-permute-start | bytes 147464 | tf_op jit(solution)/shard_map/ppermute | solution.py:22
  87.4 160.6 %reduce-scatter.3.cloned.1.call-start = ((), (), s32[]{:S(2)}) async-start(), calls=%async_computation.7 | async-start | bytes 2949120 | tf_op jit(solution)/shard_map/reduce_scatter | solution.py:319
  154.9 29.6 %all-to-all-start.1 = ((bf16[8,80,1536]{2,1,0:T(8,128)(2,1)}), bf16[8,80,1536]{2,1,0:T(8,128)(2,1)}, u32[]{:S(2)}, u32[]{:S(2)}) async-start(bf16[8,80,1536]{2,1,0:T(8,128)(2,1)} %bitcast.293), calls=%async_computation.1 | async-start | bytes 3932160 | tf_op jit(solution)/shard_map/all_to_all | solution.py:132
  159.3 107.7 %reduce-scatter.5.cloned.1.call-start = ((), (), s32[]{:S(2)}) async-start(), calls=%async_computation.8 | async-start | bytes 2949120 | tf_op jit(solution)/shard_map/reduce_scatter | solution.py:320
  195.1 7.3 %collective-permute-start.19 = (bf16[128,192]{0,1:T(8,128)(2,1)}, bf16[128,192]{0,1:T(8,128)(2,1)S(1)}, u32[]{:S(2)}, u32[]{:S(2)}) collective-permute-start(bf16[128,192]{0,1:T(8,128)(2,1)} %get-tuple-element.125), channel_id=1, source_target_pairs={{8,0},{16,8},{24,16},{0,24},{9,1},{17,9},{25,17},{1,25},{10,2},{18... | collective-permute-start | bytes 147464 | tf_op jit(solution)/shard_map/ppermute | solution.py:22
  195.9 9.0 %collective-permute-start.20 = (bf16[128,192]{0,1:T(8,128)(2,1)}, bf16[128,192]{0,1:T(8,128)(2,1)S(1)}, u32[]{:S(2)}, u32[]{:S(2)}) collective-permute-start(bf16[128,192]{0,1:T(8,128)(2,1)} %get-tuple-element.124), channel_id=1, source_target_pairs={{16,0},{24,8},{0,16},{8,24},{17,1},{25,9},{1,17},{9,25},{18,2},{26... | collective-permute-start | bytes 147464 | tf_op jit(solution)/shard_map/ppermute | solution.py:22
  196.4 8.5 %collective-permute-start.21 = (bf16[128,192]{0,1:T(8,128)(2,1)}, bf16[128,192]{0,1:T(8,128)(2,1)S(1)}, u32[]{:S(2)}, u32[]{:S(2)}) collective-permute-start(bf16[128,192]{0,1:T(8,128)(2,1)} %get-tuple-element.123), channel_id=1, source_target_pairs={{24,0},{0,8},{8,16},{16,24},{25,1},{1,9},{9,17},{17,25},{26,2},{2,... | collective-permute-start | bytes 147464 | tf_op jit(solution)/shard_map/ppermute | solution.py:22
  202.4 19.1 %collective-permute-start.27 = (bf16[4,96,896]{2,1,0:T(8,128)(2,1)}, bf16[4,96,896]{2,1,0:T(8,128)(2,1)}, u32[]{:S(2)}, u32[]{:S(2)}) collective-permute-start(bf16[4,96,896]{2,1,0:T(8,128)(2,1)} %dynamic-slice_bitcast_fusion), channel_id=1, source_target_pairs={{1,0},{0,1},{3,2},{2,3},{5,4},{4,5},{7,6},{6,7},{9,8},{8,9},{11,10... | collective-permute-start | bytes 2064392 | tf_op jit(solution)/shard_map/ppermute | solution.py:29
  208.8 9.2 %collective-permute-start.22 = (bf16[512,384]{0,1:T(8,128)(2,1)}, bf16[512,384]{0,1:T(8,128)(2,1)S(1)}, u32[]{:S(2)}, u32[]{:S(2)}) collective-permute-start(bf16[512,384]{0,1:T(8,128)(2,1)} %fusion.22), channel_id=1, source_target_pairs={{4,0},{0,4},{5,1},{1,5},{6,2},{2,6},{7,3},{3,7},{12,8},{8,12},{13,... | collective-permute-start | bytes 1179656 | tf_op jit(solution)/shard_map/ppermute | solution.py:29
  211.9 8.7 %collective-permute-start.29 = (f32[3,32]{1,0:T(4,128)S(1)}, f32[3,32]{1,0:T(4,128)}, u32[]{:S(2)}, u32[]{:S(2)}) collective-permute-start(f32[3,32]{1,0:T(4,128)S(1)} %select_reduce_fusion.1), channel_id=1, source_target_pairs={{1,0},{0,1},{3,2},{2,3},{5,4},{4,5},{7,6},{6,7},{9,8},{8,9},{11,10... | collective-permute-start | bytes 1160 | tf_op jit(solution)/shard_map/ppermute | solution.py:29
  220.6 2.2 collective-permute-start.28
  225.8 21.4 %all-to-all-start.2 = ((bf16[4,96,1536]{2,1,0:T(8,128)(2,1)}), bf16[4,96,1536]{2,1,0:T(8,128)(2,1)S(1)}, u32[]{:S(2)}, u32[]{:S(2)}) async-start(bf16[4,96,1536]{2,1,0:T(8,128)(2,1)} %concatenate.173), calls=%async_computation.3 | async-start | bytes 2359296 | tf_op jit(solution)/shard_map/all_to_all | solution.py:132
  236.8 36.4 %collective-permute-start.23 = (bf16[128,768]{1,0:T(8,128)(2,1)}, bf16[128,768]{1,0:T(8,128)(2,1)}, u32[]{:S(2)}, u32[]{:S(2)}) collective-permute-start(bf16[128,768]{1,0:T(8,128)(2,1)} %get-tuple-element.80), channel_id=1, source_target_pairs={{24,0},{0,8},{8,16},{16,24},{25,1},{1,9},{9,17},{17,25},{26,2},{2,... | collective-permute-start | bytes 589832 | tf_op jit(solution)/shard_map/ppermute | solution.py:22
  236.8 36.4 %collective-permute-start.24 = (bf16[128,768]{1,0:T(8,128)(2,1)}, bf16[128,768]{1,0:T(8,128)(2,1)}, u32[]{:S(2)}, u32[]{:S(2)}) collective-permute-start(bf16[128,768]{1,0:T(8,128)(2,1)} %get-tuple-element.82), channel_id=1, source_target_pairs={{16,0},{24,8},{0,16},{8,24},{17,1},{25,9},{1,17},{9,25},{18,2},{26... | collective-permute-start | bytes 589832 | tf_op jit(solution)/shard_map/ppermute | solution.py:22
  237.5 35.7 %collective-permute-start.25 = (bf16[128,768]{1,0:T(8,128)(2,1)}, bf16[128,768]{1,0:T(8,128)(2,1)}, u32[]{:S(2)}, u32[]{:S(2)}) collective-permute-start(bf16[128,768]{1,0:T(8,128)(2,1)} %get-tuple-element.81), channel_id=1, source_target_pairs={{8,0},{16,8},{24,16},{0,24},{9,1},{17,9},{25,17},{1,25},{10,2},{18... | collective-permute-start | bytes 589832 | tf_op jit(solution)/shard_map/ppermute | solution.py:22
  249.5 19.6 %collective-permute-start.26 = (bf16[96,1536]{1,0:T(8,128)(2,1)S(1)}, bf16[96,1536]{1,0:T(8,128)(2,1)S(1)}, u32[]{:S(2)}, u32[]{:S(2)}) collective-permute-start(bf16[96,1536]{1,0:T(8,128)(2,1)S(1)} %dynamic-slice_bitcast_fusion.2), channel_id=1, source_target_pairs={{4,0},{0,4},{5,1},{1,5},{6,2},{2,6},{7,3},{3,7},{12,8},{8,12},{13,... | collective-permute-start | bytes 884744 | tf_op jit(solution)/shard_map/ppermute | solution.py:29
  253.0 16.8 %copy-start.55 = (bf16[192,1536]{1,0:T(8,128)(2,1)S(1)}, bf16[192,1536]{1,0:T(8,128)(2,1)}, u32[]{:S(2)}) copy-start(bf16[192,1536]{1,0:T(8,128)(2,1)} %reduce-scatter.3.cloned.1.call-done) | copy-start | bytes 1769476
  253.8 23.0 %all-to-all-start.3 = ((bf16[4,24,1536]{2,1,0:T(8,128)(2,1)}), bf16[4,24,1536]{2,1,0:T(8,128)(2,1)}, u32[]{:S(2)}, u32[]{:S(2)}) async-start(bf16[4,24,1536]{2,1,0:T(8,128)(2,1)} %pad.20), calls=%async_computation.4 | async-start | bytes 589824 | tf_op jit(solution)/shard_map/all_to_all | solution.py:132
  (77 other events, 273.5 us)
Sparse Core Ops, SparseCore 0:
  22.1 53.1 all-gather.5
  87.5 51.3 all-gather.3
  155.0 49.5 reduce-scatter.2
  206.7 60.1 reduce-scatter.4

commit v5 on v4

--- a/solution.py
+++ b/solution.py
@@ -106,7 +106,7 @@
             pl.BlockSpec((block, width), lambda i: (i, 0)),
         ),
         scratch_shapes=[pltpu.VMEM(both.shape, WIDE), pltpu.VMEM((width, count), LOW)],
-        compiler_params=pltpu.CompilerParams(vmem_limit_bytes=56 * 1024 * 1024),
+        compiler_params=pltpu.CompilerParams(vmem_limit_bytes=(44 if count <= 1024 else 56) * 1024 * 1024),
         cost_estimate=pl.CostEstimate(
             flops=flops, bytes_accessed=4 * both.size + 8 * w_first.size, transcendentals=count * units
         ),

time: 292 us -> 290 us (level)
    reduce_scatter x1, waiting for transfers between devices: 9.11 us -> 0.02 us  [body(): lax.psum_scatter(grad_second, 'hz', scatter_dimension=0, tiled=True)]
    all_to_all x3, waiting for transfers between devices: 30.7 us -> 35.1 us  [every_block(): return lax.all_to_all(x, axes, split_axis=0, concat_axis=0, tiled=True)]
  transfers between devices with their start and end apart: 37 -> 37, of which waited for: 16 -> 14; matrix products, arithmetic and copies ran while one was open for 25% -> 26% of each run, Pallas kernels for 0% -> 0%
where the time goes in v5:
time: 290 us; the launch traced here: 289 us
  waiting for transfers between devices  84.3 us (29%)
  starting transfers between devices  56.8 us (20%)
  other arithmetic  31.8 us (11%)
  local copies, waits for them, and re-layouts  28.9 us (10%)
  blocking collectives  28.6 us (10%)
  matrix products  22.7 us (8%)
  between operations  20.4 us (7%)
  Pallas kernels  15.3 us (5%)
    all_to_all x3, waiting for transfers between devices, every_block(): return lax.all_to_all(x, axes, split_axis=0, concat_axis=0, tiled=True)  35.1 us
    ppermute x15, starting transfers between devices, shift(): return lax.ppermute(x, axis, [((j + d) % n, j) for j in range(n)])  30.3 us
    all_to_all x1, blocking collectives, every_block(): return lax.all_to_all(x, axes, split_axis=0, concat_axis=0, tiled=True)  28.6 us
    ppermute x15, waiting for transfers between devices, shift(): return lax.ppermute(x, axis, [((j + d) % n, j) for j in range(n)])  23.8 us
    pallas_call x1, Pallas kernels, expert(): pl.pallas_call(expert_kernel, grid=(units // block,), out_shape=(jax.Shap...  15.3 us
    dot_general x13, matrix products, dot(): lax.dot_general(left, right, (contract, ((), ())), preferred_element_type...  14.6 us
    all_to_all x3, starting transfers between devices, every_block(): return lax.all_to_all(x, axes, split_axis=0, concat_axis=0, tiled=True)  14.4 us
    all_gather x1, waiting for transfers between devices, body(): w_first = lax.all_gather(in_rows, 'hz', axis=0, tiled=True)  13.5 us
  transfers between devices with their start and end apart: 37, of which 14 were waited for; matrix products, arithmetic and copies ran while one was open for 26% of the time, Pallas kernels for 0%

profile of v5, /device:TPU:0, one launch (start us, length us, event | category | flops | bytes accessed | tf_op | source)
XLA Modules:
  0.0 288.8 jit_solution(9380663174391018035)
XLA Ops:
  7.3 5.1 %collective-permute-start = (bf16[128,768]{1,0:T(8,128)(2,1)}, bf16[128,768]{1,0:T(8,128)(2,1)S(1)}, u32[]{:S(2)}, u32[]{:S(2)}) collective-permute-start(bf16[128,768]{1,0:T(8,128)(2,1)} %bitcast.295), channel_id=1, source_target_pairs={{8,0},{16,8},{24,16},{0,24},{9,1},{17,9},{25,17},{1,25},{10,2},{18... | collective-permute-start | bytes 589832 | tf_op jit(solution)/shard_map/ppermute | solution.py:22
  16.5 1.6 collective-permute-start.5
  19.0 3.0 %collective-permute-start.4 = (bf16[24,1408]{1,0:T(8,128)(2,1)S(1)}, bf16[24,1408]{1,0:T(8,128)(2,1)S(1)}, u32[]{:S(2)}, u32[]{:S(2)}) collective-permute-start(bf16[24,1408]{1,0:T(8,128)(2,1)S(1)} %concatenate.143), channel_id=1, source_target_pairs={{16,0},{24,8},{0,16},{8,24},{17,1},{25,9},{1,17},{9,25},{18,2},{26... | collective-permute-start | bytes 202760 | tf_op jit(solution)/shard_map/ppermute | solution.py:22
  25.7 5.2 %collective-permute-done.4 = bf16[24,1408]{1,0:T(8,128)(2,1)S(1)} collective-permute-done((bf16[24,1408]{1,0:T(8,128)(2,1)S(1)}, bf16[24,1408]{1,0:T(8,128)(2,1)S(1)}, u32[]{:S(2)}, u32[]{:S(2)}) %collective-permute-start.4) | collective-permute-done | bytes 67616 | tf_op jit(solution)/shard_map/ppermute | solution.py:22
  30.9 2.5 collective-permute-start.6
  35.7 2.1 collective-permute-done.6
  37.8 5.0 %collective-permute-start.2 = (bf16[128,768]{1,0:T(8,128)(2,1)S(1)}, bf16[128,768]{1,0:T(8,128)(2,1)S(1)}, u32[]{:S(2)}, u32[]{:S(2)}) collective-permute-start(bf16[128,768]{1,0:T(8,128)(2,1)S(1)} %bitcast.297), channel_id=1, source_target_pairs={{24,0},{0,8},{8,16},{16,24},{25,1},{1,9},{9,17},{17,25},{26,2},{2,... | collective-permute-start | bytes 589832 | tf_op jit(solution)/shard_map/ppermute | solution.py:22
  44.8 8.9 %collective-permute-done.2 = bf16[128,768]{1,0:T(8,128)(2,1)S(1)} collective-permute-done((bf16[128,768]{1,0:T(8,128)(2,1)S(1)}, bf16[128,768]{1,0:T(8,128)(2,1)S(1)}, u32[]{:S(2)}, u32[]{:S(2)}) %collective-permute-start.2) | collective-permute-done | bytes 196640 | tf_op jit(solution)/shard_map/ppermute | solution.py:22
  59.2 1.2 collective-permute-start.10
  61.6 1.5 collective-permute-start.15
  63.1 1.6 collective-permute-start.16
  66.4 1.5 collective-permute-done.15
  67.9 3.2 %collective-permute-done.16 = bf16[4,24,768]{2,1,0:T(8,128)(2,1)S(1)} collective-permute-done((bf16[4,24,768]{2,1,0:T(8,128)(2,1)S(1)}, bf16[4,24,768]{2,1,0:T(8,128)(2,1)S(1)}, u32[]{:S(2)}, u32[]{:S(2)}) %collective-permute-start.16) | collective-permute-done | bytes 147488 | tf_op jit(solution)/shard_map/ppermute | solution.py:29
  72.9 2.1 fusion.23
  75.1 2.6 fusion.165
  80.1 6.5 %collective-permute-start.12 = (bf16[128,192]{0,1:T(8,128)(2,1)S(1)}, bf16[128,192]{0,1:T(8,128)(2,1)S(1)}, u32[]{:S(2)}, u32[]{:S(2)}) collective-permute-start(bf16[128,192]{0,1:T(8,128)(2,1)S(1)} %bitcast.327), channel_id=1, source_target_pairs={{8,0},{16,8},{24,16},{0,24},{9,1},{17,9},{25,17},{1,25},{10,2},{18... | collective-permute-start | bytes 147464 | tf_op jit(solution)/shard_map/ppermute | solution.py:22
  88.8 3.9 %collective-permute-done.13 = bf16[128,192]{0,1:T(8,128)(2,1)S(1)} collective-permute-done((bf16[128,192]{0,1:T(8,128)(2,1)S(1)}, bf16[128,192]{0,1:T(8,128)(2,1)S(1)}, u32[]{:S(2)}, u32[]{:S(2)}) %collective-permute-start.13) | collective-permute-done | bytes 49184 | tf_op jit(solution)/shard_map/ppermute | solution.py:22
  97.5 28.6 %all_to_all.20 = bf16[8,80,1536]{2,1,0:T(8,128)(2,1)S(1)} all-to-all(bf16[8,80,1536]{2,1,0:T(8,128)(2,1)S(1)} %pad_maximum_fusion), channel_id=1, replica_groups=mesh['hz'=4,'yy'=2,'xx'=2,'cc'=2] {'yy','xx','cc'}, dimensions={0} | all-to-all | bytes 3932160 | tf_op jit(solution)/shard_map/all_to_all | solution.py:132
  126.1 13.5 %all-gather.4.cloned.1.call-done.w_first = bf16[768,1536]{1,0:T(8,128)(2,1)} async-done(((bf16[192,1536]{1,0:T(8,128)(2,1)}), bf16[768,1536]{1,0:T(8,128)(2,1)}) %all-gather.4.cloned.1.call-update) | async-done | bytes 2359312 | tf_op jit(solution)/shard_map/all_gather | solution.py:205
  139.6 15.3 %shard_map.195 = (bf16[640,1536]{1,0:T(8,128)(2,1)}, bf16[768,1536]{1,0:T(8,128)(2,1)}, bf16[1536,768]{1,0:T(8,128)(2,1)}) custom-call(bf16[640,1536]{1,0:T(8,128)(2,1)S(1)} %bitcast.269, bf16[768,1536]{1,0:T(8,128)(2,1)} %all-gather.4.cloned.1.call-done.w_first, bf16[1536,768]{1,0:T(8,128)(2,1)} %bitcast.333), custom_call_target="tpu_custom_call" | custom-call | flops 9059696640 | bytes 13369344 | tf_op jit(solution)/shard_map/pallas_call | solution.py:90
  154.9 4.4 %all-to-all-start.1 = ((bf16[8,80,1536]{2,1,0:T(8,128)(2,1)}), bf16[8,80,1536]{2,1,0:T(8,128)(2,1)}, u32[]{:S(2)}, u32[]{:S(2)}) async-start(bf16[8,80,1536]{2,1,0:T(8,128)(2,1)} %bitcast.55), calls=%async_computation.1 | async-start | bytes 3932160 | tf_op jit(solution)/shard_map/all_to_all | solution.py:132
  159.8 24.7 %all-to-all-done.1 = bf16[8,80,1536]{2,1,0:T(8,128)(2,1)} async-done(((bf16[8,80,1536]{2,1,0:T(8,128)(2,1)}), bf16[8,80,1536]{2,1,0:T(8,128)(2,1)}, u32[]{:S(2)}, u32[]{:S(2)}) %all-to-all-start.1) | async-done | bytes 1966112 | tf_op jit(solution)/shard_map/all_to_all | solution.py:132
  184.5 1.6 fusion.12
  186.1 1.6 fusion.15
  187.8 2.5 fusion.49
  191.4 1.5 convolution_convert_fusion
  194.9 1.8 collective-permute-start.21
  197.0 1.4 pad_maximum_fusion.1
  200.2 4.6 %collective-permute-done.20 = bf16[128,192]{0,1:T(8,128)(2,1)S(1)} collective-permute-done((bf16[128,192]{0,1:T(8,128)(2,1)S(1)}, bf16[128,192]{0,1:T(8,128)(2,1)S(1)}, u32[]{:S(2)}, u32[]{:S(2)}) %collective-permute-start.20) | collective-permute-done | bytes 49184 | tf_op jit(solution)/shard_map/ppermute | solution.py:22
  212.0 4.7 %collective-permute-done.22 = bf16[512,384]{0,1:T(8,128)(2,1)} collective-permute-done((bf16[512,384]{0,1:T(8,128)(2,1)}, bf16[512,384]{0,1:T(8,128)(2,1)}, u32[]{:S(2)}, u32[]{:S(2)}) %collective-permute-start.22) | collective-permute-done | bytes 393248 | tf_op jit(solution)/shard_map/ppermute | solution.py:29
  217.9 1.7 convolution_convert_fusion.3
  219.6 2.2 copy.81
  221.8 1.4 copy.82
  225.9 1.4 fusion.7
  228.4 1.8 concatenate.173
  230.2 6.0 %all-to-all-start.2 = ((bf16[4,96,1536]{2,1,0:T(8,128)(2,1)}), bf16[4,96,1536]{2,1,0:T(8,128)(2,1)S(1)}, u32[]{:S(2)}, u32[]{:S(2)}) async-start(bf16[4,96,1536]{2,1,0:T(8,128)(2,1)} %concatenate.173), calls=%async_computation.3 | async-start | bytes 2359296 | tf_op jit(solution)/shard_map/all_to_all | solution.py:132
  236.2 1.4 convert_multiply_fusion
  237.6 2.0 fusion.166
  240.9 1.6 collective-permute-start.24
  242.5 2.9 %collective-permute-start.25 = (bf16[128,768]{1,0:T(8,128)(2,1)}, bf16[128,768]{1,0:T(8,128)(2,1)}, u32[]{:S(2)}, u32[]{:S(2)}) collective-permute-start(bf16[128,768]{1,0:T(8,128)(2,1)} %get-tuple-element.81), channel_id=1, source_target_pairs={{8,0},{16,8},{24,16},{0,24},{9,1},{17,9},{25,17},{1,25},{10,2},{18... | collective-permute-start | bytes 589832 | tf_op jit(solution)/shard_map/ppermute | solution.py:22
  246.1 6.0 %all-to-all-done.2 = bf16[4,96,1536]{2,1,0:T(8,128)(2,1)S(1)} async-done(((bf16[4,96,1536]{2,1,0:T(8,128)(2,1)}), bf16[4,96,1536]{2,1,0:T(8,128)(2,1)S(1)}, u32[]{:S(2)}, u32[]{:S(2)}) %all-to-all-start.2) | async-done | bytes 1179680 | tf_op jit(solution)/shard_map/all_to_all | solution.py:132
  254.4 1.2 collective-permute-start.26
  258.5 4.1 %all-to-all-start.3 = ((bf16[4,24,1536]{2,1,0:T(8,128)(2,1)}), bf16[4,24,1536]{2,1,0:T(8,128)(2,1)}, u32[]{:S(2)}, u32[]{:S(2)}) async-start(bf16[4,24,1536]{2,1,0:T(8,128)(2,1)} %pad.20), calls=%async_computation.4 | async-start | bytes 589824 | tf_op jit(solution)/shard_map/all_to_all | solution.py:132
  262.6 2.2 bitcast_convert_fusion
  266.9 1.3 slice.325
  268.9 1.4 multiply_reduce_fusion.1
  270.3 2.1 add_bitcast_fusion
  272.4 4.4 %all-to-all-done.3 = bf16[4,24,1536]{2,1,0:T(8,128)(2,1)} async-done(((bf16[4,24,1536]{2,1,0:T(8,128)(2,1)}), bf16[4,24,1536]{2,1,0:T(8,128)(2,1)}, u32[]{:S(2)}, u32[]{:S(2)}) %all-to-all-start.3) | async-done | bytes 294944 | tf_op jit(solution)/shard_map/all_to_all | solution.py:132
  (403 shorter events, 59.9 us)
Async XLA Ops:
  7.2 15.5 %copy-start = (f32[32,12]{0,1:T(8,128)S(1)}, f32[32,12]{0,1:T(8,128)}, u32[]{:S(2)}) copy-start(f32[32,12]{0,1:T(8,128)} %param.16) | copy-start | bytes 4612
  7.2 16.5 %copy-start.57 = (bf16[24,768]{1,0:T(8,128)(2,1)S(1)}, bf16[24,768]{1,0:T(8,128)(2,1)}, u32[]{:S(2)}) copy-start(bf16[24,768]{1,0:T(8,128)(2,1)} %param.15) | copy-start | bytes 110596
  7.2 15.0 %copy-start.94 = (s32[8]{0:T(128)S(1)}, s32[8]{0:T(128)}, u32[]{:S(2)}) copy-start(s32[8]{0:T(128)} %param.22) | copy-start | bytes 100
  7.2 15.8 %copy-start.95 = (s32[1,128,2]{1,2,0:T(2,128)S(1)}, s32[1,128,2]{1,2,0:T(2,128)}, u32[]{:S(2)}) copy-start(s32[1,128,2]{1,2,0:T(2,128)} %param.21) | copy-start | bytes 3076
  7.2 17.8 %copy-start.55 = (bf16[1,96,3072]{2,1,0:T(8,128)(2,1)S(1)}, bf16[1,96,3072]{2,1,0:T(8,128)(2,1)}, u32[]{:S(2)}) copy-start(bf16[1,96,3072]{2,1,0:T(8,128)(2,1)} %param.19) | copy-start | bytes 1769476
  7.2 118.9 %all-gather.6.cloned.1.call-start = ((), (), s32[]{:S(2)}) async-start(), calls=%async_computation.9 | async-start | bytes 2949120 | tf_op jit(solution)/shard_map/all_gather | solution.py:191
  7.3 37.5 %collective-permute-start = (bf16[128,768]{1,0:T(8,128)(2,1)}, bf16[128,768]{1,0:T(8,128)(2,1)S(1)}, u32[]{:S(2)}, u32[]{:S(2)}) collective-permute-start(bf16[128,768]{1,0:T(8,128)(2,1)} %bitcast.295), channel_id=1, source_target_pairs={{8,0},{16,8},{24,16},{0,24},{9,1},{17,9},{25,17},{1,25},{10,2},{18... | collective-permute-start | bytes 589832 | tf_op jit(solution)/shard_map/ppermute | solution.py:22
  12.4 32.4 %collective-permute-start.1 = (bf16[128,768]{1,0:T(8,128)(2,1)}, bf16[128,768]{1,0:T(8,128)(2,1)S(1)}, u32[]{:S(2)}, u32[]{:S(2)}) collective-permute-start(bf16[128,768]{1,0:T(8,128)(2,1)} %bitcast.296), channel_id=1, source_target_pairs={{16,0},{24,8},{0,16},{8,24},{17,1},{25,9},{1,17},{9,25},{18,2},{26... | collective-permute-start | bytes 589832 | tf_op jit(solution)/shard_map/ppermute | solution.py:22
  15.1 10.6 %collective-permute-start.3 = (bf16[24,1408]{1,0:T(8,128)(2,1)S(1)}, bf16[24,1408]{1,0:T(8,128)(2,1)S(1)}, u32[]{:S(2)}, u32[]{:S(2)}) collective-permute-start(bf16[24,1408]{1,0:T(8,128)(2,1)S(1)} %concatenate.142), channel_id=1, source_target_pairs={{8,0},{16,8},{24,16},{0,24},{9,1},{17,9},{25,17},{1,25},{10,2},{18... | collective-permute-start | bytes 202760 | tf_op jit(solution)/shard_map/ppermute | solution.py:22
  16.5 9.2 %collective-permute-start.5 = (bf16[24,1408]{1,0:T(8,128)(2,1)S(1)}, bf16[24,1408]{1,0:T(8,128)(2,1)S(1)}, u32[]{:S(2)}, u32[]{:S(2)}) collective-permute-start(bf16[24,1408]{1,0:T(8,128)(2,1)S(1)} %concatenate.144), channel_id=1, source_target_pairs={{24,0},{0,8},{8,16},{16,24},{25,1},{1,9},{9,17},{17,25},{26,2},{2,... | collective-permute-start | bytes 202760 | tf_op jit(solution)/shard_map/ppermute | solution.py:22
  19.0 11.9 %collective-permute-start.4 = (bf16[24,1408]{1,0:T(8,128)(2,1)S(1)}, bf16[24,1408]{1,0:T(8,128)(2,1)S(1)}, u32[]{:S(2)}, u32[]{:S(2)}) collective-permute-start(bf16[24,1408]{1,0:T(8,128)(2,1)S(1)} %concatenate.143), channel_id=1, source_target_pairs={{16,0},{24,8},{0,16},{8,24},{17,1},{25,9},{1,17},{9,25},{18,2},{26... | collective-permute-start | bytes 202760 | tf_op jit(solution)/shard_map/ppermute | solution.py:22
  22.0 117.6 %all-gather.4.cloned.1.call-start = ((), (), s32[]{:S(2)}) async-start(), calls=%async_computation.6 | async-start | bytes 2949120 | tf_op jit(solution)/shard_map/all_gather | solution.py:205
  23.7 14.1 %copy-start.25 = (bf16[1,128,768]{2,1,0:T(8,128)(2,1)S(1)}, bf16[1,128,768]{2,1,0:T(8,128)(2,1)}, u32[]{:S(2)}) copy-start(bf16[1,128,768]{2,1,0:T(8,128)(2,1)} %param.12) | copy-start | bytes 589828
  30.9 6.9 %collective-permute-start.6 = (bf16[4,24,640]{2,1,0:T(8,128)(2,1)S(1)}, bf16[4,24,640]{2,1,0:T(8,128)(2,1)S(1)}, u32[]{:S(2)}, u32[]{:S(2)}) collective-permute-start(bf16[4,24,640]{2,1,0:T(8,128)(2,1)S(1)} %pad_maximum_fusion.16), channel_id=1, source_target_pairs={{6,0},{4,2},{2,4},{0,6},{7,1},{5,3},{3,5},{1,7},{14,8},{12,10},{10... | collective-permute-start | bytes 368648 | tf_op jit(solution)/shard_map/ppermute | solution.py:29
  33.4 9.4 %collective-permute-start.7 = (bf16[4,24,640]{2,1,0:T(8,128)(2,1)S(1)}, bf16[4,24,640]{2,1,0:T(8,128)(2,1)S(1)}, u32[]{:S(2)}, u32[]{:S(2)}) collective-permute-start(bf16[4,24,640]{2,1,0:T(8,128)(2,1)S(1)} %pad_maximum_fusion.16), channel_id=1, source_target_pairs={{4,0},{6,2},{0,4},{2,6},{5,1},{7,3},{1,5},{3,7},{12,8},{14,10},{8,... | collective-permute-start | bytes 368648 | tf_op jit(solution)/shard_map/ppermute | solution.py:29
  33.9 9.9 %collective-permute-start.8 = (bf16[4,24,640]{2,1,0:T(8,128)(2,1)S(1)}, bf16[4,24,640]{2,1,0:T(8,128)(2,1)S(1)}, u32[]{:S(2)}, u32[]{:S(2)}) collective-permute-start(bf16[4,24,640]{2,1,0:T(8,128)(2,1)S(1)} %pad_maximum_fusion.16), channel_id=1, source_target_pairs={{2,0},{0,2},{6,4},{4,6},{3,1},{1,3},{7,5},{5,7},{10,8},{8,10},{14,... | collective-permute-start | bytes 368648 | tf_op jit(solution)/shard_map/ppermute | solution.py:29
  37.8 15.9 %collective-permute-start.2 = (bf16[128,768]{1,0:T(8,128)(2,1)S(1)}, bf16[128,768]{1,0:T(8,128)(2,1)S(1)}, u32[]{:S(2)}, u32[]{:S(2)}) collective-permute-start(bf16[128,768]{1,0:T(8,128)(2,1)S(1)} %bitcast.297), channel_id=1, source_target_pairs={{24,0},{0,8},{8,16},{16,24},{25,1},{1,9},{9,17},{17,25},{26,2},{2,... | collective-permute-start | bytes 589832 | tf_op jit(solution)/shard_map/ppermute | solution.py:22
  42.8 11.2 %collective-permute-start.11 = (bf16[96,1536]{1,0:T(8,128)(2,1)S(1)}, bf16[96,1536]{1,0:T(8,128)(2,1)S(1)}, u32[]{:S(2)}, u32[]{:S(2)}) collective-permute-start(bf16[96,1536]{1,0:T(8,128)(2,1)S(1)} %maximum_add_fusion), channel_id=1, source_target_pairs={{4,0},{0,4},{5,1},{1,5},{6,2},{2,6},{7,3},{3,7},{12,8},{8,12},{13,... | collective-permute-start | bytes 884744 | tf_op jit(solution)/shard_map/ppermute | solution.py:29
  44.8 12.3 %collective-permute-start.9 = (bf16[4,4,24,640]{3,2,1,0:T(8,128)(2,1)}, bf16[4,4,24,640]{3,2,1,0:T(8,128)(2,1)S(1)}, u32[]{:S(2)}, u32[]{:S(2)}) collective-permute-start(bf16[4,4,24,640]{3,2,1,0:T(8,128)(2,1)} %pad_maximum_fusion.8), channel_id=1, source_target_pairs={{1,0},{0,1},{3,2},{2,3},{5,4},{4,5},{7,6},{6,7},{9,8},{8,9},{11,10... | collective-permute-start | bytes 1474568 | tf_op jit(solution)/shard_map/ppermute | solution.py:29
  44.8 20.4 %copy-start.40 = (bf16[128,768]{1,0:T(8,128)(2,1)}, bf16[128,768]{1,0:T(8,128)(2,1)S(1)}, u32[]{:S(2)}) copy-start(bf16[128,768]{1,0:T(8,128)(2,1)S(1)} %collective-permute-done) | copy-start | bytes 589828
  57.5 38.1 %copy-start.4 = (bf16[4,4,2,24,640]{4,3,2,1,0:T(8,128)(2,1)}, bf16[4,4,2,24,640]{4,3,2,1,0:T(8,128)(2,1)S(1)}, u32[]{:S(2)}) copy-start(bf16[4,4,2,24,640]{4,3,2,1,0:T(8,128)(2,1)S(1)} %copy.72) | copy-start | bytes 2949124
  59.2 13.0 %collective-permute-start.10 = (bf16[512,384]{1,0:T(8,128)(2,1)S(1)}, bf16[512,384]{1,0:T(8,128)(2,1)S(1)}, u32[]{:S(2)}, u32[]{:S(2)}) collective-permute-start(bf16[512,384]{1,0:T(8,128)(2,1)S(1)} %convolution_convert_fusion.4), channel_id=1, source_target_pairs={{4,0},{0,4},{5,1},{1,5},{6,2},{2,6},{7,3},{3,7},{12,8},{8,12},{13,... | collective-permute-start | bytes 1179656 | tf_op jit(solution)/shard_map/ppermute | solution.py:29
  61.6 6.2 %collective-permute-start.15 = (bf16[4,24,768]{2,1,0:T(8,128)(2,1)S(1)}, bf16[4,24,768]{2,1,0:T(8,128)(2,1)S(1)}, u32[]{:S(2)}, u32[]{:S(2)}) collective-permute-start(bf16[4,24,768]{2,1,0:T(8,128)(2,1)S(1)} %fusion.63), channel_id=1, source_target_pairs={{6,0},{4,2},{2,4},{0,6},{7,1},{5,3},{3,5},{1,7},{14,8},{12,10},{10... | collective-permute-start | bytes 442376 | tf_op jit(solution)/shard_map/ppermute | solution.py:29
  63.1 7.9 %collective-permute-start.16 = (bf16[4,24,768]{2,1,0:T(8,128)(2,1)S(1)}, bf16[4,24,768]{2,1,0:T(8,128)(2,1)S(1)}, u32[]{:S(2)}, u32[]{:S(2)}) collective-permute-start(bf16[4,24,768]{2,1,0:T(8,128)(2,1)S(1)} %fusion.63), channel_id=1, source_target_pairs={{4,0},{6,2},{0,4},{2,6},{5,1},{7,3},{1,5},{3,7},{12,8},{14,10},{8,... | collective-permute-start | bytes 442376 | tf_op jit(solution)/shard_map/ppermute | solution.py:29
  64.7 6.4 %collective-permute-start.17 = (bf16[4,24,768]{2,1,0:T(8,128)(2,1)S(1)}, bf16[4,24,768]{2,1,0:T(8,128)(2,1)S(1)}, u32[]{:S(2)}, u32[]{:S(2)}) collective-permute-start(bf16[4,24,768]{2,1,0:T(8,128)(2,1)S(1)} %fusion.63), channel_id=1, source_target_pairs={{2,0},{0,2},{6,4},{4,6},{3,1},{1,3},{7,5},{5,7},{10,8},{8,10},{14,... | collective-permute-start | bytes 442376 | tf_op jit(solution)/shard_map/ppermute | solution.py:29
  72.2 20.6 %collective-permute-start.18 = (bf16[4,4,24,768]{3,2,1,0:T(8,128)(2,1)}, bf16[4,4,24,768]{3,2,1,0:T(8,128)(2,1)}, u32[]{:S(2)}, u32[]{:S(2)}) collective-permute-start(bf16[4,4,24,768]{3,2,1,0:T(8,128)(2,1)} %pad_maximum_fusion.5), channel_id=1, source_target_pairs={{1,0},{0,1},{3,2},{2,3},{5,4},{4,5},{7,6},{6,7},{9,8},{8,9},{11,10... | collective-permute-start | bytes 1769480 | tf_op jit(solution)/shard_map/ppermute | solution.py:29
  80.1 13.9 %copy-start.23 = (bf16[3,64,512]{2,1,0:T(8,128)(2,1)}, bf16[3,64,512]{2,1,0:T(8,128)(2,1)S(1)}, u32[]{:S(2)}) copy-start(bf16[3,64,512]{2,1,0:T(8,128)(2,1)S(1)} %convolution_convert_fusion.6) | copy-start | bytes 589828
  80.1 8.6 %collective-permute-start.12 = (bf16[128,192]{0,1:T(8,128)(2,1)S(1)}, bf16[128,192]{0,1:T(8,128)(2,1)S(1)}, u32[]{:S(2)}, u32[]{:S(2)}) collective-permute-start(bf16[128,192]{0,1:T(8,128)(2,1)S(1)} %bitcast.327), channel_id=1, source_target_pairs={{8,0},{16,8},{24,16},{0,24},{9,1},{17,9},{25,17},{1,25},{10,2},{18... | collective-permute-start | bytes 147464 | tf_op jit(solution)/shard_map/ppermute | solution.py:22
  86.6 6.0 %collective-permute-start.13 = (bf16[128,192]{0,1:T(8,128)(2,1)S(1)}, bf16[128,192]{0,1:T(8,128)(2,1)S(1)}, u32[]{:S(2)}, u32[]{:S(2)}) collective-permute-start(bf16[128,192]{0,1:T(8,128)(2,1)S(1)} %bitcast.326), channel_id=1, source_target_pairs={{16,0},{24,8},{0,16},{8,24},{17,1},{25,9},{1,17},{9,25},{18,2},{26... | collective-permute-start | bytes 147464 | tf_op jit(solution)/shard_map/ppermute | solution.py:22
  86.7 6.0 %collective-permute-start.14 = (bf16[128,192]{0,1:T(8,128)(2,1)S(1)}, bf16[128,192]{0,1:T(8,128)(2,1)S(1)}, u32[]{:S(2)}, u32[]{:S(2)}) collective-permute-start(bf16[128,192]{0,1:T(8,128)(2,1)S(1)} %bitcast.325), channel_id=1, source_target_pairs={{24,0},{0,8},{8,16},{16,24},{25,1},{1,9},{9,17},{17,25},{26,2},{2,... | collective-permute-start | bytes 147464 | tf_op jit(solution)/shard_map/ppermute | solution.py:22
  88.2 164.7 %reduce-scatter.3.cloned.1.call-start = ((), (), s32[]{:S(2)}) async-start(), calls=%async_computation.7 | async-start | bytes 2949120 | tf_op jit(solution)/shard_map/reduce_scatter | solution.py:319
  154.9 29.6 %all-to-all-start.1 = ((bf16[8,80,1536]{2,1,0:T(8,128)(2,1)}), bf16[8,80,1536]{2,1,0:T(8,128)(2,1)}, u32[]{:S(2)}, u32[]{:S(2)}) async-start(bf16[8,80,1536]{2,1,0:T(8,128)(2,1)} %bitcast.55), calls=%async_computation.1 | async-start | bytes 3932160 | tf_op jit(solution)/shard_map/all_to_all | solution.py:132
  159.2 25.3 %copy-start.53 = (bf16[256,640]{1,0:T(8,128)(2,1)S(1)}, bf16[256,640]{1,0:T(8,128)(2,1)}, u32[]{:S(2)}) copy-start(bf16[256,640]{1,0:T(8,128)(2,1)} %copy-done.52) | copy-start | bytes 983044
  159.3 103.3 %reduce-scatter.5.cloned.1.call-start = ((), (), s32[]{:S(2)}) async-start(), calls=%async_computation.8 | async-start | bytes 2949120 | tf_op jit(solution)/shard_map/reduce_scatter | solution.py:320
  159.3 26.8 %copy-start.66 = (pred[256,640]{1,0:T(32,128)(4,1)S(1)}, pred[256,640]{1,0:T(32,128)(4,1)}, u32[]{:S(2)}) copy-start(pred[256,640]{1,0:T(32,128)(4,1)} %get-tuple-element.149) | copy-start | bytes 491524
  193.4 6.8 %collective-permute-start.19 = (bf16[128,192]{0,1:T(8,128)(2,1)S(1)}, bf16[128,192]{0,1:T(8,128)(2,1)S(1)}, u32[]{:S(2)}, u32[]{:S(2)}) collective-permute-start(bf16[128,192]{0,1:T(8,128)(2,1)S(1)} %get-tuple-element.125), channel_id=1, source_target_pairs={{8,0},{16,8},{24,16},{0,24},{9,1},{17,9},{25,17},{1,25},{10,2},{18... | collective-permute-start | bytes 147464 | tf_op jit(solution)/shard_map/ppermute | solution.py:22
  194.3 10.5 %collective-permute-start.20 = (bf16[128,192]{0,1:T(8,128)(2,1)S(1)}, bf16[128,192]{0,1:T(8,128)(2,1)S(1)}, u32[]{:S(2)}, u32[]{:S(2)}) collective-permute-start(bf16[128,192]{0,1:T(8,128)(2,1)S(1)} %get-tuple-element.124), channel_id=1, source_target_pairs={{16,0},{24,8},{0,16},{8,24},{17,1},{25,9},{1,17},{9,25},{18,2},{26... | collective-permute-start | bytes 147464 | tf_op jit(solution)/shard_map/ppermute | solution.py:22
  194.9 10.0 %collective-permute-start.21 = (bf16[128,192]{0,1:T(8,128)(2,1)S(1)}, bf16[128,192]{0,1:T(8,128)(2,1)S(1)}, u32[]{:S(2)}, u32[]{:S(2)}) collective-permute-start(bf16[128,192]{0,1:T(8,128)(2,1)S(1)} %get-tuple-element.123), channel_id=1, source_target_pairs={{24,0},{0,8},{8,16},{16,24},{25,1},{1,9},{9,17},{17,25},{26,2},{2,... | collective-permute-start | bytes 147464 | tf_op jit(solution)/shard_map/ppermute | solution.py:22
  199.4 26.4 %collective-permute-start.27 = (bf16[4,96,896]{2,1,0:T(8,128)(2,1)}, bf16[4,96,896]{2,1,0:T(8,128)(2,1)}, u32[]{:S(2)}, u32[]{:S(2)}) collective-permute-start(bf16[4,96,896]{2,1,0:T(8,128)(2,1)} %dynamic-slice_bitcast_fusion), channel_id=1, source_target_pairs={{1,0},{0,1},{3,2},{2,3},{5,4},{4,5},{7,6},{6,7},{9,8},{8,9},{11,10... | collective-permute-start | bytes 2064392 | tf_op jit(solution)/shard_map/ppermute | solution.py:29
  208.6 8.1 %collective-permute-start.22 = (bf16[512,384]{0,1:T(8,128)(2,1)}, bf16[512,384]{0,1:T(8,128)(2,1)}, u32[]{:S(2)}, u32[]{:S(2)}) collective-permute-start(bf16[512,384]{0,1:T(8,128)(2,1)} %fusion.22), channel_id=1, source_target_pairs={{4,0},{0,4},{5,1},{1,5},{6,2},{2,6},{7,3},{3,7},{12,8},{8,12},{13,... | collective-permute-start | bytes 1179656 | tf_op jit(solution)/shard_map/ppermute | solution.py:29
  212.0 13.0 %collective-permute-start.29 = (f32[3,32]{1,0:T(4,128)}, f32[3,32]{1,0:T(4,128)S(1)}, u32[]{:S(2)}, u32[]{:S(2)}) collective-permute-start(f32[3,32]{1,0:T(4,128)} %select_reduce_fusion.1), channel_id=1, source_target_pairs={{1,0},{0,1},{3,2},{2,3},{5,4},{4,5},{7,6},{6,7},{9,8},{8,9},{11,10... | collective-permute-start | bytes 1160 | tf_op jit(solution)/shard_map/ppermute | solution.py:29
  225.0 2.2 collective-permute-start.28
  230.2 22.0 %all-to-all-start.2 = ((bf16[4,96,1536]{2,1,0:T(8,128)(2,1)}), bf16[4,96,1536]{2,1,0:T(8,128)(2,1)S(1)}, u32[]{:S(2)}, u32[]{:S(2)}) async-start(bf16[4,96,1536]{2,1,0:T(8,128)(2,1)} %concatenate.173), calls=%async_computation.3 | async-start | bytes 2359296 | tf_op jit(solution)/shard_map/all_to_all | solution.py:132
  240.9 28.0 %collective-permute-start.23 = (bf16[128,768]{1,0:T(8,128)(2,1)}, bf16[128,768]{1,0:T(8,128)(2,1)}, u32[]{:S(2)}, u32[]{:S(2)}) collective-permute-start(bf16[128,768]{1,0:T(8,128)(2,1)} %get-tuple-element.80), channel_id=1, source_target_pairs={{24,0},{0,8},{8,16},{16,24},{25,1},{1,9},{9,17},{17,25},{26,2},{2,... | collective-permute-start | bytes 589832 | tf_op jit(solution)/shard_map/ppermute | solution.py:22
  240.9 28.0 %collective-permute-start.24 = (bf16[128,768]{1,0:T(8,128)(2,1)}, bf16[128,768]{1,0:T(8,128)(2,1)}, u32[]{:S(2)}, u32[]{:S(2)}) collective-permute-start(bf16[128,768]{1,0:T(8,128)(2,1)} %get-tuple-element.82), channel_id=1, source_target_pairs={{16,0},{24,8},{0,16},{8,24},{17,1},{25,9},{1,17},{9,25},{18,2},{26... | collective-permute-start | bytes 589832 | tf_op jit(solution)/shard_map/ppermute | solution.py:22
  242.5 26.4 %collective-permute-start.25 = (bf16[128,768]{1,0:T(8,128)(2,1)}, bf16[128,768]{1,0:T(8,128)(2,1)}, u32[]{:S(2)}, u32[]{:S(2)}) collective-permute-start(bf16[128,768]{1,0:T(8,128)(2,1)} %get-tuple-element.81), channel_id=1, source_target_pairs={{8,0},{16,8},{24,16},{0,24},{9,1},{17,9},{25,17},{1,25},{10,2},{18... | collective-permute-start | bytes 589832 | tf_op jit(solution)/shard_map/ppermute | solution.py:22
  254.4 10.3 %collective-permute-start.26 = (bf16[96,1536]{1,0:T(8,128)(2,1)S(1)}, bf16[96,1536]{1,0:T(8,128)(2,1)S(1)}, u32[]{:S(2)}, u32[]{:S(2)}) collective-permute-start(bf16[96,1536]{1,0:T(8,128)(2,1)S(1)} %dynamic-slice_bitcast_fusion.2), channel_id=1, source_target_pairs={{4,0},{0,4},{5,1},{1,5},{6,2},{2,6},{7,3},{3,7},{12,8},{8,12},{13,... | collective-permute-start | bytes 884744 | tf_op jit(solution)/shard_map/ppermute | solution.py:29
  258.5 18.3 %all-to-all-start.3 = ((bf16[4,24,1536]{2,1,0:T(8,128)(2,1)}), bf16[4,24,1536]{2,1,0:T(8,128)(2,1)}, u32[]{:S(2)}, u32[]{:S(2)}) async-start(bf16[4,24,1536]{2,1,0:T(8,128)(2,1)} %pad.20), calls=%async_computation.4 | async-start | bytes 589824 | tf_op jit(solution)/shard_map/all_to_all | solution.py:132
  (87 other events, 357.5 us)
Sparse Core Ops, SparseCore 0:
  22.1 53.1 all-gather.5
  88.3 51.2 all-gather.3
  155.0 49.9 reduce-scatter.2
  207.1 55.2 reduce-scatter.4
